TPU v7x, 512 devices: a whole 4x8x8 slice. The times are simulated.
512 devices in a mesh: dp: 64 (over y, x, z_lo), seq: 8 (over z_hi, core).
Axes of the slice: x: 4, y: 8, z: 8 (z_hi: 4, z_lo: 2; z = z_hi * 2 + z_lo), core: 2. Of those that a mesh axis runs over, the one named last changes fastest.
Arguments:
- queries: bfloat16 [64, 1024, 4096], P('dp', 'seq'), may hold values from -6.5 to 6.5
- resp_kv: bfloat16 [64, 1024, 2048], P('dp', 'seq'), may hold values from -6 to 6
- prompt_kv: bfloat16 [64, 128, 2048], P('dp', 'seq'), may hold values from -6 to 6
- d_out: bfloat16 [64, 1024, 4096], P('dp', 'seq'), may hold values from -6 to 6
- resp_lengths: int32 [64, 3], P('dp'), may hold values from 1 to 640, 1024 in all within a row
- prompt_home: int32 [64], P('dp'), may hold values from 0 to 63, as said below
Outputs:
- d_queries: bfloat16 [64, 1024, 4096], P('dp', 'seq')
- d_resp_kv: bfloat16 [64, 1024, 2048], P('dp', 'seq')
- d_prompt_kv: bfloat16 [64, 128, 2048], P('dp', 'seq')
Inputs may be any that keep to these rules, and one draw needn't show every extreme that they name: (l - prompt_home[l]) mod 64 lies below 8, and equals 7 for learner 0.
All inputs are finite; a program needn't handle non-finite values.
Results may differ from a plain program's by a relative error of at most 0.017.
Values may be sent and summed in bfloat16 or wider, within the bound.
No kernel may reach another device: no remote copies, remote signals or barrier semaphores. Data moves between devices by JAX's collectives and lax.ppermute only.
A program may use at most 64 MiB of HBM per device.

v0:
```python
import jax
import jax.numpy as jnp
from jax import lax
from jax.sharding import PartitionSpec as P

KVH = 8
SPREAD = 8


def from_behind(block, axis, distance):
    devices = range(lax.axis_size(axis))
    route = [(i - distance, i) for i in devices if i - distance in devices]
    return lax.ppermute(block, axis, route)


def passed_along(value, axis, by):
    peers = lax.axis_size(axis)
    return lax.ppermute(value, axis, [(i, (i + by) % peers) for i in range(peers)])


def attend(q_rows, grad_rows, keys_all, visible, heads_kv, head_size):
    count = q_rows.shape[0]
    total = keys_all.shape[0]
    group = q_rows.shape[1] // (heads_kv * head_size)
    scale = head_size ** (-0.5)
    qg = q_rows.reshape(count, heads_kv, group, head_size).transpose(1, 0, 2, 3)
    dg = grad_rows.reshape(count, heads_kv, group, head_size).transpose(1, 0, 2, 3)
    keys = (
        keys_all[:, : heads_kv * head_size].reshape(total, heads_kv, head_size).transpose(1, 0, 2)
    )
    values = (
        keys_all[:, heads_kv * head_size :].reshape(total, heads_kv, head_size).transpose(1, 0, 2)
    )

    def one_head(operands):
        qh, dh, kh, vh = operands
        scores = jnp.einsum("rgd,kd->grk", qh, kh, preferred_element_type=jnp.float32) * scale
        scores = jnp.where(visible[None], scores, -1e30)
        top = jnp.max(scores, axis=-1, keepdims=True)
        expo = jnp.exp(scores - top)
        weights = expo / jnp.sum(expo, axis=-1, keepdims=True)
        weights_b = weights.astype(jnp.bfloat16)
        out = jnp.einsum("grk,kd->rgd", weights_b, vh, preferred_element_type=jnp.float32).astype(
            jnp.bfloat16
        )
        delta = jnp.sum(dh.astype(jnp.float32) * out.astype(jnp.float32), axis=-1).T
        d_weights = jnp.einsum("rgd,kd->grk", dh, vh, preferred_element_type=jnp.float32)
        d_scores = (scale * weights * (d_weights - delta[:, :, None])).astype(jnp.bfloat16)
        d_query = jnp.einsum("grk,kd->rgd", d_scores, kh, preferred_element_type=jnp.float32)
        d_key = jnp.einsum("grk,rgd->kd", d_scores, qh, preferred_element_type=jnp.float32)
        d_value = jnp.einsum("grk,rgd->kd", weights_b, dh, preferred_element_type=jnp.float32)
        return (d_query, d_key, d_value)

    d_query, d_key, d_value = lax.map(one_head, (qg, dg, keys, values))
    d_query = d_query.transpose(1, 0, 2, 3).reshape(count, q_rows.shape[1]).astype(jnp.bfloat16)
    d_key = d_key.transpose(1, 0, 2).reshape(total, heads_kv * head_size)
    d_value = d_value.transpose(1, 0, 2).reshape(total, heads_kv * head_size)
    return (d_query, jnp.concatenate([d_key, d_value], axis=1))


def on_device(queries, resp_kv, prompt_kv, d_out, resp_lengths, prompt_home):
    q_rows = queries[0]
    own_kv = resp_kv[0]
    own_prompt = prompt_kv[0]
    grad_rows = d_out[0]
    rows = q_rows.shape[0]
    n_seq = lax.axis_size("seq")
    n_dp = lax.axis_size("dp")
    span = 5 * n_seq // 8
    me_seq = lax.axis_index("seq")
    me_dp = lax.axis_index("dp")
    offset = jnp.mod(me_dp - prompt_home[0], n_dp)
    earlier = [from_behind(own_kv, "seq", step) for step in range(span, 0, -1)]
    near = jnp.concatenate(earlier + [own_kv], axis=0)
    chosen = jnp.where(offset == 0, own_prompt, jnp.zeros_like(own_prompt))
    for step in range(1, SPREAD):
        arrived = passed_along(own_prompt, "dp", step)
        chosen = jnp.where(offset == step, arrived, chosen)
    prompt_whole = lax.all_gather(chosen, "seq", axis=0, tiled=True)
    plen = prompt_whole.shape[0]
    lengths = resp_lengths[0]
    starts = jnp.cumsum(lengths) - lengths
    q_ids = me_seq * rows + jnp.arange(rows, dtype=jnp.int32)
    k_ids = me_seq * rows - span * rows + jnp.arange(near.shape[0], dtype=jnp.int32)
    q_start = jnp.max(jnp.where(starts[None, :] <= q_ids[:, None], starts[None, :], 0), axis=1)
    near_seen = (k_ids[None, :] >= q_start[:, None]) & (k_ids[None, :] <= q_ids[:, None])
    visible = jnp.concatenate([jnp.ones((rows, plen), bool), near_seen], axis=1)
    heads_kv = KVH
    head_size = own_kv.shape[1] // (2 * heads_kv)
    d_query, d_kv = attend(
        q_rows,
        grad_rows,
        jnp.concatenate([prompt_whole, near], axis=0),
        visible,
        heads_kv,
        head_size,
    )
    near_parts = d_kv[plen:].astype(jnp.bfloat16)
    near_total = near_parts[span * rows :].astype(jnp.float32)
    for index in range(span):
        piece = near_parts[index * rows : (index + 1) * rows]
        near_total = near_total + from_behind(piece, "seq", index - span).astype(jnp.float32)
    prompt_grad = lax.psum_scatter(d_kv[:plen], "seq", scatter_dimension=0, tiled=True)
    returned = jnp.where(offset == 0, prompt_grad, 0.0)
    for step in range(1, SPREAD):
        masked = jnp.where(offset == step, prompt_grad, 0.0)
        returned = returned + passed_along(masked, "dp", -step)
    return (
        d_query[None],
        near_total.astype(jnp.bfloat16)[None],
        returned.astype(jnp.bfloat16)[None],
    )


def solution(mesh):
    placed = (
        P("dp", "seq", None),
        P("dp", "seq", None),
        P("dp", "seq", None),
        P("dp", "seq", None),
        P("dp", None),
        P("dp"),
    )
    return jax.shard_map(
        on_device,
        mesh=mesh,
        in_specs=placed,
        out_specs=(P("dp", "seq", None), P("dp", "seq", None), P("dp", "seq", None)),
        check_vma=False,
    )
```

profile of v0, /device:TPU:24, one launch (start us, length us, event | category | flops | bytes accessed | tf_op | source)
XLA Modules:
  0.0 403.8 jit_solution(3461214697248829210)
XLA Ops:
  7.2 4.4 %collective-permute-start.6 = (bf16[16,2048]{1,0:T(8,128)(2,1)}, bf16[16,2048]{1,0:T(8,128)(2,1)S(1)}, u32[]{:S(2)}, u32[]{:S(2)}) collective-permute-start(bf16[16,2048]{1,0:T(8,128)(2,1)} %bitcast.208), channel_id=1, source_target_pairs={{0,8},{8,16},{16,24},{24,32},{32,40},{40,48},{48,56},{56,64},{64,7... | collective-permute-start | bytes 196616 | tf_op jit(solution)/shard_map/ppermute | solution.py:18
  11.6 3.4 collective-permute-start.5
  15.1 3.1 collective-permute-start.4
  18.2 6.1 %collective-permute-start.3 = (bf16[16,2048]{1,0:T(8,128)(2,1)}, bf16[16,2048]{1,0:T(8,128)(2,1)S(1)}, u32[]{:S(2)}, u32[]{:S(2)}) collective-permute-start(bf16[16,2048]{1,0:T(8,128)(2,1)} %bitcast.211), channel_id=1, source_target_pairs={{0,32},{8,40},{16,48},{24,56},{32,64},{40,72},{48,80},{56,88},{64,... | collective-permute-start | bytes 196616 | tf_op jit(solution)/shard_map/ppermute | solution.py:18
  24.3 5.8 %collective-permute-start.2 = (bf16[16,2048]{1,0:T(8,128)(2,1)}, bf16[16,2048]{1,0:T(8,128)(2,1)S(1)}, u32[]{:S(2)}, u32[]{:S(2)}) collective-permute-start(bf16[16,2048]{1,0:T(8,128)(2,1)} %bitcast.212), channel_id=1, source_target_pairs={{0,40},{8,48},{16,56},{24,64},{32,72},{40,80},{48,88},{56,96},{64,... | collective-permute-start | bytes 196616 | tf_op jit(solution)/shard_map/ppermute | solution.py:18
  31.8 3.5 collective-permute-start.1
  35.3 1.9 collective-permute-start
  38.1 1.7 copy.39
  41.2 1.3 collective-permute-start.11
  42.5 6.7 %collective-permute-start.10 = (bf16[128,2048]{1,0:T(8,128)(2,1)S(1)}, bf16[128,2048]{1,0:T(8,128)(2,1)S(1)}, u32[]{:S(2)}, u32[]{:S(2)}) collective-permute-start(bf16[128,2048]{1,0:T(8,128)(2,1)S(1)} %bitcast.204), channel_id=1, source_target_pairs={{0,2},{1,3},{2,4},{3,5},{4,6},{5,7},{8,10},{9,11},{10,12},{11,13},... | collective-permute-start | bytes 1572872 | tf_op jit(solution)/shard_map/ppermute | solution.py:13
  49.2 8.3 %collective-permute-start.9 = (bf16[128,2048]{1,0:T(8,128)(2,1)S(1)}, bf16[128,2048]{1,0:T(8,128)(2,1)S(1)}, u32[]{:S(2)}, u32[]{:S(2)}) collective-permute-start(bf16[128,2048]{1,0:T(8,128)(2,1)S(1)} %bitcast.205), channel_id=1, source_target_pairs={{0,3},{1,4},{2,5},{3,6},{4,7},{8,11},{9,12},{10,13},{11,14},{12,15... | collective-permute-start | bytes 1572872 | tf_op jit(solution)/shard_map/ppermute | solution.py:13
  57.5 1.9 collective-permute-start.8
  60.8 93.2 %all_gather.3 = bf16[128,2048]{1,0:T(8,128)(2,1)S(1)} all-gather(bf16[16,2048]{1,0:T(8,128)(2,1)S(1)} %select_select_fusion), channel_id=1, replica_groups=mesh['dp'=64,'seq'=8] {'seq'}, dimensions={0}, use_global_device_ids=true | all-gather | bytes 589824 | tf_op jit(solution)/shard_map/all_gather | solution.py:79
  155.4 2.2 bitcast_bitcast_fusion
  157.6 97.7 %while.14 = (s32[]{:T(128)}, bf16[8,128,4,128]{1,3,2,0:T(8,128)(2,1)}, f32[8,896,128]{2,1,0:T(8,128)}, f32[8,896,128]{2,1,0:T(8,128)}, bf16[8,896,128]{2,1,0:T(8...) while((s32[]{:T(128)}, ...), condition=%wide.region_6.7_spmd, body=%wide.region_2.6_spmd.sunk | while | flops 948571264 | bytes 10784369 | solution.py:54
  158.6 1.9 fusion.119
  160.5 2.3 fusion.120
  162.8 2.1 fusion.121
  167.1 2.6 fusion.124
  170.8 1.9 fusion.119
  172.7 2.3 fusion.120
  175.0 2.1 fusion.121
  179.3 2.7 fusion.124
  183.1 1.9 fusion.119
  184.9 2.3 fusion.120
  187.2 2.1 fusion.121
  191.6 2.7 fusion.124
  195.3 1.9 fusion.119
  197.2 2.3 fusion.120
  199.5 2.1 fusion.121
  203.8 2.7 fusion.124
  207.5 1.9 fusion.119
  209.4 2.3 fusion.120
  211.7 2.1 fusion.121
  216.0 2.7 fusion.124
  219.7 1.9 fusion.119
  221.6 2.3 fusion.120
  223.9 2.1 fusion.121
  228.2 2.7 fusion.124
  232.0 1.9 fusion.119
  233.9 2.3 fusion.120
  236.1 2.1 fusion.121
  240.5 2.6 fusion.124
  244.2 1.9 fusion.119
  246.1 2.3 fusion.120
  248.3 2.1 fusion.121
  252.7 2.6 fusion.124
  255.3 2.7 bitcast_dynamic-update-slice_fusion.1
  259.0 2.9 copy-done
  263.0 3.6 convert.4
  266.6 1.6 fusion.76
  275.6 67.3 %reduce-scatter.2.cloned.1.call-done = f32[16,2048]{1,0:T(8,128)} async-done(((f32[128,2048]{1,0:T(8,128)}), f32[16,2048]{1,0:T(8,128)}) %reduce-scatter.2.cloned.1.call-update) | async-done | bytes 131088 | tf_op jit(solution)/shard_map/reduce_scatter | solution.py:103
  342.9 1.7 broadcast_select_fusion.6
  344.6 4.3 %collective-permute-start.17 = (f32[16,2048]{1,0:T(8,128)}, f32[16,2048]{1,0:T(8,128)}, u32[]{:S(2)}, u32[]{:S(2)}) collective-permute-start(f32[16,2048]{1,0:T(8,128)} %get-tuple-element.100), channel_id=1, source_target_pairs={{0,504},{8,0},{16,8},{24,16},{32,24},{40,32},{48,40},{56,48},{64,5... | collective-permute-start | bytes 393224 | tf_op jit(solution)/shard_map/ppermute | solution.py:18
  348.9 2.6 collective-permute-start.23
  351.5 2.3 copy.54
  353.8 3.3 collective-permute-start.22
  357.1 5.0 %collective-permute-start.21 = (f32[16,2048]{1,0:T(8,128)}, f32[16,2048]{1,0:T(8,128)S(1)}, u32[]{:S(2)}, u32[]{:S(2)}) collective-permute-start(f32[16,2048]{1,0:T(8,128)} %get-tuple-element.103), channel_id=1, source_target_pairs={{0,472},{8,480},{16,488},{24,496},{32,504},{40,0},{48,8},{56,16},{... | collective-permute-start | bytes 393224 | tf_op jit(solution)/shard_map/ppermute | solution.py:18
  362.1 4.1 %collective-permute-start.20 = (f32[16,2048]{1,0:T(8,128)S(1)}, f32[16,2048]{1,0:T(8,128)S(1)}, u32[]{:S(2)}, u32[]{:S(2)}) collective-permute-start(f32[16,2048]{1,0:T(8,128)S(1)} %get-tuple-element.104), channel_id=1, source_target_pairs={{0,480},{8,488},{16,496},{24,504},{32,0},{40,8},{48,16},{56,24},{6... | collective-permute-start | bytes 393224 | tf_op jit(solution)/shard_map/ppermute | solution.py:18
  366.2 22.1 %collective-permute-start.19 = (f32[16,2048]{1,0:T(8,128)S(1)}, f32[16,2048]{1,0:T(8,128)S(1)}, u32[]{:S(2)}, u32[]{:S(2)}) collective-permute-start(f32[16,2048]{1,0:T(8,128)S(1)} %get-tuple-element.105), channel_id=1, source_target_pairs={{0,488},{8,496},{16,504},{24,0},{32,8},{40,16},{48,24},{56,32},{64... | collective-permute-start | bytes 393224 | tf_op jit(solution)/shard_map/ppermute | solution.py:18
  388.3 2.1 collective-permute-start.18
  390.4 2.3 fusion.69
  392.8 2.6 collective-permute-done.18
  395.3 1.7 fusion.70
  (98 shorter events, 40.9 us)
Async XLA Ops:
  7.2 32.6 %copy-start.3 = (bf16[1,128,4096]{2,1,0:T(8,128)(2,1)S(1)}, bf16[1,128,4096]{2,1,0:T(8,128)(2,1)}, u32[]{:S(2)}) copy-start(bf16[1,128,4096]{2,1,0:T(8,128)(2,1)} %param.11) | copy-start | bytes 3145732
  7.2 335.7 %reduce-scatter.2.cloned.1.call-start = ((), (), s32[]{:S(2)}) async-start(), calls=%async_computation.1 | async-start | bytes 1179648 | tf_op jit(solution)/shard_map/reduce_scatter | solution.py:103
  7.2 24.6 %collective-permute-start.6 = (bf16[16,2048]{1,0:T(8,128)(2,1)}, bf16[16,2048]{1,0:T(8,128)(2,1)S(1)}, u32[]{:S(2)}, u32[]{:S(2)}) collective-permute-start(bf16[16,2048]{1,0:T(8,128)(2,1)} %bitcast.208), channel_id=1, source_target_pairs={{0,8},{8,16},{16,24},{24,32},{32,40},{40,48},{48,56},{56,64},{64,7... | collective-permute-start | bytes 196616 | tf_op jit(solution)/shard_map/ppermute | solution.py:18
  11.6 23.6 %collective-permute-start.5 = (bf16[16,2048]{1,0:T(8,128)(2,1)}, bf16[16,2048]{1,0:T(8,128)(2,1)S(1)}, u32[]{:S(2)}, u32[]{:S(2)}) collective-permute-start(bf16[16,2048]{1,0:T(8,128)(2,1)} %bitcast.209), channel_id=1, source_target_pairs={{0,16},{8,24},{16,32},{24,40},{32,48},{40,56},{48,64},{56,72},{64,... | collective-permute-start | bytes 196616 | tf_op jit(solution)/shard_map/ppermute | solution.py:18
  15.1 26.1 %collective-permute-start.4 = (bf16[16,2048]{1,0:T(8,128)(2,1)}, bf16[16,2048]{1,0:T(8,128)(2,1)S(1)}, u32[]{:S(2)}, u32[]{:S(2)}) collective-permute-start(bf16[16,2048]{1,0:T(8,128)(2,1)} %bitcast.210), channel_id=1, source_target_pairs={{0,24},{8,32},{16,40},{24,48},{32,56},{40,64},{48,72},{56,80},{64,... | collective-permute-start | bytes 196616 | tf_op jit(solution)/shard_map/ppermute | solution.py:18
  18.2 24.3 %collective-permute-start.3 = (bf16[16,2048]{1,0:T(8,128)(2,1)}, bf16[16,2048]{1,0:T(8,128)(2,1)S(1)}, u32[]{:S(2)}, u32[]{:S(2)}) collective-permute-start(bf16[16,2048]{1,0:T(8,128)(2,1)} %bitcast.211), channel_id=1, source_target_pairs={{0,32},{8,40},{16,48},{24,56},{32,64},{40,72},{48,80},{56,88},{64,... | collective-permute-start | bytes 196616 | tf_op jit(solution)/shard_map/ppermute | solution.py:18
  24.3 24.9 %collective-permute-start.2 = (bf16[16,2048]{1,0:T(8,128)(2,1)}, bf16[16,2048]{1,0:T(8,128)(2,1)S(1)}, u32[]{:S(2)}, u32[]{:S(2)}) collective-permute-start(bf16[16,2048]{1,0:T(8,128)(2,1)} %bitcast.212), channel_id=1, source_target_pairs={{0,40},{8,48},{16,56},{24,64},{32,72},{40,80},{48,88},{56,96},{64,... | collective-permute-start | bytes 196616 | tf_op jit(solution)/shard_map/ppermute | solution.py:18
  31.8 25.7 %collective-permute-start.1 = (bf16[16,2048]{1,0:T(8,128)(2,1)}, bf16[16,2048]{1,0:T(8,128)(2,1)S(1)}, u32[]{:S(2)}, u32[]{:S(2)}) collective-permute-start(bf16[16,2048]{1,0:T(8,128)(2,1)} %bitcast.213), channel_id=1, source_target_pairs={{0,48},{8,56},{16,64},{24,72},{32,80},{40,88},{48,96},{56,104},{64... | collective-permute-start | bytes 196616 | tf_op jit(solution)/shard_map/ppermute | solution.py:18
  35.3 24.2 %collective-permute-start = (bf16[16,2048]{1,0:T(8,128)(2,1)}, bf16[16,2048]{1,0:T(8,128)(2,1)S(1)}, u32[]{:S(2)}, u32[]{:S(2)}) collective-permute-start(bf16[16,2048]{1,0:T(8,128)(2,1)} %bitcast.214), channel_id=1, source_target_pairs={{0,56},{8,64},{16,72},{24,80},{32,88},{40,96},{48,104},{56,112},{6... | collective-permute-start | bytes 196616 | tf_op jit(solution)/shard_map/ppermute | solution.py:18
  38.1 3.1 copy-start.4
  38.1 22.7 %copy-start.6 = (bf16[1,16,2048]{2,1,0:T(8,128)(2,1)S(1)}, bf16[1,16,2048]{2,1,0:T(8,128)(2,1)}, u32[]{:S(2)}) copy-start(bf16[1,16,2048]{2,1,0:T(8,128)(2,1)} %param.10) | copy-start | bytes 196612
  41.2 113.1 %collective-permute-start.11 = (bf16[128,2048]{1,0:T(8,128)(2,1)S(1)}, bf16[128,2048]{1,0:T(8,128)(2,1)S(1)}, u32[]{:S(2)}, u32[]{:S(2)}) collective-permute-start(bf16[128,2048]{1,0:T(8,128)(2,1)S(1)} %bitcast.203), channel_id=1, source_target_pairs={{0,1},{1,2},{2,3},{3,4},{4,5},{5,6},{6,7},{8,9},{9,10},{10,11},{11... | collective-permute-start | bytes 1572872 | tf_op jit(solution)/shard_map/ppermute | solution.py:13
  42.5 111.7 %collective-permute-start.10 = (bf16[128,2048]{1,0:T(8,128)(2,1)S(1)}, bf16[128,2048]{1,0:T(8,128)(2,1)S(1)}, u32[]{:S(2)}, u32[]{:S(2)}) collective-permute-start(bf16[128,2048]{1,0:T(8,128)(2,1)S(1)} %bitcast.204), channel_id=1, source_target_pairs={{0,2},{1,3},{2,4},{3,5},{4,6},{5,7},{8,10},{9,11},{10,12},{11,13},... | collective-permute-start | bytes 1572872 | tf_op jit(solution)/shard_map/ppermute | solution.py:13
  49.2 104.9 %collective-permute-start.9 = (bf16[128,2048]{1,0:T(8,128)(2,1)S(1)}, bf16[128,2048]{1,0:T(8,128)(2,1)S(1)}, u32[]{:S(2)}, u32[]{:S(2)}) collective-permute-start(bf16[128,2048]{1,0:T(8,128)(2,1)S(1)} %bitcast.205), channel_id=1, source_target_pairs={{0,3},{1,4},{2,5},{3,6},{4,7},{8,11},{9,12},{10,13},{11,14},{12,15... | collective-permute-start | bytes 1572872 | tf_op jit(solution)/shard_map/ppermute | solution.py:13
  57.5 96.6 %collective-permute-start.8 = (bf16[128,2048]{1,0:T(8,128)(2,1)S(1)}, bf16[128,2048]{1,0:T(8,128)(2,1)S(1)}, u32[]{:S(2)}, u32[]{:S(2)}) collective-permute-start(bf16[128,2048]{1,0:T(8,128)(2,1)S(1)} %bitcast.206), channel_id=1, source_target_pairs={{0,4},{1,5},{2,6},{3,7},{8,12},{9,13},{10,14},{11,15},{16,20},{17,... | collective-permute-start | bytes 1572872 | tf_op jit(solution)/shard_map/ppermute | solution.py:13
  59.5 94.6 %collective-permute-start.7 = (bf16[128,2048]{1,0:T(8,128)(2,1)S(1)}, bf16[128,2048]{1,0:T(8,128)(2,1)S(1)}, u32[]{:S(2)}, u32[]{:S(2)}) collective-permute-start(bf16[128,2048]{1,0:T(8,128)(2,1)S(1)} %bitcast.207), channel_id=1, source_target_pairs={{0,5},{1,6},{2,7},{8,13},{9,14},{10,15},{16,21},{17,22},{18,23},{2... | collective-permute-start | bytes 1572872 | tf_op jit(solution)/shard_map/ppermute | solution.py:13
  255.3 3.1 copy-start.2
  259.0 2.9 copy-start
  266.6 2.5 copy-start.1
  269.1 75.5 %collective-permute-start.12 = (bf16[128,2048]{1,0:T(8,128)(2,1)}, bf16[128,2048]{1,0:T(8,128)(2,1)S(1)}, u32[]{:S(2)}, u32[]{:S(2)}) collective-permute-start(bf16[128,2048]{1,0:T(8,128)(2,1)} %get-tuple-element.93), channel_id=1, source_target_pairs={{5,0},{6,1},{7,2},{13,8},{14,9},{15,10},{21,16},{22,17},{23,18},{2... | collective-permute-start | bytes 1572872 | tf_op jit(solution)/shard_map/ppermute | solution.py:13
  270.4 78.5 %collective-permute-start.16 = (bf16[128,2048]{1,0:T(8,128)(2,1)}, bf16[128,2048]{1,0:T(8,128)(2,1)S(1)}, u32[]{:S(2)}, u32[]{:S(2)}) collective-permute-start(bf16[128,2048]{1,0:T(8,128)(2,1)} %get-tuple-element.94), channel_id=1, source_target_pairs={{1,0},{2,1},{3,2},{4,3},{5,4},{6,5},{7,6},{9,8},{10,9},{11,10},{12... | collective-permute-start | bytes 1572872 | tf_op jit(solution)/shard_map/ppermute | solution.py:13
  271.7 82.1 %collective-permute-start.15 = (bf16[128,2048]{1,0:T(8,128)(2,1)}, bf16[128,2048]{1,0:T(8,128)(2,1)S(1)}, u32[]{:S(2)}, u32[]{:S(2)}) collective-permute-start(bf16[128,2048]{1,0:T(8,128)(2,1)} %get-tuple-element.95), channel_id=1, source_target_pairs={{2,0},{3,1},{4,2},{5,3},{6,4},{7,5},{10,8},{11,9},{12,10},{13,11},... | collective-permute-start | bytes 1572872 | tf_op jit(solution)/shard_map/ppermute | solution.py:13
  273.0 84.1 %collective-permute-start.14 = (bf16[128,2048]{1,0:T(8,128)(2,1)}, bf16[128,2048]{1,0:T(8,128)(2,1)S(1)}, u32[]{:S(2)}, u32[]{:S(2)}) collective-permute-start(bf16[128,2048]{1,0:T(8,128)(2,1)} %get-tuple-element.96), channel_id=1, source_target_pairs={{3,0},{4,1},{5,2},{6,3},{7,4},{11,8},{12,9},{13,10},{14,11},{15,12... | collective-permute-start | bytes 1572872 | tf_op jit(solution)/shard_map/ppermute | solution.py:13
  274.3 87.8 %collective-permute-start.13 = (bf16[128,2048]{1,0:T(8,128)(2,1)S(1)}, bf16[128,2048]{1,0:T(8,128)(2,1)S(1)}, u32[]{:S(2)}, u32[]{:S(2)}) collective-permute-start(bf16[128,2048]{1,0:T(8,128)(2,1)S(1)} %get-tuple-element.97), channel_id=1, source_target_pairs={{4,0},{5,1},{6,2},{7,3},{12,8},{13,9},{14,10},{15,11},{20,16},{21,... | collective-permute-start | bytes 1572872 | tf_op jit(solution)/shard_map/ppermute | solution.py:13
  344.6 21.5 %collective-permute-start.17 = (f32[16,2048]{1,0:T(8,128)}, f32[16,2048]{1,0:T(8,128)}, u32[]{:S(2)}, u32[]{:S(2)}) collective-permute-start(f32[16,2048]{1,0:T(8,128)} %get-tuple-element.100), channel_id=1, source_target_pairs={{0,504},{8,0},{16,8},{24,16},{32,24},{40,32},{48,40},{56,48},{64,5... | collective-permute-start | bytes 393224 | tf_op jit(solution)/shard_map/ppermute | solution.py:18
  348.9 39.4 %collective-permute-start.23 = (f32[16,2048]{1,0:T(8,128)}, f32[16,2048]{1,0:T(8,128)}, u32[]{:S(2)}, u32[]{:S(2)}) collective-permute-start(f32[16,2048]{1,0:T(8,128)} %get-tuple-element.101), channel_id=1, source_target_pairs={{0,456},{8,464},{16,472},{24,480},{32,488},{40,496},{48,504},{56,0... | collective-permute-start | bytes 393224 | tf_op jit(solution)/shard_map/ppermute | solution.py:18
  353.8 38.9 %collective-permute-start.22 = (f32[16,2048]{1,0:T(8,128)}, f32[16,2048]{1,0:T(8,128)S(1)}, u32[]{:S(2)}, u32[]{:S(2)}) collective-permute-start(f32[16,2048]{1,0:T(8,128)} %get-tuple-element.102), channel_id=1, source_target_pairs={{0,464},{8,472},{16,480},{24,488},{32,496},{40,504},{48,0},{56,8},... | collective-permute-start | bytes 393224 | tf_op jit(solution)/shard_map/ppermute | solution.py:18
  357.1 35.6 %collective-permute-start.21 = (f32[16,2048]{1,0:T(8,128)}, f32[16,2048]{1,0:T(8,128)S(1)}, u32[]{:S(2)}, u32[]{:S(2)}) collective-permute-start(f32[16,2048]{1,0:T(8,128)} %get-tuple-element.103), channel_id=1, source_target_pairs={{0,472},{8,480},{16,488},{24,496},{32,504},{40,0},{48,8},{56,16},{... | collective-permute-start | bytes 393224 | tf_op jit(solution)/shard_map/ppermute | solution.py:18
  362.1 30.6 %collective-permute-start.20 = (f32[16,2048]{1,0:T(8,128)S(1)}, f32[16,2048]{1,0:T(8,128)S(1)}, u32[]{:S(2)}, u32[]{:S(2)}) collective-permute-start(f32[16,2048]{1,0:T(8,128)S(1)} %get-tuple-element.104), channel_id=1, source_target_pairs={{0,480},{8,488},{16,496},{24,504},{32,0},{40,8},{48,16},{56,24},{6... | collective-permute-start | bytes 393224 | tf_op jit(solution)/shard_map/ppermute | solution.py:18
  366.2 26.6 %collective-permute-start.19 = (f32[16,2048]{1,0:T(8,128)S(1)}, f32[16,2048]{1,0:T(8,128)S(1)}, u32[]{:S(2)}, u32[]{:S(2)}) collective-permute-start(f32[16,2048]{1,0:T(8,128)S(1)} %get-tuple-element.105), channel_id=1, source_target_pairs={{0,488},{8,496},{16,504},{24,0},{32,8},{40,16},{48,24},{56,32},{64... | collective-permute-start | bytes 393224 | tf_op jit(solution)/shard_map/ppermute | solution.py:18
  388.3 7.0 %copy-start.5 = (f32[16,2048]{1,0:T(8,128)S(1)}, f32[16,2048]{1,0:T(8,128)}, u32[]{:S(2)}) copy-start(f32[16,2048]{1,0:T(8,128)} %reduce-scatter.2.cloned.1.call-done) | copy-start | bytes 393220
  388.3 7.0 %collective-permute-start.18 = (f32[16,2048]{1,0:T(8,128)S(1)}, f32[16,2048]{1,0:T(8,128)S(1)}, u32[]{:S(2)}, u32[]{:S(2)}) collective-permute-start(f32[16,2048]{1,0:T(8,128)S(1)} %get-tuple-element.106), channel_id=1, source_target_pairs={{0,496},{8,504},{16,0},{24,8},{32,16},{40,24},{48,32},{56,40},{64,... | collective-permute-start | bytes 393224 | tf_op jit(solution)/shard_map/ppermute | solution.py:18
Sparse Core Ops, SparseCore 0:
  263.1 79.7 reduce-scatter.1
where the time goes:
time: 406 us; the launch traced here: 404 us
  starting transfers between devices  97.7 us (24%)
  blocking collectives  93.2 us (23%)
  matrix products  89.2 us (22%)
  waiting for transfers between devices  69.9 us (17%)
  local copies, waits for them, and re-layouts  27.2 us (7%)
  between operations  15.3 us (4%)
  other arithmetic  11.2 us (3%)
    all_gather x1, blocking collectives, on_device(): prompt_whole = lax.all_gather(chosen, 'seq', axis=0, tiled=True)  93.2 us
    ppermute x14, starting transfers between devices, passed_along(): lax.ppermute(value, axis, [(i, (i + by) % peers) for i in range(peers)])  71.7 us
    reduce_scatter x1, waiting for transfers between devices, on_device(): lax.psum_scatter(d_kv[:plen], 'seq', scatter_dimension=0, tiled=True)  67.3 us
    ppermute x10, starting transfers between devices, from_behind(): return lax.ppermute(block, axis, route)  26 us
    dot_general x8, matrix products, one_head(): jnp.einsum('grk,rgd->kd', weights_b, dh, preferred_element_type=jnp.float32)  21.3 us
    dot_general x8, matrix products, one_head(): jnp.einsum('grk,kd->rgd', weights_b, vh, preferred_element_type=jnp.float32)  18.3 us
    dot_general x8, matrix products, one_head(): jnp.einsum('rgd,kd->grk', dh, vh, preferred_element_type=jnp.float32)  17.2 us
    sub x8, matrix products, one_head(): expo = jnp.exp(scores - top)  15.1 us
  transfers between devices with their start and end apart: 25, of which 2 were waited for; matrix products, arithmetic and copies ran while one was open for 4% of the time, Pallas kernels for 0%

commit v1 on v0

v1 whole, which is shorter than its diff:
```python
import functools

import jax
import jax.numpy as jnp
from jax import lax
from jax.experimental import pallas as pl
from jax.experimental.pallas import tpu as pltpu
from jax.sharding import PartitionSpec as P

KVH = 8
HD = 128
SPREAD = 8
NEG = -1e30
LOG2E = 1.4426950408889634


def passed_along(value, axis, by):
    peers = lax.axis_size(axis)
    return lax.ppermute(value, axis, [(i, (i + by) % peers) for i in range(peers)])


def stacked(block):
    heads = block.shape[1] // HD
    return jnp.concatenate([block[:, h * HD : (h + 1) * HD] for h in range(heads)], axis=0)


def attention_kernel(span, info, q_ref, g_ref, k_ref, v_ref, pk_ref, pv_ref, start_ref,
                     dq_ref, dk_ref, dv_ref, dpk_ref, dpv_ref, bias):
    rows = q_ref.shape[0]
    heads = q_ref.shape[1] // HD
    plen = pk_ref.shape[0]
    window = (span + 1) * rows
    scale = HD ** -0.5
    first = pl.multiple_of(info[0], rows)
    own = info[1]

    @pl.when(pl.program_id(0) == 0)
    def _():
        k_ids = first + lax.broadcasted_iota(jnp.int32, (window, rows), 0)
        q_ids = own + lax.broadcasted_iota(jnp.int32, (window, rows), 1)
        seen = (k_ids >= start_ref[...]) & (k_ids <= q_ids)
        bias[...] = jnp.where(seen, 0.0, NEG)

    near = pl.ds(first, window)
    keys = jnp.concatenate([pk_ref[...], k_ref[near, :]], axis=0)
    values = jnp.concatenate([pv_ref[...], v_ref[near, :]], axis=0)
    q_rows = stacked(q_ref[...])
    g_rows = stacked(g_ref[...])
    nt = (((1,), (1,)), ((), ()))
    nn = (((1,), (0,)), ((), ()))
    tn = (((0,), (0,)), ((), ()))
    scores = lax.dot_general(keys, q_rows, nt, preferred_element_type=jnp.float32)
    shade = jnp.concatenate([bias[...]] * heads, axis=1)
    scores = jnp.concatenate([scores[:plen], scores[plen:] + shade], axis=0)
    top = jnp.max(scores, axis=0, keepdims=True)
    expo = jnp.exp2((scores - top) * (scale * LOG2E))
    weights = expo * (1.0 / jnp.sum(expo, axis=0, keepdims=True))
    d_weights = lax.dot_general(values, g_rows, nt, preferred_element_type=jnp.float32)
    delta = jnp.sum(weights * d_weights, axis=0, keepdims=True)
    d_scores = (weights * (d_weights - delta)).astype(jnp.bfloat16)
    weights_b = weights.astype(jnp.bfloat16)
    d_value = lax.dot_general(weights_b, g_rows, nn, preferred_element_type=jnp.float32)
    d_key = lax.dot_general(d_scores, q_rows, nn, preferred_element_type=jnp.float32) * scale
    d_query = lax.dot_general(d_scores, keys, tn, preferred_element_type=jnp.float32) * scale
    d_query = d_query.astype(jnp.bfloat16)
    for h in range(heads):
        dq_ref[:, h * HD : (h + 1) * HD] = d_query[h * rows : (h + 1) * rows]
    dpk_ref[...] = d_key[:plen].astype(dpk_ref.dtype)
    dpv_ref[...] = d_value[:plen].astype(dpv_ref.dtype)
    dk_ref[...] = jnp.zeros_like(dk_ref)
    dv_ref[...] = jnp.zeros_like(dv_ref)
    dk_ref[near, :] = d_key[plen:].astype(dk_ref.dtype)
    dv_ref[near, :] = d_value[plen:].astype(dv_ref.dtype)


def attend(q_rows, grad_rows, kv, prompt, q_start, first, own, span):
    rows, columns = q_rows.shape
    total = kv.shape[0]
    plen = prompt.shape[0]
    group = columns // KVH
    half = KVH * HD
    info = jnp.stack([first, own]).astype(jnp.int32)
    bf16 = jnp.bfloat16
    at = lambda n, col: pl.BlockSpec((n, col), lambda g, s: (0, g))
    later = lambda n: pl.BlockSpec((n, HD), lambda g, s: (0, KVH + g))
    pairs = (span + 1) * rows + plen
    return pl.pallas_call(
        functools.partial(attention_kernel, span),
        grid_spec=pltpu.PrefetchScalarGridSpec(
            num_scalar_prefetch=1,
            grid=(KVH,),
            in_specs=[
                at(rows, group),
                at(rows, group),
                at(total, HD),
                later(total),
                at(plen, HD),
                later(plen),
                pl.BlockSpec((1, rows), lambda g, s: (0, 0)),
            ],
            out_specs=[
                at(rows, group),
                at(total, HD),
                at(total, HD),
                at(plen, HD),
                at(plen, HD),
            ],
            scratch_shapes=[pltpu.VMEM(((span + 1) * rows, rows), jnp.float32)],
        ),
        out_shape=[
            jax.ShapeDtypeStruct((rows, columns), bf16),
            jax.ShapeDtypeStruct((total, half), bf16),
            jax.ShapeDtypeStruct((total, half), bf16),
            jax.ShapeDtypeStruct((plen, half), bf16),
            jax.ShapeDtypeStruct((plen, half), bf16),
        ],
        compiler_params=pltpu.CompilerParams(vmem_limit_bytes=48 * 1024 * 1024),
        cost_estimate=pl.CostEstimate(
            flops=10 * rows * columns * pairs,
            bytes_accessed=12 * 1024 * 1024,
            transcendentals=rows * columns * pairs // HD,
        ),
    )(info, q_rows, grad_rows, kv, kv, prompt, prompt, q_start[None])


def on_device(queries, resp_kv, prompt_kv, d_out, resp_lengths, prompt_home):
    q_rows = queries[0]
    own_kv = resp_kv[0]
    own_prompt = prompt_kv[0]
    grad_rows = d_out[0]
    rows = q_rows.shape[0]
    n_seq = lax.axis_size("seq")
    n_dp = lax.axis_size("dp")
    span = 5 * n_seq // 8
    me_seq = lax.axis_index("seq")
    me_dp = lax.axis_index("dp")
    offset = jnp.mod(me_dp - prompt_home[0], n_dp)

    kv = lax.all_gather(own_kv, "seq", axis=0, tiled=True)

    window = own_prompt[None]
    reach = 1
    while reach < SPREAD:
        window = jnp.concatenate([window, passed_along(window, "dp", reach)], axis=0)
        reach *= 2
    chosen = lax.dynamic_index_in_dim(window, offset, 0, keepdims=False)
    prompt = lax.all_gather(chosen, "seq", axis=0, tiled=True)

    lengths = resp_lengths[0]
    starts = jnp.cumsum(lengths) - lengths
    own = me_seq * rows
    q_ids = own + jnp.arange(rows, dtype=jnp.int32)
    q_start = jnp.max(jnp.where(starts[None, :] <= q_ids[:, None], starts[None, :], 0), axis=1)
    first = jnp.maximum(me_seq - span, 0) * rows
    d_query, d_key, d_value, d_pkey, d_pvalue = attend(
        q_rows, grad_rows, kv, prompt, q_start, first, own, span
    )

    prompt_grad = lax.psum_scatter(
        jnp.concatenate([d_pkey, d_pvalue], axis=1), "seq", scatter_dimension=0, tiled=True
    )
    d_kv = lax.psum_scatter(
        jnp.concatenate([d_key, d_value], axis=1), "seq", scatter_dimension=0, tiled=True
    )

    slots = jnp.arange(SPREAD, dtype=jnp.int32)[:, None, None]
    held = jnp.where(slots == offset, prompt_grad[None], jnp.zeros((), prompt_grad.dtype))
    reach = SPREAD // 2
    while reach > 0:
        arrived = passed_along(held[reach:], "dp", -reach)
        held = (held[:reach].astype(jnp.float32) + arrived.astype(jnp.float32)).astype(held.dtype)
        reach //= 2
    return (d_query[None], d_kv[None], held)


def solution(mesh):
    placed = (
        P("dp", "seq", None),
        P("dp", "seq", None),
        P("dp", "seq", None),
        P("dp", "seq", None),
        P("dp", None),
        P("dp"),
    )
    return jax.shard_map(
        on_device,
        mesh=mesh,
        in_specs=placed,
        out_specs=(P("dp", "seq", None), P("dp", "seq", None), P("dp", "seq", None)),
        check_vma=False,
    )
```

time: 406 us -> 211 us (0.52)
  the two profiles are of different devices: /device:TPU:24 before, /device:TPU:1 now
where the time goes in v1:
time: 211 us; the launch traced here: 208 us
  waiting for transfers between devices  103 us (49%)
  starting transfers between devices  30.1 us (14%)
  blocking collectives  28.6 us (14%)
  Pallas kernels  19.2 us (9%)
  between operations  14.5 us (7%)
  other arithmetic  10 us (5%)
  local copies, waits for them, and re-layouts  2.48 us (1%)
    reduce_scatter x1, waiting for transfers between devices, on_device(): lax.psum_scatter(jnp.concatenate([d_key, d_value], axis=1), 'seq', scatte...  36 us
    reduce_scatter x1, waiting for transfers between devices, on_device(): lax.psum_scatter(jnp.concatenate([d_pkey, d_pvalue], axis=1), 'seq', scat...  32.6 us
    ppermute x6, starting transfers between devices, passed_along(): lax.ppermute(value, axis, [(i, (i + by) % peers) for i in range(peers)])  30 us
    all_gather x1, blocking collectives, on_device(): prompt = lax.all_gather(chosen, 'seq', axis=0, tiled=True)  28.6 us
    ppermute x6, waiting for transfers between devices, passed_along(): lax.ppermute(value, axis, [(i, (i + by) % peers) for i in range(peers)])  27 us
    pallas_call x1, Pallas kernels, attend(): pl.pallas_call(functools.partial(attention_kernel, span), grid_spec=pltpu...  19.2 us
    all_gather x1, waiting for transfers between devices, on_device(): kv = lax.all_gather(own_kv, 'seq', axis=0, tiled=True)  6.62 us
  transfers between devices with their start and end apart: 9, of which 9 were waited for; matrix products, arithmetic and copies ran while one was open for 4% of the time, Pallas kernels for 0%

profile of v1, /device:TPU:1, one launch (start us, length us, event | category | flops | bytes accessed | tf_op | source)
XLA Modules:
  0.0 207.9 jit_solution(9695180909445200751)
XLA Ops:
  7.2 0.0 all-gather.4.cloned.1.call-start
  7.2 0.7 all-gather.4.cloned.1.call-update
  7.9 0.0 reduce-scatter.5.cloned.1.call-start
  7.9 4.8 %collective-permute-start = (bf16[1,16,2048]{2,1,0:T(8,128)(2,1)}, bf16[1,16,2048]{2,1,0:T(8,128)(2,1)S(1)}, u32[]{:S(2)}, u32[]{:S(2)}) collective-permute-start(bf16[1,16,2048]{2,1,0:T(8,128)(2,1)} %param.8), channel_id=1, source_target_pairs={{0,8},{8,16},{16,24},{24,32},{32,40},{40,48},{48,56},{56,64},{64,7... | collective-permute-start | bytes 196616 | tf_op jit(solution)/shard_map/ppermute | solution.py:19
  12.8 0.8 reduce-window_clone.1
  13.6 6.1 %collective-permute-done = bf16[1,16,2048]{2,1,0:T(8,128)(2,1)S(1)} collective-permute-done((bf16[1,16,2048]{2,1,0:T(8,128)(2,1)}, bf16[1,16,2048]{2,1,0:T(8,128)(2,1)S(1)}, u32[]{:S(2)}, u32[]{:S(2)}) %collective-permute-start) | collective-permute-done | bytes 65568 | tf_op jit(solution)/shard_map/ppermute | solution.py:19
  19.7 0.9 pad_maximum_fusion.3
  20.6 1.9 collective-permute-start.1
  22.5 0.7 subtract_bitcast_fusion
  23.2 6.4 %collective-permute-done.1 = bf16[2,16,2048]{2,1,0:T(8,128)(2,1)S(1)} collective-permute-done((bf16[2,16,2048]{2,1,0:T(8,128)(2,1)S(1)}, bf16[2,16,2048]{2,1,0:T(8,128)(2,1)S(1)}, u32[]{:S(2)}, u32[]{:S(2)}) %collective-permute-start.1) | collective-permute-done | bytes 131104 | tf_op jit(solution)/shard_map/ppermute | solution.py:19
  29.6 0.9 pad_maximum_fusion.2
  30.5 1.9 collective-permute-start.2
  33.1 0.1 pad_add_fusion.info
  33.2 0.1 select_reduce_fusion
  33.3 8.0 %collective-permute-done.2 = bf16[4,16,2048]{2,1,0:T(8,128)(2,1)S(1)} collective-permute-done((bf16[4,16,2048]{2,1,0:T(8,128)(2,1)S(1)}, bf16[4,16,2048]{2,1,0:T(8,128)(2,1)S(1)}, u32[]{:S(2)}, u32[]{:S(2)}) %collective-permute-start.2) | collective-permute-done | bytes 262176 | tf_op jit(solution)/shard_map/ppermute | solution.py:19
  41.2 0.1 fusion.2
  41.3 28.6 %all-gather.1 = bf16[1,128,2048]{2,1,0:T(8,128)(2,1)S(1)} all-gather(bf16[1,16,2048]{2,1,0:T(8,128)(2,1)S(1)} %fusion.2), channel_id=3, replica_groups=mesh['dp'=64,'seq'=8] {'seq'}, dimensions={1}, use_global_device_ids=true | all-gather | bytes 589824 | tf_op jit(solution)/shard_map/all_gather | solution.py:147
  69.9 6.6 %all-gather.4.cloned.1.call-done = bf16[1,1024,2048]{2,1,0:T(8,128)(2,1)} async-done(((bf16[1,128,2048]{2,1,0:T(8,128)(2,1)}), bf16[1,1024,2048]{2,1,0:T(8,128)(2,1)}) %all-gather.4.cloned.1.call-update) | async-done | bytes 4194320 | tf_op jit(solution)/shard_map/all_gather | solution.py:139
  76.5 0.0 copy-start
  76.5 1.2 copy-done
  77.8 0.0 copy-start.1
  77.8 1.2 copy-done.1
  79.0 19.2 %shard_map.85 = (bf16[128,4096]{1,0:T(8,128)(2,1)}, bf16[1024,1024]{1,0:T(8,128)(2,1)S(1)}, bf16[1024,1024]{1,0:T(8,128)(2,1)}, bf16[128,1024]{1,0:T(8,128)(2,1)S(1)}, bf16[128,1024]{1,0:T(8,128)(2,1)S(1)}) custom-call(s32[2]{0:T(128)S(1)} %pad_add_fusion.info, bf16[128,4096]{1,0:T(8,128)(2,1)S(1)} %bitcast.15, bf16[128,4096]{1,0:T(8,128)(2,1)S(1)} %bitcast.16, ...), custom_call_target="tpu_custom_call" | custom-call | flops 4697620480 | bytes 12582912 | tf_op jit(solution)/shard_map/pallas_call | solution.py:87
  98.1 0.9 pad_maximum_fusion.1
  99.0 0.0 reduce-scatter.5.cloned.1.call-update
  99.0 0.0 reduce-scatter.3.cloned.1.call-start
  99.1 4.1 %pad_maximum_fusion = bf16[1024,2048]{1,0:T(8,128)(2,1)} fusion(bf16[1024,1024]{1,0:T(8,128)(2,1)} %get-tuple-element.10, bf16[1024,1024]{1,0:T(8,128)(2,1)S(1)} %get-tuple-element.9), kind=kLoop, calls=%fused_computation | loop fusion | flops 8388608 | bytes 8388608 | tf_op jit(solution)/shard_map/concatenate | solution.py:163
  103.1 0.0 reduce-scatter.3.cloned.1.call-update
  103.2 32.6 %reduce-scatter.5.cloned.1.call-done = bf16[16,2048]{1,0:T(8,128)(2,1)} async-done(((bf16[128,2048]{1,0:T(8,128)(2,1)}), bf16[16,2048]{1,0:T(8,128)(2,1)}) %reduce-scatter.5.cloned.1.call-update) | async-done | bytes 65552 | tf_op jit(solution)/shard_map/reduce_scatter | solution.py:159
  135.8 0.9 broadcast_select_fusion
  136.7 6.9 %collective-permute-start.3 = (bf16[4,16,2048]{2,1,0:T(8,128)(2,1)S(1)}, bf16[4,16,2048]{2,1,0:T(8,128)(2,1)S(1)}, u32[]{:S(2)}, u32[]{:S(2)}) collective-permute-start(bf16[4,16,2048]{2,1,0:T(8,128)(2,1)S(1)} %slice.25), channel_id=1, source_target_pairs={{0,480},{8,488},{16,496},{24,504},{32,0},{40,8},{48,16},{56,24},{6... | collective-permute-start | bytes 786440 | tf_op jit(solution)/shard_map/ppermute | solution.py:19
  143.6 3.3 %collective-permute-done.3 = bf16[4,16,2048]{2,1,0:T(8,128)(2,1)S(1)} collective-permute-done((bf16[4,16,2048]{2,1,0:T(8,128)(2,1)S(1)}, bf16[4,16,2048]{2,1,0:T(8,128)(2,1)S(1)}, u32[]{:S(2)}, u32[]{:S(2)}) %collective-permute-start.3) | collective-permute-done | bytes 262176 | tf_op jit(solution)/shard_map/ppermute | solution.py:19
  146.9 0.1 add_convert_fusion
  147.0 7.1 %collective-permute-start.4 = (bf16[2,16,2048]{2,1,0:T(8,128)(2,1)S(1)}, bf16[2,16,2048]{2,1,0:T(8,128)(2,1)S(1)}, u32[]{:S(2)}, u32[]{:S(2)}) collective-permute-start(bf16[2,16,2048]{2,1,0:T(8,128)(2,1)S(1)} %slice.27), channel_id=1, source_target_pairs={{0,496},{8,504},{16,0},{24,8},{32,16},{40,24},{48,32},{56,40},{64,... | collective-permute-start | bytes 393224 | tf_op jit(solution)/shard_map/ppermute | solution.py:19
  154.1 1.9 collective-permute-done.4
  156.0 7.4 %collective-permute-start.5 = (bf16[1,16,2048]{2,1,0:T(8,128)(2,1)S(1)}, bf16[1,16,2048]{2,1,0:T(8,128)(2,1)S(1)}, u32[]{:S(2)}, u32[]{:S(2)}) collective-permute-start(bf16[1,16,2048]{2,1,0:T(8,128)(2,1)S(1)} %slice.29), channel_id=1, source_target_pairs={{0,504},{8,0},{16,8},{24,16},{32,24},{40,32},{48,40},{56,48},{64,5... | collective-permute-start | bytes 196616 | tf_op jit(solution)/shard_map/ppermute | solution.py:19
  163.5 1.3 collective-permute-done.5
  164.8 0.6 add_convert_fusion.2
  165.4 36.0 %reduce-scatter.3.cloned.1.call-done = bf16[128,2048]{1,0:T(8,128)(2,1)} async-done(((bf16[1024,2048]{1,0:T(8,128)(2,1)}), bf16[128,2048]{1,0:T(8,128)(2,1)}) %reduce-scatter.3.cloned.1.call-update) | async-done | bytes 524304 | tf_op jit(solution)/shard_map/reduce_scatter | solution.py:162
  (6 shorter events, 0.1 us)
Async XLA Ops:
  7.2 69.4 %all-gather.4.cloned.1.call-start = ((), (), s32[]{:S(2)}) async-start(), calls=%async_computation.4 | async-start | bytes 4718592 | tf_op jit(solution)/shard_map/all_gather | solution.py:139
  7.9 127.9 %reduce-scatter.5.cloned.1.call-start = ((), (), s32[]{:S(2)}) async-start(), calls=%async_computation.3 | async-start | bytes 589824 | tf_op jit(solution)/shard_map/reduce_scatter | solution.py:159
  7.9 11.8 %collective-permute-start = (bf16[1,16,2048]{2,1,0:T(8,128)(2,1)}, bf16[1,16,2048]{2,1,0:T(8,128)(2,1)S(1)}, u32[]{:S(2)}, u32[]{:S(2)}) collective-permute-start(bf16[1,16,2048]{2,1,0:T(8,128)(2,1)} %param.8), channel_id=1, source_target_pairs={{0,8},{8,16},{16,24},{24,32},{32,40},{40,48},{48,56},{56,64},{64,7... | collective-permute-start | bytes 196616 | tf_op jit(solution)/shard_map/ppermute | solution.py:19
  20.6 9.0 %collective-permute-start.1 = (bf16[2,16,2048]{2,1,0:T(8,128)(2,1)S(1)}, bf16[2,16,2048]{2,1,0:T(8,128)(2,1)S(1)}, u32[]{:S(2)}, u32[]{:S(2)}) collective-permute-start(bf16[2,16,2048]{2,1,0:T(8,128)(2,1)S(1)} %pad_maximum_fusion.3), channel_id=1, source_target_pairs={{0,16},{8,24},{16,32},{24,40},{32,48},{40,56},{48,64},{56,72},{64,... | collective-permute-start | bytes 393224 | tf_op jit(solution)/shard_map/ppermute | solution.py:19
  30.5 10.7 %collective-permute-start.2 = (bf16[4,16,2048]{2,1,0:T(8,128)(2,1)S(1)}, bf16[4,16,2048]{2,1,0:T(8,128)(2,1)S(1)}, u32[]{:S(2)}, u32[]{:S(2)}) collective-permute-start(bf16[4,16,2048]{2,1,0:T(8,128)(2,1)S(1)} %pad_maximum_fusion.2), channel_id=1, source_target_pairs={{0,32},{8,40},{16,48},{24,56},{32,64},{40,72},{48,80},{56,88},{64,... | collective-permute-start | bytes 786440 | tf_op jit(solution)/shard_map/ppermute | solution.py:19
  76.5 1.2 copy-start
  77.8 1.2 copy-start.1
  99.0 102.4 %reduce-scatter.3.cloned.1.call-start = ((), (), s32[]{:S(2)}) async-start(), calls=%async_computation.2 | async-start | bytes 4718592 | tf_op jit(solution)/shard_map/reduce_scatter | solution.py:162
  136.7 10.2 %collective-permute-start.3 = (bf16[4,16,2048]{2,1,0:T(8,128)(2,1)S(1)}, bf16[4,16,2048]{2,1,0:T(8,128)(2,1)S(1)}, u32[]{:S(2)}, u32[]{:S(2)}) collective-permute-start(bf16[4,16,2048]{2,1,0:T(8,128)(2,1)S(1)} %slice.25), channel_id=1, source_target_pairs={{0,480},{8,488},{16,496},{24,504},{32,0},{40,8},{48,16},{56,24},{6... | collective-permute-start | bytes 786440 | tf_op jit(solution)/shard_map/ppermute | solution.py:19
  147.0 9.0 %collective-permute-start.4 = (bf16[2,16,2048]{2,1,0:T(8,128)(2,1)S(1)}, bf16[2,16,2048]{2,1,0:T(8,128)(2,1)S(1)}, u32[]{:S(2)}, u32[]{:S(2)}) collective-permute-start(bf16[2,16,2048]{2,1,0:T(8,128)(2,1)S(1)} %slice.27), channel_id=1, source_target_pairs={{0,496},{8,504},{16,0},{24,8},{32,16},{40,24},{48,32},{56,40},{64,... | collective-permute-start | bytes 393224 | tf_op jit(solution)/shard_map/ppermute | solution.py:19
  156.0 8.7 %collective-permute-start.5 = (bf16[1,16,2048]{2,1,0:T(8,128)(2,1)S(1)}, bf16[1,16,2048]{2,1,0:T(8,128)(2,1)S(1)}, u32[]{:S(2)}, u32[]{:S(2)}) collective-permute-start(bf16[1,16,2048]{2,1,0:T(8,128)(2,1)S(1)} %slice.29), channel_id=1, source_target_pairs={{0,504},{8,0},{16,8},{24,16},{32,24},{40,32},{48,40},{56,48},{64,5... | collective-permute-start | bytes 196616 | tf_op jit(solution)/shard_map/ppermute | solution.py:19
Sparse Core Ops, SparseCore 0:
  10.1 66.3 all-gather.3
  99.1 36.5 reduce-scatter.4
  139.4 61.9 reduce-scatter.2

commit v2 on v1

--- a/solution.py
+++ b/solution.py
@@ -25,25 +25,30 @@
 
 
 def attention_kernel(span, info, q_ref, g_ref, k_ref, v_ref, pk_ref, pv_ref, start_ref,
-                     dq_ref, dk_ref, dv_ref, dpk_ref, dpv_ref, bias):
+                     dq_ref, keep_ref, give_ref, dp_ref, bias):
     rows = q_ref.shape[0]
     heads = q_ref.shape[1] // HD
     plen = pk_ref.shape[0]
+    half = KVH * HD
     window = (span + 1) * rows
     scale = HD ** -0.5
-    first = pl.multiple_of(info[0], rows)
-    own = info[1]
-
-    @pl.when(pl.program_id(0) == 0)
+    me = info[0]
+    head = pl.program_id(0)
+
+    @pl.when(head == 0)
     def _():
-        k_ids = first + lax.broadcasted_iota(jnp.int32, (window, rows), 0)
+        own = me * rows
+        k_ids = own - span * rows + lax.broadcasted_iota(jnp.int32, (window, rows), 0)
         q_ids = own + lax.broadcasted_iota(jnp.int32, (window, rows), 1)
         seen = (k_ids >= start_ref[...]) & (k_ids <= q_ids)
         bias[...] = jnp.where(seen, 0.0, NEG)
 
-    near = pl.ds(first, window)
-    keys = jnp.concatenate([pk_ref[...], k_ref[near, :]], axis=0)
-    values = jnp.concatenate([pv_ref[...], v_ref[near, :]], axis=0)
+    near = [
+        pl.ds(pl.multiple_of(jnp.maximum(me - back, 0) * rows, rows), rows)
+        for back in range(span, -1, -1)
+    ]
+    keys = jnp.concatenate([pk_ref[...]] + [k_ref[at, :] for at in near], axis=0)
+    values = jnp.concatenate([pv_ref[...]] + [v_ref[at, :] for at in near], axis=0)
     q_rows = stacked(q_ref[...])
     g_rows = stacked(g_ref[...])
     nt = (((1,), (1,)), ((), ()))
@@ -65,25 +70,26 @@
     d_query = d_query.astype(jnp.bfloat16)
     for h in range(heads):
         dq_ref[:, h * HD : (h + 1) * HD] = d_query[h * rows : (h + 1) * rows]
-    dpk_ref[...] = d_key[:plen].astype(dpk_ref.dtype)
-    dpv_ref[...] = d_value[:plen].astype(dpv_ref.dtype)
-    dk_ref[...] = jnp.zeros_like(dk_ref)
-    dv_ref[...] = jnp.zeros_like(dv_ref)
-    dk_ref[near, :] = d_key[plen:].astype(dk_ref.dtype)
-    dv_ref[near, :] = d_value[plen:].astype(dv_ref.dtype)
-
-
-def attend(q_rows, grad_rows, kv, prompt, q_start, first, own, span):
+    for part, base in ((d_key, 0), (d_value, half)):
+        part = part.astype(jnp.bfloat16)
+        columns = pl.ds(pl.multiple_of(base + head * HD, HD), HD)
+        dp_ref[:, columns] = part[:plen]
+        for back in range(span + 1):
+            block = part[plen + (span - back) * rows : plen + (span - back + 1) * rows]
+            into = (keep_ref, give_ref)[back % 2]
+            into[back // 2, :, columns] = block
+
+
+def attend(q_rows, grad_rows, kv, prompt, q_start, me, span):
     rows, columns = q_rows.shape
-    total = kv.shape[0]
+    total, width = kv.shape
     plen = prompt.shape[0]
     group = columns // KVH
-    half = KVH * HD
-    info = jnp.stack([first, own]).astype(jnp.int32)
     bf16 = jnp.bfloat16
     at = lambda n, col: pl.BlockSpec((n, col), lambda g, s: (0, g))
     later = lambda n: pl.BlockSpec((n, HD), lambda g, s: (0, KVH + g))
     pairs = (span + 1) * rows + plen
+    kept, given = span // 2 + 1, (span + 1) // 2
     return pl.pallas_call(
         functools.partial(attention_kernel, span),
         grid_spec=pltpu.PrefetchScalarGridSpec(
@@ -100,27 +106,54 @@
             ],
             out_specs=[
                 at(rows, group),
-                at(total, HD),
-                at(total, HD),
-                at(plen, HD),
-                at(plen, HD),
+                pl.BlockSpec((kept, rows, width), lambda g, s: (0, 0, 0)),
+                pl.BlockSpec((given, rows, width), lambda g, s: (0, 0, 0)),
+                pl.BlockSpec((plen, width), lambda g, s: (0, 0)),
             ],
             scratch_shapes=[pltpu.VMEM(((span + 1) * rows, rows), jnp.float32)],
         ),
         out_shape=[
             jax.ShapeDtypeStruct((rows, columns), bf16),
-            jax.ShapeDtypeStruct((total, half), bf16),
-            jax.ShapeDtypeStruct((total, half), bf16),
-            jax.ShapeDtypeStruct((plen, half), bf16),
-            jax.ShapeDtypeStruct((plen, half), bf16),
+            jax.ShapeDtypeStruct((kept, rows, width), bf16),
+            jax.ShapeDtypeStruct((given, rows, width), bf16),
+            jax.ShapeDtypeStruct((plen, width), bf16),
         ],
-        compiler_params=pltpu.CompilerParams(vmem_limit_bytes=48 * 1024 * 1024),
+        compiler_params=pltpu.CompilerParams(vmem_limit_bytes=56 * 1024 * 1024),
         cost_estimate=pl.CostEstimate(
             flops=10 * rows * columns * pairs,
             bytes_accessed=12 * 1024 * 1024,
             transcendentals=rows * columns * pairs // HD,
         ),
-    )(info, q_rows, grad_rows, kv, kv, prompt, prompt, q_start[None])
+    )(me.astype(jnp.int32)[None], q_rows, grad_rows, kv, kv, prompt, prompt, q_start[None])
+
+
+def added(*parts):
+    total = parts[0].astype(jnp.float32)
+    for part in parts[1:]:
+        total = total + part.astype(jnp.float32)
+    return total.astype(jnp.bfloat16)
+
+
+def gradients_home(keep, give, me_seq):
+    n = lax.axis_size("seq")
+    rows = keep.shape[1]
+    cut = rows // 2
+    odd = jnp.mod(me_seq, 2) == 1
+    got = lax.ppermute(give, "seq", [(i, i ^ 1) for i in range(n)])
+    none = jnp.zeros_like(got[:1])
+    sums = added(
+        jnp.concatenate([keep, none]),
+        jnp.where(odd, jnp.concatenate([none, got]), jnp.concatenate([got, none])),
+    )
+    own, one, two, three = sums[0], sums[1], sums[2], sums[3]
+    back = lax.ppermute(two[:cut], "seq", [(i, i - 2) for i in range(4, n)])
+    ahead = lax.ppermute(two[cut:], "seq", [(i, (i + 2) % n) for i in range(4, n)])
+    zero = jnp.zeros_like(back)
+    one = added(one, jnp.concatenate([back, zero]))
+    three = added(three, jnp.concatenate([zero, ahead]))
+    from_next = lax.ppermute(one, "seq", [(i, i - 2) for i in range(2, n)])
+    from_last = lax.ppermute(three, "seq", [(i, (i + 2) % n) for i in (n - 2, n - 1, 0, 1)])
+    return added(own, from_next, from_last)
 
 
 def on_device(queries, resp_kv, prompt_kv, d_out, resp_lengths, prompt_home):
@@ -148,20 +181,13 @@
 
     lengths = resp_lengths[0]
     starts = jnp.cumsum(lengths) - lengths
-    own = me_seq * rows
-    q_ids = own + jnp.arange(rows, dtype=jnp.int32)
+    q_ids = me_seq * rows + jnp.arange(rows, dtype=jnp.int32)
     q_start = jnp.max(jnp.where(starts[None, :] <= q_ids[:, None], starts[None, :], 0), axis=1)
-    first = jnp.maximum(me_seq - span, 0) * rows
-    d_query, d_key, d_value, d_pkey, d_pvalue = attend(
-        q_rows, grad_rows, kv, prompt, q_start, first, own, span
-    )
-
-    prompt_grad = lax.psum_scatter(
-        jnp.concatenate([d_pkey, d_pvalue], axis=1), "seq", scatter_dimension=0, tiled=True
-    )
-    d_kv = lax.psum_scatter(
-        jnp.concatenate([d_key, d_value], axis=1), "seq", scatter_dimension=0, tiled=True
-    )
+    d_query, keep, give, d_prompt = attend(
+        q_rows, grad_rows, kv, prompt, q_start, me_seq, span
+    )
+    prompt_grad = lax.psum_scatter(d_prompt, "seq", scatter_dimension=0, tiled=True)
+    d_kv = gradients_home(keep, give, me_seq)
 
     slots = jnp.arange(SPREAD, dtype=jnp.int32)[:, None, None]
     held = jnp.where(slots == offset, prompt_grad[None], jnp.zeros((), prompt_grad.dtype))

time: 211 us -> 199 us (0.943); the launches traced: 208 us -> 198 us
  waiting for transfers between devices: 103 us -> 85.3 us
  starting transfers between devices: 30.1 us -> 42.7 us
  other arithmetic: 10 us -> 7.49 us
  local copies, waits for them, and re-layouts: 2.48 us -> 0.08 us
    reduce_scatter x2 -> x1, waiting for transfers between devices: 68.6 us -> 36.7 us  [on_device(): lax.psum_scatter(d_prompt, 'seq', scatter_dimension=0, tiled=True)]
    ppermute x0 -> x5, waiting for transfers between devices: none -> 19.7 us  [the longest x1 13.6 us: gradients_home(): from_next = lax.ppermute(one, 'seq', [(i, i - 2) for i in range(2, n)])]
    ppermute x0 -> x5, starting transfers between devices: none -> 14.6 us  [the longest x1 9.02 us: gradients_home(): lax.ppermute(three, 'seq', [(i, (i + 2) % n) for i in (n - 2, n - 1, 0, 1)])]
    ppermute x6, waiting for transfers between devices: 27 us -> 22 us  [passed_along(): lax.ppermute(value, axis, [(i, (i + by) % peers) for i in range(peers)])]
    concatenate x2 -> x0, other arithmetic: 4.91 us -> none  [the longest x1 4.06 us: on_device(): jnp.concatenate([d_key, d_value], axis=1)]
    unnamed x4 -> x2, local copies, waits for them, and re-layouts: 2.45 us -> 0.01 us
  transfers between devices with their start and end apart: 9 -> 13, of which waited for: 9 -> 10; matrix products, arithmetic and copies ran while one was open for 4% -> 3% of each run, Pallas kernels for 0% -> 0%
where the time goes in v2:
time: 199 us; the launch traced here: 198 us
  waiting for transfers between devices  85.3 us (43%)
  starting transfers between devices  42.7 us (21%)
  blocking collectives  29.1 us (15%)
  Pallas kernels  18.6 us (9%)
  between operations  14.9 us (7%)
  other arithmetic  7.49 us (4%)
    reduce_scatter x1, waiting for transfers between devices, on_device(): lax.psum_scatter(d_prompt, 'seq', scatter_dimension=0, tiled=True)  36.7 us
    all_gather x1, blocking collectives, on_device(): prompt = lax.all_gather(chosen, 'seq', axis=0, tiled=True)  29.1 us
    ppermute x6, starting transfers between devices, passed_along(): lax.ppermute(value, axis, [(i, (i + by) % peers) for i in range(peers)])  28.1 us
    ppermute x6, waiting for transfers between devices, passed_along(): lax.ppermute(value, axis, [(i, (i + by) % peers) for i in range(peers)])  22 us
    pallas_call x1, Pallas kernels, attend(): pl.pallas_call(functools.partial(attention_kernel, span), grid_spec=pltpu...  18.6 us
    ppermute x1, waiting for transfers between devices, gradients_home(): from_next = lax.ppermute(one, 'seq', [(i, i - 2) for i in range(2, n)])  13.6 us
    ppermute x1, starting transfers between devices, gradients_home(): lax.ppermute(three, 'seq', [(i, (i + 2) % n) for i in (n - 2, n - 1, 0, 1)])  9.02 us
    all_gather x1, waiting for transfers between devices, on_device(): kv = lax.all_gather(own_kv, 'seq', axis=0, tiled=True)  6.17 us
  transfers between devices with their start and end apart: 13, of which 10 were waited for; matrix products, arithmetic and copies ran while one was open for 3% of the time, Pallas kernels for 0%

profile of v2, /device:TPU:1, one launch (start us, length us, event | category | flops | bytes accessed | tf_op | source)
XLA Modules:
  0.0 198.2 jit_solution(2620907400613849906)
XLA Ops:
  7.2 0.0 all-gather.4.cloned.1.call-start
  7.2 0.7 all-gather.4.cloned.1.call-update
  7.9 0.0 reduce-scatter.2.cloned.1.call-start
  7.9 4.8 %collective-permute-start = (bf16[1,16,2048]{2,1,0:T(8,128)(2,1)}, bf16[1,16,2048]{2,1,0:T(8,128)(2,1)S(1)}, u32[]{:S(2)}, u32[]{:S(2)}) collective-permute-start(bf16[1,16,2048]{2,1,0:T(8,128)(2,1)} %param.8), channel_id=1, source_target_pairs={{0,8},{8,16},{16,24},{24,32},{32,40},{40,48},{48,56},{56,64},{64,7... | collective-permute-start | bytes 196616 | tf_op jit(solution)/shard_map/ppermute | solution.py:19
  12.8 7.0 %collective-permute-done = bf16[1,16,2048]{2,1,0:T(8,128)(2,1)S(1)} collective-permute-done((bf16[1,16,2048]{2,1,0:T(8,128)(2,1)}, bf16[1,16,2048]{2,1,0:T(8,128)(2,1)S(1)}, u32[]{:S(2)}, u32[]{:S(2)}) %collective-permute-start) | collective-permute-done | bytes 65568 | tf_op jit(solution)/shard_map/ppermute | solution.py:19
  19.7 0.9 pad_maximum_fusion.1
  20.6 1.9 collective-permute-start.1
  22.5 0.8 reduce-window_clone.1
  23.3 6.3 %collective-permute-done.1 = bf16[2,16,2048]{2,1,0:T(8,128)(2,1)S(1)} collective-permute-done((bf16[2,16,2048]{2,1,0:T(8,128)(2,1)S(1)}, bf16[2,16,2048]{2,1,0:T(8,128)(2,1)S(1)}, u32[]{:S(2)}, u32[]{:S(2)}) %collective-permute-start.1) | collective-permute-done | bytes 131104 | tf_op jit(solution)/shard_map/ppermute | solution.py:19
  29.6 0.9 pad_maximum_fusion
  30.5 1.9 collective-permute-start.2
  32.4 0.7 subtract_bitcast_fusion
  33.8 0.7 select_reduce_fusion
  34.4 6.8 %collective-permute-done.2 = bf16[4,16,2048]{2,1,0:T(8,128)(2,1)S(1)} collective-permute-done((bf16[4,16,2048]{2,1,0:T(8,128)(2,1)S(1)}, bf16[4,16,2048]{2,1,0:T(8,128)(2,1)S(1)}, u32[]{:S(2)}, u32[]{:S(2)}) %collective-permute-start.2) | collective-permute-done | bytes 262176 | tf_op jit(solution)/shard_map/ppermute | solution.py:19
  41.2 0.1 fusion.7
  41.3 29.1 %all-gather.1 = bf16[1,128,2048]{2,1,0:T(8,128)(2,1)} all-gather(bf16[1,16,2048]{2,1,0:T(8,128)(2,1)S(1)} %fusion.7), channel_id=3, replica_groups=mesh['dp'=64,'seq'=8] {'seq'}, dimensions={1}, use_global_device_ids=true | all-gather | bytes 589824 | tf_op jit(solution)/shard_map/all_gather | solution.py:180
  70.4 6.2 %all-gather.4.cloned.1.call-done = bf16[1,1024,2048]{2,1,0:T(8,128)(2,1)} async-done(((bf16[1,128,2048]{2,1,0:T(8,128)(2,1)}), bf16[1,1024,2048]{2,1,0:T(8,128)(2,1)}) %all-gather.4.cloned.1.call-update) | async-done | bytes 4194320 | tf_op jit(solution)/shard_map/all_gather | solution.py:172
  76.5 18.6 %shard_map.85 = (bf16[128,4096]{1,0:T(8,128)(2,1)}, bf16[3,128,2048]{2,1,0:T(8,128)(2,1)}, bf16[3,128,2048]{2,1,0:T(8,128)(2,1)}, bf16[128,2048]{1,0:T(8,128)(2,1)}) custom-call(s32[1]{0:T(128)} %bitcast.info, bf16[128,4096]{1,0:T(8,128)(2,1)} %bitcast.36, bf16[128,4096]{1,0:T(8,128)(2,1)} %bitcast.37, bf16[1024,2048]{1,0:T(8,128)(2,1)} %bitcast.34, ...), custom_call_target="tpu_custom_call" | custom-call | flops 4697620480 | bytes 12582912 | tf_op jit(solution)/shard_map/pallas_call | solution.py:93
  95.1 0.0 copy-start
  95.1 2.3 %collective-permute-start.3 = (bf16[3,128,2048]{2,1,0:T(8,128)(2,1)}, bf16[3,128,2048]{2,1,0:T(8,128)(2,1)S(1)}, u32[]{:S(2)}, u32[]{:S(2)}) collective-permute-start(bf16[3,128,2048]{2,1,0:T(8,128)(2,1)} %get-tuple-element.9), channel_id=1, source_target_pairs={{0,1},{1,0},{2,3},{3,2},{4,5},{5,4},{6,7},{7,6},{8,9},{9,8},{10,11... | collective-permute-start | bytes 4718600 | tf_op jit(solution)/shard_map/ppermute | solution.py:142
  97.5 0.0 reduce-scatter.2.cloned.1.call-update
  97.5 36.7 %reduce-scatter.2.cloned.1.call-done = bf16[16,2048]{1,0:T(8,128)(2,1)} async-done(((bf16[128,2048]{1,0:T(8,128)(2,1)}), bf16[16,2048]{1,0:T(8,128)(2,1)}) %reduce-scatter.2.cloned.1.call-update) | async-done | bytes 65552 | tf_op jit(solution)/shard_map/reduce_scatter | solution.py:189
  134.3 0.9 broadcast_select_fusion
  135.2 6.8 %collective-permute-start.8 = (bf16[4,16,2048]{2,1,0:T(8,128)(2,1)S(1)}, bf16[4,16,2048]{2,1,0:T(8,128)(2,1)S(1)}, u32[]{:S(2)}, u32[]{:S(2)}) collective-permute-start(bf16[4,16,2048]{2,1,0:T(8,128)(2,1)S(1)} %slice.61), channel_id=1, source_target_pairs={{0,480},{8,488},{16,496},{24,504},{32,0},{40,8},{48,16},{56,24},{6... | collective-permute-start | bytes 786440 | tf_op jit(solution)/shard_map/ppermute | solution.py:19
  142.1 0.0 collective-permute-done.3
  142.1 0.0 copy-done
  142.1 0.6 add_convert_fusion
  142.8 0.7 collective-permute-start.4
  143.5 1.3 collective-permute-start.6
  144.8 0.6 collective-permute-done.8
  145.4 0.1 add_convert_fusion.1
  145.4 7.1 %collective-permute-start.9 = (bf16[2,16,2048]{2,1,0:T(8,128)(2,1)S(1)}, bf16[2,16,2048]{2,1,0:T(8,128)(2,1)S(1)}, u32[]{:S(2)}, u32[]{:S(2)}) collective-permute-start(bf16[2,16,2048]{2,1,0:T(8,128)(2,1)S(1)} %slice.63), channel_id=1, source_target_pairs={{0,496},{8,504},{16,0},{24,8},{32,16},{40,24},{48,32},{56,40},{64,... | collective-permute-start | bytes 393224 | tf_op jit(solution)/shard_map/ppermute | solution.py:19
  152.6 0.0 collective-permute-done.4
  152.6 2.9 %collective-permute-done.6 = bf16[64,2048]{1,0:T(8,128)(2,1)S(1)} collective-permute-done((bf16[64,2048]{1,0:T(8,128)(2,1)S(1)}, bf16[64,2048]{1,0:T(8,128)(2,1)S(1)}, u32[]{:S(2)}, u32[]{:S(2)}) %collective-permute-start.6) | collective-permute-done | bytes 262176 | tf_op jit(solution)/shard_map/ppermute | solution.py:150
  155.5 0.2 fusion.1
  155.6 1.3 collective-permute-start.5
  156.9 9.0 %collective-permute-start.7 = (bf16[128,2048]{1,0:T(8,128)(2,1)S(1)}, bf16[128,2048]{1,0:T(8,128)(2,1)S(1)}, u32[]{:S(2)}, u32[]{:S(2)}) collective-permute-start(bf16[128,2048]{1,0:T(8,128)(2,1)S(1)} %get-tuple-element.12), channel_id=1, source_target_pairs={{6,0},{7,1},{0,2},{1,3},{14,8},{15,9},{8,10},{9,11},{22,16},{23,17... | collective-permute-start | bytes 1572872 | tf_op jit(solution)/shard_map/ppermute | solution.py:155
  166.0 0.0 collective-permute-done.9
  166.0 5.4 %collective-permute-start.10 = (bf16[1,16,2048]{2,1,0:T(8,128)(2,1)S(1)}, bf16[1,16,2048]{2,1,0:T(8,128)(2,1)S(1)}, u32[]{:S(2)}, u32[]{:S(2)}) collective-permute-start(bf16[1,16,2048]{2,1,0:T(8,128)(2,1)S(1)} %slice.65), channel_id=1, source_target_pairs={{0,504},{8,0},{16,8},{24,16},{32,24},{40,32},{48,40},{56,48},{64,5... | collective-permute-start | bytes 196616 | tf_op jit(solution)/shard_map/ppermute | solution.py:19
  171.5 1.4 collective-permute-done.10
  172.8 0.6 add_convert_fusion.3
  173.5 13.6 %collective-permute-done.5 = bf16[128,2048]{1,0:T(8,128)(2,1)S(1)} collective-permute-done((bf16[128,2048]{1,0:T(8,128)(2,1)S(1)}, bf16[128,2048]{1,0:T(8,128)(2,1)S(1)}, u32[]{:S(2)}, u32[]{:S(2)}) %collective-permute-start.5) | collective-permute-done | bytes 524320 | tf_op jit(solution)/shard_map/ppermute | solution.py:154
  187.1 3.3 %collective-permute-done.7 = bf16[128,2048]{1,0:T(8,128)(2,1)S(1)} collective-permute-done((bf16[128,2048]{1,0:T(8,128)(2,1)S(1)}, bf16[128,2048]{1,0:T(8,128)(2,1)S(1)}, u32[]{:S(2)}, u32[]{:S(2)}) %collective-permute-start.7) | collective-permute-done | bytes 524320 | tf_op jit(solution)/shard_map/ppermute | solution.py:155
  190.4 1.0 fusion.4
  (7 shorter events, 0.1 us)
Async XLA Ops:
  7.2 69.4 %all-gather.4.cloned.1.call-start = ((), (), s32[]{:S(2)}) async-start(), calls=%async_computation.2 | async-start | bytes 4718592 | tf_op jit(solution)/shard_map/all_gather | solution.py:172
  7.9 126.4 %reduce-scatter.2.cloned.1.call-start = ((), (), s32[]{:S(2)}) async-start(), calls=%async_computation.1 | async-start | bytes 589824 | tf_op jit(solution)/shard_map/reduce_scatter | solution.py:189
  7.9 11.8 %collective-permute-start = (bf16[1,16,2048]{2,1,0:T(8,128)(2,1)}, bf16[1,16,2048]{2,1,0:T(8,128)(2,1)S(1)}, u32[]{:S(2)}, u32[]{:S(2)}) collective-permute-start(bf16[1,16,2048]{2,1,0:T(8,128)(2,1)} %param.8), channel_id=1, source_target_pairs={{0,8},{8,16},{16,24},{24,32},{32,40},{40,48},{48,56},{56,64},{64,7... | collective-permute-start | bytes 196616 | tf_op jit(solution)/shard_map/ppermute | solution.py:19
  20.6 9.0 %collective-permute-start.1 = (bf16[2,16,2048]{2,1,0:T(8,128)(2,1)S(1)}, bf16[2,16,2048]{2,1,0:T(8,128)(2,1)S(1)}, u32[]{:S(2)}, u32[]{:S(2)}) collective-permute-start(bf16[2,16,2048]{2,1,0:T(8,128)(2,1)S(1)} %pad_maximum_fusion.1), channel_id=1, source_target_pairs={{0,16},{8,24},{16,32},{24,40},{32,48},{40,56},{48,64},{56,72},{64,... | collective-permute-start | bytes 393224 | tf_op jit(solution)/shard_map/ppermute | solution.py:19
  30.5 10.7 %collective-permute-start.2 = (bf16[4,16,2048]{2,1,0:T(8,128)(2,1)S(1)}, bf16[4,16,2048]{2,1,0:T(8,128)(2,1)S(1)}, u32[]{:S(2)}, u32[]{:S(2)}) collective-permute-start(bf16[4,16,2048]{2,1,0:T(8,128)(2,1)S(1)} %pad_maximum_fusion), channel_id=1, source_target_pairs={{0,32},{8,40},{16,48},{24,56},{32,64},{40,72},{48,80},{56,88},{64,... | collective-permute-start | bytes 786440 | tf_op jit(solution)/shard_map/ppermute | solution.py:19
  95.1 46.9 %copy-start = (bf16[3,128,2048]{2,1,0:T(8,128)(2,1)S(1)}, bf16[3,128,2048]{2,1,0:T(8,128)(2,1)}, u32[]{:S(2)}) copy-start(bf16[3,128,2048]{2,1,0:T(8,128)(2,1)} %get-tuple-element.8) | copy-start | bytes 4718596
  95.1 46.9 %collective-permute-start.3 = (bf16[3,128,2048]{2,1,0:T(8,128)(2,1)}, bf16[3,128,2048]{2,1,0:T(8,128)(2,1)S(1)}, u32[]{:S(2)}, u32[]{:S(2)}) collective-permute-start(bf16[3,128,2048]{2,1,0:T(8,128)(2,1)} %get-tuple-element.9), channel_id=1, source_target_pairs={{0,1},{1,0},{2,3},{3,2},{4,5},{5,4},{6,7},{7,6},{8,9},{9,8},{10,11... | collective-permute-start | bytes 4718600 | tf_op jit(solution)/shard_map/ppermute | solution.py:142
  135.2 10.1 %collective-permute-start.8 = (bf16[4,16,2048]{2,1,0:T(8,128)(2,1)S(1)}, bf16[4,16,2048]{2,1,0:T(8,128)(2,1)S(1)}, u32[]{:S(2)}, u32[]{:S(2)}) collective-permute-start(bf16[4,16,2048]{2,1,0:T(8,128)(2,1)S(1)} %slice.61), channel_id=1, source_target_pairs={{0,480},{8,488},{16,496},{24,504},{32,0},{40,8},{48,16},{56,24},{6... | collective-permute-start | bytes 786440 | tf_op jit(solution)/shard_map/ppermute | solution.py:19
  142.8 9.8 %collective-permute-start.4 = (bf16[64,2048]{1,0:T(8,128)(2,1)S(1)}, bf16[64,2048]{1,0:T(8,128)(2,1)S(1)}, u32[]{:S(2)}, u32[]{:S(2)}) collective-permute-start(bf16[64,2048]{1,0:T(8,128)(2,1)S(1)} %get-tuple-element.13), channel_id=1, source_target_pairs={{4,2},{5,3},{6,4},{7,5},{12,10},{13,11},{14,12},{15,13},{20,18},{2... | collective-permute-start | bytes 786440 | tf_op jit(solution)/shard_map/ppermute | solution.py:149
  143.5 12.0 %collective-permute-start.6 = (bf16[64,2048]{1,0:T(8,128)(2,1)S(1)}, bf16[64,2048]{1,0:T(8,128)(2,1)S(1)}, u32[]{:S(2)}, u32[]{:S(2)}) collective-permute-start(bf16[64,2048]{1,0:T(8,128)(2,1)S(1)} %get-tuple-element.14), channel_id=1, source_target_pairs={{4,6},{5,7},{6,0},{7,1},{12,14},{13,15},{14,8},{15,9},{20,22},{21,... | collective-permute-start | bytes 786440 | tf_op jit(solution)/shard_map/ppermute | solution.py:150
  145.4 20.5 %collective-permute-start.9 = (bf16[2,16,2048]{2,1,0:T(8,128)(2,1)S(1)}, bf16[2,16,2048]{2,1,0:T(8,128)(2,1)S(1)}, u32[]{:S(2)}, u32[]{:S(2)}) collective-permute-start(bf16[2,16,2048]{2,1,0:T(8,128)(2,1)S(1)} %slice.63), channel_id=1, source_target_pairs={{0,496},{8,504},{16,0},{24,8},{32,16},{40,24},{48,32},{56,40},{64,... | collective-permute-start | bytes 393224 | tf_op jit(solution)/shard_map/ppermute | solution.py:19
  155.6 31.5 %collective-permute-start.5 = (bf16[128,2048]{1,0:T(8,128)(2,1)S(1)}, bf16[128,2048]{1,0:T(8,128)(2,1)S(1)}, u32[]{:S(2)}, u32[]{:S(2)}) collective-permute-start(bf16[128,2048]{1,0:T(8,128)(2,1)S(1)} %get-tuple-element.11), channel_id=1, source_target_pairs={{2,0},{3,1},{4,2},{5,3},{6,4},{7,5},{10,8},{11,9},{12,10},{13,11},... | collective-permute-start | bytes 1572872 | tf_op jit(solution)/shard_map/ppermute | solution.py:154
  156.9 33.4 %collective-permute-start.7 = (bf16[128,2048]{1,0:T(8,128)(2,1)S(1)}, bf16[128,2048]{1,0:T(8,128)(2,1)S(1)}, u32[]{:S(2)}, u32[]{:S(2)}) collective-permute-start(bf16[128,2048]{1,0:T(8,128)(2,1)S(1)} %get-tuple-element.12), channel_id=1, source_target_pairs={{6,0},{7,1},{0,2},{1,3},{14,8},{15,9},{8,10},{9,11},{22,16},{23,17... | collective-permute-start | bytes 1572872 | tf_op jit(solution)/shard_map/ppermute | solution.py:155
  166.0 6.8 %collective-permute-start.10 = (bf16[1,16,2048]{2,1,0:T(8,128)(2,1)S(1)}, bf16[1,16,2048]{2,1,0:T(8,128)(2,1)S(1)}, u32[]{:S(2)}, u32[]{:S(2)}) collective-permute-start(bf16[1,16,2048]{2,1,0:T(8,128)(2,1)S(1)} %slice.65), channel_id=1, source_target_pairs={{0,504},{8,0},{16,8},{24,16},{32,24},{40,32},{48,40},{56,48},{64,5... | collective-permute-start | bytes 196616 | tf_op jit(solution)/shard_map/ppermute | solution.py:19
Sparse Core Ops, SparseCore 0:
  10.1 66.3 all-gather.3
  97.6 36.6 reduce-scatter.1

commit v3 on v2

v3 whole, which is shorter than its diff:
```python
import functools

import jax
import jax.numpy as jnp
from jax import lax
from jax.experimental import pallas as pl
from jax.experimental.pallas import tpu as pltpu
from jax.sharding import PartitionSpec as P

KVH = 8
HD = 128
SPREAD = 8
NEG = -1e30
LOG2E = 1.4426950408889634


def passed_along(value, axis, by):
    peers = lax.axis_size(axis)
    return lax.ppermute(value, axis, [(i, (i + by) % peers) for i in range(peers)])


def stacked(block):
    heads = block.shape[1] // HD
    return jnp.concatenate([block[:, h * HD : (h + 1) * HD] for h in range(heads)], axis=0)


def attention_kernel(span, n_seq, info, q_ref, g_ref, start_ref, *refs):
    key_refs, value_refs = refs[:8], refs[8:16]
    dq_ref, keep_ref, give_ref, pkeep_ref, bias = refs[16:]
    rows = q_ref.shape[0]
    heads = q_ref.shape[1] // HD
    slot = key_refs[0].shape[0]
    plen = slot * n_seq
    odd = lax.rem(info[0], 2) == 1
    half = KVH * HD
    window = (span + 1) * rows
    scale = HD ** -0.5
    me = info[0]
    head = pl.program_id(0)

    @pl.when(head == 0)
    def _():
        own = me * rows
        k_ids = own - span * rows + lax.broadcasted_iota(jnp.int32, (window, rows), 0)
        q_ids = own + lax.broadcasted_iota(jnp.int32, (window, rows), 1)
        seen = (k_ids >= start_ref[...]) & (k_ids <= q_ids)
        bias[...] = jnp.where(seen, 0.0, NEG)

    def laid_out(refs):
        mine, across, last, next_, own, two, got_near, got_far = [ref[...] for ref in refs]
        cut = rows // 2
        far = cut + slot
        four = [last[:cut], next_[:cut]]
        other4 = jnp.concatenate([got_far[:cut], got_far[far : far + cut]], axis=0)
        other3 = got_near[rows:]
        blocks = [mine, last[cut:], across, next_[cut:]]
        blocks += [got_far[2 * far : 2 * far + slot], got_far[cut:far]]
        blocks += [got_far[2 * far + slot :], got_far[far + cut : 2 * far]]
        blocks += [jnp.where(odd, other4, other3), *four, jnp.where(odd, other3, other4)]
        blocks += [two, got_near[:rows], own]
        return jnp.concatenate(blocks, axis=0)

    keys = laid_out(key_refs)
    values = laid_out(value_refs)
    q_rows = stacked(q_ref[...])
    g_rows = stacked(g_ref[...])
    nt = (((1,), (1,)), ((), ()))
    nn = (((1,), (0,)), ((), ()))
    tn = (((0,), (0,)), ((), ()))
    scores = lax.dot_general(keys, q_rows, nt, preferred_element_type=jnp.float32)
    shade = jnp.concatenate([bias[...]] * heads, axis=1)
    scores = jnp.concatenate([scores[:plen], scores[plen:] + shade], axis=0)
    top = jnp.max(scores, axis=0, keepdims=True)
    expo = jnp.exp2((scores - top) * (scale * LOG2E))
    weights = expo * (1.0 / jnp.sum(expo, axis=0, keepdims=True))
    d_weights = lax.dot_general(values, g_rows, nt, preferred_element_type=jnp.float32)
    delta = jnp.sum(weights * d_weights, axis=0, keepdims=True)
    d_scores = (weights * (d_weights - delta)).astype(jnp.bfloat16)
    weights_b = weights.astype(jnp.bfloat16)
    d_value = lax.dot_general(weights_b, g_rows, nn, preferred_element_type=jnp.float32)
    d_key = lax.dot_general(d_scores, q_rows, nn, preferred_element_type=jnp.float32) * scale
    d_query = lax.dot_general(d_scores, keys, tn, preferred_element_type=jnp.float32) * scale
    d_query = d_query.astype(jnp.bfloat16)
    for h in range(heads):
        dq_ref[:, h * HD : (h + 1) * HD] = d_query[h * rows : (h + 1) * rows]
    given = (span + 1) // 2 * rows
    for part, base in ((d_key, 0), (d_value, half)):
        part = part.astype(jnp.bfloat16)
        columns = pl.ds(pl.multiple_of(base + head * HD, HD), HD)
        for back in range(span + 1):
            block = part[plen + (span - back) * rows : plen + (span - back + 1) * rows]
            if back % 2 == 0:
                keep_ref[back // 2, :, columns] = block
            else:
                give_ref[back // 2 * rows : (back // 2 + 1) * rows, columns] = block
        pkeep_ref[:, columns] = part[: plen // 2]
        give_ref[given:, columns] = part[plen // 2 : plen]


def attend(q_rows, grad_rows, kv, q_start, me, span, n_seq):
    rows, columns = q_rows.shape
    plen, width = n_seq * kv[0].shape[0], kv[0].shape[1]
    group = columns // KVH
    bf16 = jnp.bfloat16
    at = lambda n, col: pl.BlockSpec((n, col), lambda g, s: (0, g))
    later = lambda n: pl.BlockSpec((n, HD), lambda g, s: (0, KVH + g))
    pairs = (span + 1) * rows + plen
    kept, given = span // 2 + 1, (span + 1) // 2
    return pl.pallas_call(
        functools.partial(attention_kernel, span, n_seq),
        grid_spec=pltpu.PrefetchScalarGridSpec(
            num_scalar_prefetch=1,
            grid=(KVH,),
            in_specs=[
                at(rows, group),
                at(rows, group),
                pl.BlockSpec((1, rows), lambda g, s: (0, 0)),
            ]
            + [at(x.shape[0], HD) for x in kv]
            + [later(x.shape[0]) for x in kv],
            out_specs=[
                at(rows, group),
                pl.BlockSpec((kept, rows, width), lambda g, s: (0, 0, 0)),
                pl.BlockSpec((given * rows + plen // 2, width), lambda g, s: (0, 0)),
                pl.BlockSpec((plen // 2, width), lambda g, s: (0, 0)),
            ],
            scratch_shapes=[pltpu.VMEM(((span + 1) * rows, rows), jnp.float32)],
        ),
        out_shape=[
            jax.ShapeDtypeStruct((rows, columns), bf16),
            jax.ShapeDtypeStruct((kept, rows, width), bf16),
            jax.ShapeDtypeStruct((given * rows + plen // 2, width), bf16),
            jax.ShapeDtypeStruct((plen // 2, width), bf16),
        ],
        compiler_params=pltpu.CompilerParams(vmem_limit_bytes=56 * 1024 * 1024),
        cost_estimate=pl.CostEstimate(
            flops=10 * rows * columns * pairs,
            bytes_accessed=12 * 1024 * 1024,
            transcendentals=rows * columns * pairs // HD,
        ),
    )(me.astype(jnp.int32)[None], q_rows, grad_rows, q_start[None], *kv, *kv)


def added(*parts):
    total = parts[0].astype(jnp.float32)
    for part in parts[1:]:
        total = total + part.astype(jnp.float32)
    return total.astype(jnp.bfloat16)


def along_seq(value, pairs):
    return lax.ppermute(value, "seq", pairs)


def rounds_in(own, prompt, offset, odd):
    n = lax.axis_size("seq")
    cut = own.shape[0] // 2
    behind = [(i, (i - 2) % n) for i in range(n)]
    ahead = [(i, (i + 2) % n) for i in range(n)]
    across = [(i, (i + 4) % n) for i in range(n)]
    swap = [(i, i ^ 1) for i in range(n)]
    tied = lax.optimization_barrier

    by1 = passed_along(prompt, "dp", 1)
    pair = jnp.concatenate([prompt, by1])
    pair, own = tied((pair, own))
    two = along_seq(own, [(i, i + 2) for i in range(n - 2)])
    six = along_seq(own, [(i, (i - 2) % n) for i in range(4)])
    pairs = [passed_along(pair, "dp", step) for step in range(2, SPREAD, 2)]
    *pairs, two, six = tied((*pairs, two, six))
    top2, low6 = two[:cut], six[cut:]

    window = jnp.concatenate([pair, *pairs])
    chosen = lax.dynamic_index_in_dim(window, offset, 0, keepdims=False)
    from_last = along_seq(jnp.concatenate([top2, chosen]), ahead)
    from_next = along_seq(jnp.concatenate([low6, chosen]), behind)
    from_across = along_seq(chosen, across)
    near = jnp.concatenate([jnp.where(odd, two, own), jnp.where(odd, six, two)])
    got_near = along_seq(near, swap)
    from_last, from_next, from_across, chosen, got_near = tied(
        (from_last, from_next, from_across, chosen, got_near)
    )
    got_far = along_seq(jnp.concatenate([from_last, from_next, chosen, from_across]), swap)
    return [chosen, from_across, from_last, from_next, own, two, got_near, got_far]


def rounds_out(keep, give, pkeep, offset):
    n = lax.axis_size("seq")
    rows = keep.shape[1]
    cut = rows // 2
    slot = pkeep.shape[0] // (n // 2)
    behind = [(i, (i - 2) % n) for i in range(n)]
    ahead = [(i, (i + 2) % n) for i in range(n)]
    across = [(i, (i + 4) % n) for i in range(n)]
    swap = [(i, i ^ 1) for i in range(n)]
    tied = lax.optimization_barrier
    me = lax.axis_index("seq")
    odd = jnp.mod(me, 2) == 1

    got = along_seq(give, swap)
    got, pgot = got[: -pkeep.shape[0]].reshape((-1,) + keep.shape[1:]), got[-pkeep.shape[0] :]
    none = jnp.zeros_like(got[:1])
    sums = added(
        jnp.concatenate([keep, none]),
        jnp.where(odd, jnp.concatenate([none, got]), jnp.concatenate([got, none])),
    )
    own, one, two, three = sums[0], sums[1], sums[2], sums[3]
    prompt = added(pkeep, pgot)
    mine, to_behind, to_across, to_ahead = [prompt[i * slot : (i + 1) * slot] for i in range(4)]

    from_next = along_seq(jnp.concatenate([two[:cut], to_behind]), behind)
    from_last = along_seq(jnp.concatenate([two[cut:], to_ahead]), ahead)
    from_across = along_seq(to_across, across)
    from_next, from_last, from_across, one, three = tied(
        (from_next, from_last, from_across, one, three)
    )

    prompt = added(mine, from_next[cut:], from_last[cut:], from_across)
    none = jnp.zeros((), prompt.dtype)
    left = [jnp.where(offset == i, prompt, none) for i in range(SPREAD)]
    zero = jnp.zeros_like(prompt, shape=(cut,) + prompt.shape[1:])
    passing = (me >= n - 2) | (me < 2)
    one = added(one, jnp.concatenate([from_next[:cut], zero]))
    three = added(
        three, jnp.concatenate([zero, jnp.where(passing, from_last[:cut], none)])
    )
    from_next = along_seq(one, [(i, i - 2) for i in range(2, n)])
    from_last = along_seq(three, [(i, (i + 2) % n) for i in (n - 2, n - 1, 0, 1)])
    pairs = [
        passed_along(jnp.stack(left[step : step + 2]), "dp", -step)
        for step in range(2, SPREAD, 2)
    ]
    *pairs, from_next, from_last = tied((*pairs, from_next, from_last))
    by1 = passed_along(added(left[1], *[pair[1] for pair in pairs]), "dp", -1)
    d_kv = added(own, from_next, from_last)
    return d_kv, added(left[0], by1, *[pair[0] for pair in pairs])


def on_device(queries, resp_kv, prompt_kv, d_out, resp_lengths, prompt_home):
    q_rows = queries[0]
    own_kv = resp_kv[0]
    grad_rows = d_out[0]
    rows = q_rows.shape[0]
    n_seq = lax.axis_size("seq")
    n_dp = lax.axis_size("dp")
    span = 5 * n_seq // 8
    me_seq = lax.axis_index("seq")
    me_dp = lax.axis_index("dp")
    odd = jnp.mod(me_seq, 2) == 1
    offset = jnp.mod(me_dp - prompt_home[0], n_dp)

    kv = rounds_in(own_kv, prompt_kv, offset, odd)

    lengths = resp_lengths[0]
    starts = jnp.cumsum(lengths) - lengths
    q_ids = me_seq * rows + jnp.arange(rows, dtype=jnp.int32)
    q_start = jnp.max(jnp.where(starts[None, :] <= q_ids[:, None], starts[None, :], 0), axis=1)
    d_query, keep, give, pkeep = attend(
        q_rows, grad_rows, kv, q_start, me_seq, span, n_seq
    )
    d_kv, d_prompt = rounds_out(keep, give, pkeep, offset)
    return (d_query[None], d_kv[None], d_prompt[None])


def solution(mesh):
    placed = (
        P("dp", "seq", None),
        P("dp", "seq", None),
        P("dp", "seq", None),
        P("dp", "seq", None),
        P("dp", None),
        P("dp"),
    )
    return jax.shard_map(
        on_device,
        mesh=mesh,
        in_specs=placed,
        out_specs=(P("dp", "seq", None), P("dp", "seq", None), P("dp", "seq", None)),
        check_vma=False,
    )
```

time: 199 us -> 178 us (0.89)
  starting transfers between devices: 42.7 us -> 88.8 us
  waiting for transfers between devices: 85.3 us -> 55.2 us
  blocking collectives: 29.1 us -> 0 us
  between operations: 14.9 us -> 1.74 us
  other arithmetic: 7.49 us -> 10.7 us
    reduce_scatter x1 -> x0, waiting for transfers between devices: 36.7 us -> none  [on_device(): lax.psum_scatter(d_prompt, 'seq', scatter_dimension=0, tiled=True)]
    ppermute x5 -> x13, starting transfers between devices: 14.6 us -> 49 us  [along_seq(): return lax.ppermute(value, 'seq', pairs)]
    all_gather x1 -> x0, blocking collectives: 29.1 us -> none  [on_device(): prompt = lax.all_gather(chosen, 'seq', axis=0, tiled=True)]
    ppermute x5 -> x13, waiting for transfers between devices: 19.7 us -> 37.3 us  [along_seq(): return lax.ppermute(value, 'seq', pairs)]
    ppermute x6 -> x8, starting transfers between devices: 28.1 us -> 39.8 us  [passed_along(): lax.ppermute(value, axis, [(i, (i + by) % peers) for i in range(peers)])]
    all_gather x1 -> x0, waiting for transfers between devices: 6.17 us -> none  [on_device(): kv = lax.all_gather(own_kv, 'seq', axis=0, tiled=True)]
    ppermute x6 -> x8, waiting for transfers between devices: 22 us -> 17.9 us  [passed_along(): lax.ppermute(value, axis, [(i, (i + by) % peers) for i in range(peers)])]
    broadcast_in_dim x1 -> x2, other arithmetic: 1.03 us -> 3.76 us  [on_device(): return (d_query[None], d_kv[None], d_prompt[None])]
  transfers between devices with their start and end apart: 13 -> 21, of which waited for: 10 -> 13; matrix products, arithmetic and copies ran while one was open for 3% -> 3% of each run, Pallas kernels for 0% -> 0%
where the time goes in v3:
time: 178 us; the launch traced here: 177 us
  starting transfers between devices  88.8 us (50%)
  waiting for transfers between devices  55.2 us (31%)
  Pallas kernels  18.9 us (11%)
  other arithmetic  10.7 us (6%)
    ppermute x13, starting transfers between devices, along_seq(): return lax.ppermute(value, 'seq', pairs)  49 us
    ppermute x8, starting transfers between devices, passed_along(): lax.ppermute(value, axis, [(i, (i + by) % peers) for i in range(peers)])  39.8 us
    ppermute x13, waiting for transfers between devices, along_seq(): return lax.ppermute(value, 'seq', pairs)  37.3 us
    pallas_call x1, Pallas kernels, attend(): pl.pallas_call(functools.partial(attention_kernel, span, n_seq), grid_spe...  18.9 us
    ppermute x8, waiting for transfers between devices, passed_along(): lax.ppermute(value, axis, [(i, (i + by) % peers) for i in range(peers)])  17.9 us
    broadcast_in_dim x2, other arithmetic, on_device(): return (d_query[None], d_kv[None], d_prompt[None])  3.76 us
  transfers between devices with their start and end apart: 21, of which 13 were waited for; matrix products, arithmetic and copies ran while one was open for 3% of the time, Pallas kernels for 0%

profile of v3, /device:TPU:1, one launch (start us, length us, event | category | flops | bytes accessed | tf_op | source)
XLA Modules:
  0.0 176.9 jit_solution(465816152394039413)
XLA Ops:
  0.6 4.8 %collective-permute-start = (bf16[1,16,2048]{2,1,0:T(8,128)(2,1)}, bf16[1,16,2048]{2,1,0:T(8,128)(2,1)S(1)}, u32[]{:S(2)}, u32[]{:S(2)}) collective-permute-start(bf16[1,16,2048]{2,1,0:T(8,128)(2,1)} %param.8), channel_id=1, source_target_pairs={{0,8},{8,16},{16,24},{24,32},{32,40},{40,48},{48,56},{56,64},{64,7... | collective-permute-start | bytes 196616 | tf_op jit(solution)/shard_map/ppermute | solution.py:19
  5.5 7.0 %collective-permute-done = bf16[1,16,2048]{2,1,0:T(8,128)(2,1)S(1)} collective-permute-done((bf16[1,16,2048]{2,1,0:T(8,128)(2,1)}, bf16[1,16,2048]{2,1,0:T(8,128)(2,1)S(1)}, u32[]{:S(2)}, u32[]{:S(2)}) %collective-permute-start) | collective-permute-done | bytes 65568 | tf_op jit(solution)/shard_map/ppermute | solution.py:19
  12.4 0.9 pad_maximum_fusion.6
  13.3 5.8 %collective-permute-start.4 = (bf16[128,2048]{1,0:T(8,128)(2,1)}, bf16[128,2048]{1,0:T(8,128)(2,1)S(1)}, u32[]{:S(2)}, u32[]{:S(2)}) collective-permute-start(bf16[128,2048]{1,0:T(8,128)(2,1)} %bitcast.61), channel_id=1, source_target_pairs={{0,2},{1,3},{2,4},{3,5},{4,6},{5,7},{8,10},{9,11},{10,12},{11,13},... | collective-permute-start | bytes 1572872 | tf_op jit(solution)/shard_map/ppermute | solution.py:152
  19.1 5.2 %collective-permute-start.5 = (bf16[128,2048]{1,0:T(8,128)(2,1)}, bf16[128,2048]{1,0:T(8,128)(2,1)S(1)}, u32[]{:S(2)}, u32[]{:S(2)}) collective-permute-start(bf16[128,2048]{1,0:T(8,128)(2,1)} %bitcast.62), channel_id=1, source_target_pairs={{0,6},{1,7},{2,0},{3,1},{8,14},{9,15},{10,8},{11,9},{16,22},{17,23... | collective-permute-start | bytes 1572872 | tf_op jit(solution)/shard_map/ppermute | solution.py:152
  24.3 1.9 %collective-permute-start.1 = (bf16[2,16,2048]{2,1,0:T(8,128)(2,1)S(1)}, bf16[2,16,2048]{2,1,0:T(8,128)(2,1)S(1)}, u32[]{:S(2)}, u32[]{:S(2)}) collective-permute-start(bf16[2,16,2048]{2,1,0:T(8,128)(2,1)S(1)} %pad_maximum_fusion.6), channel_id=1, source_target_pairs={{0,16},{8,24},{16,32},{24,40},{32,48},{40,56},{48,64},{56,72},{64,... | collective-permute-start | bytes 393224 | tf_op jit(solution)/shard_map/ppermute | solution.py:19
  26.3 1.9 %collective-permute-start.2 = (bf16[2,16,2048]{2,1,0:T(8,128)(2,1)S(1)}, bf16[2,16,2048]{2,1,0:T(8,128)(2,1)S(1)}, u32[]{:S(2)}, u32[]{:S(2)}) collective-permute-start(bf16[2,16,2048]{2,1,0:T(8,128)(2,1)S(1)} %pad_maximum_fusion.6), channel_id=1, source_target_pairs={{0,32},{8,40},{16,48},{24,56},{32,64},{40,72},{48,80},{56,88},{64,... | collective-permute-start | bytes 393224 | tf_op jit(solution)/shard_map/ppermute | solution.py:19
  28.2 3.8 %collective-permute-start.3 = (bf16[2,16,2048]{2,1,0:T(8,128)(2,1)S(1)}, bf16[2,16,2048]{2,1,0:T(8,128)(2,1)S(1)}, u32[]{:S(2)}, u32[]{:S(2)}) collective-permute-start(bf16[2,16,2048]{2,1,0:T(8,128)(2,1)S(1)} %pad_maximum_fusion.6), channel_id=1, source_target_pairs={{0,48},{8,56},{16,64},{24,72},{32,80},{40,88},{48,96},{56,104},{64... | collective-permute-start | bytes 393224 | tf_op jit(solution)/shard_map/ppermute | solution.py:19
  32.0 1.4 collective-permute-done.1
  33.4 3.0 %collective-permute-done.2 = bf16[2,16,2048]{2,1,0:T(8,128)(2,1)S(1)} collective-permute-done((bf16[2,16,2048]{2,1,0:T(8,128)(2,1)S(1)}, bf16[2,16,2048]{2,1,0:T(8,128)(2,1)S(1)}, u32[]{:S(2)}, u32[]{:S(2)}) %collective-permute-start.2) | collective-permute-done | bytes 131104 | tf_op jit(solution)/shard_map/ppermute | solution.py:19
  36.4 1.7 collective-permute-done.3
  38.1 0.0 collective-permute-done.4.refs_5_.refs_13_
  38.1 6.4 %collective-permute-done.5 = bf16[128,2048]{1,0:T(8,128)(2,1)S(1)} collective-permute-done((bf16[128,2048]{1,0:T(8,128)(2,1)}, bf16[128,2048]{1,0:T(8,128)(2,1)S(1)}, u32[]{:S(2)}, u32[]{:S(2)}) %collective-permute-start.5) | collective-permute-done | bytes 524320 | tf_op jit(solution)/shard_map/ppermute | solution.py:152
  44.5 0.1 broadcast_select_fusion.1
  44.6 0.1 pad_maximum_fusion
  44.7 3.5 %collective-permute-start.9 = (bf16[256,2048]{1,0:T(8,128)(2,1)S(1)}, bf16[256,2048]{1,0:T(8,128)(2,1)}, u32[]{:S(2)}, u32[]{:S(2)}) collective-permute-start(bf16[256,2048]{1,0:T(8,128)(2,1)S(1)} %pad_maximum_fusion), channel_id=1, source_target_pairs={{0,1},{1,0},{2,3},{3,2},{4,5},{5,4},{6,7},{7,6},{8,9},{9,8},{10,11... | collective-permute-start | bytes 3145736 | tf_op jit(solution)/shard_map/ppermute | solution.py:152
  48.8 0.0 copy-start.7
  48.9 0.1 fusion.9.refs_0_.refs_8_
  48.9 0.0 copy-start.2
  49.0 0.1 pad_maximum_fusion.2
  49.0 1.9 %collective-permute-start.6 = (bf16[80,2048]{1,0:T(8,128)(2,1)S(1)}, bf16[80,2048]{1,0:T(8,128)(2,1)S(1)}, u32[]{:S(2)}, u32[]{:S(2)}) collective-permute-start(bf16[80,2048]{1,0:T(8,128)(2,1)S(1)} %get-tuple-element.72), channel_id=1, source_target_pairs={{0,2},{1,3},{2,4},{3,5},{4,6},{5,7},{6,0},{7,1},{8,10},{9,11},{10,... | collective-permute-start | bytes 983048 | tf_op jit(solution)/shard_map/ppermute | solution.py:152
  51.0 5.5 %collective-permute-start.7 = (bf16[80,2048]{1,0:T(8,128)(2,1)S(1)}, bf16[80,2048]{1,0:T(8,128)(2,1)S(1)}, u32[]{:S(2)}, u32[]{:S(2)}) collective-permute-start(bf16[80,2048]{1,0:T(8,128)(2,1)S(1)} %get-tuple-element.71), channel_id=1, source_target_pairs={{0,6},{1,7},{2,0},{3,1},{4,2},{5,3},{6,4},{7,5},{8,14},{9,15},{10,... | collective-permute-start | bytes 983048 | tf_op jit(solution)/shard_map/ppermute | solution.py:152
  56.4 3.7 %collective-permute-start.8 = (bf16[16,2048]{1,0:T(8,128)(2,1)S(1)}, bf16[16,2048]{1,0:T(8,128)(2,1)S(1)}, u32[]{:S(2)}, u32[]{:S(2)}) collective-permute-start(bf16[16,2048]{1,0:T(8,128)(2,1)S(1)} %fusion.9.refs_0_.refs_8_), channel_id=1, source_target_pairs={{0,4},{1,5},{2,6},{3,7},{4,0},{5,1},{6,2},{7,3},{8,12},{9,13},{10,... | collective-permute-start | bytes 196616 | tf_op jit(solution)/shard_map/ppermute | solution.py:152
  60.2 10.4 %collective-permute-done.8.refs_1_.refs_9_ = bf16[16,2048]{1,0:T(8,128)(2,1)S(1)} collective-permute-done((bf16[16,2048]{1,0:T(8,128)(2,1)S(1)}, bf16[16,2048]{1,0:T(8,128)(2,1)S(1)}, u32[]{:S(2)}, u32[]{:S(2)}) %collective-permute-start.8) | collective-permute-done | bytes 65568 | tf_op jit(solution)/shard_map/ppermute | solution.py:152
  70.5 0.0 collective-permute-done.6.refs_2_.refs_10_
  70.5 0.3 collective-permute-done.7.refs_3_.refs_11_
  70.8 0.1 pad_maximum_fusion.1
  70.9 2.3 %collective-permute-start.10 = (bf16[192,2048]{1,0:T(8,128)(2,1)S(1)}, bf16[192,2048]{1,0:T(8,128)(2,1)S(1)}, u32[]{:S(2)}, u32[]{:S(2)}) collective-permute-start(bf16[192,2048]{1,0:T(8,128)(2,1)S(1)} %pad_maximum_fusion.1), channel_id=1, source_target_pairs={{0,1},{1,0},{2,3},{3,2},{4,5},{5,4},{6,7},{7,6},{8,9},{9,8},{10,11... | collective-permute-start | bytes 2359304 | tf_op jit(solution)/shard_map/ppermute | solution.py:152
  73.2 0.2 reduce-window_clone.1
  73.4 0.7 select_reduce_fusion
  74.1 1.0 collective-permute-done.10.refs_7_.refs_15_
  75.1 0.9 copy-done.6
  76.0 18.9 %shard_map.85 = (bf16[128,4096]{1,0:T(8,128)(2,1)}, bf16[3,128,2048]{2,1,0:T(8,128)(2,1)}, bf16[448,2048]{1,0:T(8,128)(2,1)}, bf16[64,2048]{1,0:T(8,128)(2,1)}) custom-call(s32[1]{0:T(128)} %bitcast.info, bf16[128,4096]{1,0:T(8,128)(2,1)} %bitcast.66, bf16[128,4096]{1,0:T(8,128)(2,1)} %bitcast.67, s32[1,128]{1,0:T(1,128)} %bitcast.69, ...), custom_call_target="tpu_custom_call" | custom-call | flops 4697620480 | bytes 12582912 | tf_op jit(solution)/shard_map/pallas_call | solution.py:109
  95.0 2.3 %collective-permute-start.11 = (bf16[448,2048]{1,0:T(8,128)(2,1)}, bf16[448,2048]{1,0:T(8,128)(2,1)S(1)}, u32[]{:S(2)}, u32[]{:S(2)}) collective-permute-start(bf16[448,2048]{1,0:T(8,128)(2,1)} %get-tuple-element.43), channel_id=1, source_target_pairs={{0,1},{1,0},{2,3},{3,2},{4,5},{5,4},{6,7},{7,6},{8,9},{9,8},{10,11... | collective-permute-start | bytes 5505032 | tf_op jit(solution)/shard_map/ppermute | solution.py:152
  97.3 3.6 %collective-permute-done.11 = bf16[448,2048]{1,0:T(8,128)(2,1)S(1)} collective-permute-done((bf16[448,2048]{1,0:T(8,128)(2,1)}, bf16[448,2048]{1,0:T(8,128)(2,1)S(1)}, u32[]{:S(2)}, u32[]{:S(2)}) %collective-permute-start.11) | collective-permute-done | bytes 1835040 | tf_op jit(solution)/shard_map/ppermute | solution.py:152
  100.9 1.1 add_convert_fusion.3
  102.0 0.1 slice.103
  102.1 0.2 copy-done
  102.3 0.6 add_convert_fusion
  103.1 4.7 %collective-permute-start.12 = (bf16[80,2048]{1,0:T(8,128)(2,1)S(1)}, bf16[80,2048]{1,0:T(8,128)(2,1)S(1)}, u32[]{:S(2)}, u32[]{:S(2)}) collective-permute-start(bf16[80,2048]{1,0:T(8,128)(2,1)S(1)} %pad_maximum_fusion.4), channel_id=1, source_target_pairs={{0,6},{1,7},{2,0},{3,1},{4,2},{5,3},{6,4},{7,5},{8,14},{9,15},{10,... | collective-permute-start | bytes 983048 | tf_op jit(solution)/shard_map/ppermute | solution.py:152
  107.8 2.6 %collective-permute-start.13 = (bf16[80,2048]{1,0:T(8,128)(2,1)S(1)}, bf16[80,2048]{1,0:T(8,128)(2,1)S(1)}, u32[]{:S(2)}, u32[]{:S(2)}) collective-permute-start(bf16[80,2048]{1,0:T(8,128)(2,1)S(1)} %pad_maximum_fusion.5), channel_id=1, source_target_pairs={{0,2},{1,3},{2,4},{3,5},{4,6},{5,7},{6,0},{7,1},{8,10},{9,11},{10,... | collective-permute-start | bytes 983048 | tf_op jit(solution)/shard_map/ppermute | solution.py:152
  110.5 5.2 %collective-permute-start.14 = (bf16[16,2048]{1,0:T(8,128)(2,1)S(1)}, bf16[16,2048]{1,0:T(8,128)(2,1)S(1)}, u32[]{:S(2)}, u32[]{:S(2)}) collective-permute-start(bf16[16,2048]{1,0:T(8,128)(2,1)S(1)} %get-tuple-element.63), channel_id=1, source_target_pairs={{0,4},{1,5},{2,6},{3,7},{4,0},{5,1},{6,2},{7,3},{8,12},{9,13},{10,... | collective-permute-start | bytes 196616 | tf_op jit(solution)/shard_map/ppermute | solution.py:152
  115.7 0.1 slice_bitcast_fusion
  115.8 10.6 %collective-permute-done.14 = bf16[16,2048]{1,0:T(8,128)(2,1)S(1)} collective-permute-done((bf16[16,2048]{1,0:T(8,128)(2,1)S(1)}, bf16[16,2048]{1,0:T(8,128)(2,1)S(1)}, u32[]{:S(2)}, u32[]{:S(2)}) %collective-permute-start.14) | collective-permute-done | bytes 65568 | tf_op jit(solution)/shard_map/ppermute | solution.py:152
  126.5 0.7 pad_maximum_fusion.7
  127.2 9.8 %collective-permute-start.15 = (bf16[2,16,2048]{2,1,0:T(8,128)(2,1)}, bf16[2,16,2048]{2,1,0:T(8,128)(2,1)S(1)}, u32[]{:S(2)}, u32[]{:S(2)}) collective-permute-start(bf16[2,16,2048]{2,1,0:T(8,128)(2,1)} %pad_maximum_fusion.7), channel_id=1, source_target_pairs={{0,496},{8,504},{16,0},{24,8},{32,16},{40,24},{48,32},{56,40},{64,... | collective-permute-start | bytes 393224 | tf_op jit(solution)/shard_map/ppermute | solution.py:19
  137.0 0.1 add_convert_fusion.2
  137.1 1.3 collective-permute-start.18
  138.4 0.1 add_convert_fusion.1
  138.5 4.9 %collective-permute-start.19 = (bf16[128,2048]{1,0:T(8,128)(2,1)S(1)}, bf16[128,2048]{1,0:T(8,128)(2,1)}, u32[]{:S(2)}, u32[]{:S(2)}) collective-permute-start(bf16[128,2048]{1,0:T(8,128)(2,1)S(1)} %add_convert_fusion.1), channel_id=1, source_target_pairs={{6,0},{7,1},{0,2},{1,3},{14,8},{15,9},{8,10},{9,11},{22,16},{23,17... | collective-permute-start | bytes 1572872 | tf_op jit(solution)/shard_map/ppermute | solution.py:152
  143.4 0.7 pad_maximum_fusion.8
  144.0 2.4 %collective-permute-start.16 = (bf16[2,16,2048]{2,1,0:T(8,128)(2,1)}, bf16[2,16,2048]{2,1,0:T(8,128)(2,1)S(1)}, u32[]{:S(2)}, u32[]{:S(2)}) collective-permute-start(bf16[2,16,2048]{2,1,0:T(8,128)(2,1)} %pad_maximum_fusion.8), channel_id=1, source_target_pairs={{0,480},{8,488},{16,496},{24,504},{32,0},{40,8},{48,16},{56,24},{6... | collective-permute-start | bytes 393224 | tf_op jit(solution)/shard_map/ppermute | solution.py:19
  146.4 0.7 pad_maximum_fusion.9
  147.1 3.3 %collective-permute-start.17 = (bf16[2,16,2048]{2,1,0:T(8,128)(2,1)}, bf16[2,16,2048]{2,1,0:T(8,128)(2,1)}, u32[]{:S(2)}, u32[]{:S(2)}) collective-permute-start(bf16[2,16,2048]{2,1,0:T(8,128)(2,1)} %pad_maximum_fusion.9), channel_id=1, source_target_pairs={{0,464},{8,472},{16,480},{24,488},{32,496},{40,504},{48,0},{56,8},... | collective-permute-start | bytes 393224 | tf_op jit(solution)/shard_map/ppermute | solution.py:19
  150.4 0.0 collective-permute-done.15
  150.4 2.8 %collective-permute-done.16 = bf16[2,16,2048]{2,1,0:T(8,128)(2,1)S(1)} collective-permute-done((bf16[2,16,2048]{2,1,0:T(8,128)(2,1)}, bf16[2,16,2048]{2,1,0:T(8,128)(2,1)S(1)}, u32[]{:S(2)}, u32[]{:S(2)}) %collective-permute-start.16) | collective-permute-done | bytes 131104 | tf_op jit(solution)/shard_map/ppermute | solution.py:19
  153.3 2.1 %collective-permute-done.17 = bf16[2,16,2048]{2,1,0:T(8,128)(2,1)} collective-permute-done((bf16[2,16,2048]{2,1,0:T(8,128)(2,1)}, bf16[2,16,2048]{2,1,0:T(8,128)(2,1)}, u32[]{:S(2)}, u32[]{:S(2)}) %collective-permute-start.17) | collective-permute-done | bytes 131104 | tf_op jit(solution)/shard_map/ppermute | solution.py:19
  155.3 5.0 %collective-permute-done.18 = bf16[128,2048]{1,0:T(8,128)(2,1)} collective-permute-done((bf16[128,2048]{1,0:T(8,128)(2,1)S(1)}, bf16[128,2048]{1,0:T(8,128)(2,1)}, u32[]{:S(2)}, u32[]{:S(2)}) %collective-permute-start.18) | collective-permute-done | bytes 524320 | tf_op jit(solution)/shard_map/ppermute | solution.py:152
  160.3 0.0 collective-permute-done.19
  160.3 0.9 fusion.4
  161.2 11.9 %collective-permute-start.20 = (bf16[16,2048]{1,0:T(8,128)(2,1)S(1)}, bf16[16,2048]{1,0:T(8,128)(2,1)S(1)}, u32[]{:S(2)}, u32[]{:S(2)}) collective-permute-start(bf16[16,2048]{1,0:T(8,128)(2,1)S(1)} %fusion.4), channel_id=1, source_target_pairs={{0,504},{8,0},{16,8},{24,16},{32,24},{40,32},{48,40},{56,48},{64,5... | collective-permute-start | bytes 196616 | tf_op jit(solution)/shard_map/ppermute | solution.py:19
  173.1 2.2 %fusion.2 = bf16[1,128,2048]{2,1,0:T(8,128)(2,1)} fusion(bf16[128,2048]{1,0:T(8,128)(2,1)} %collective-permute-done.19, bf16[128,2048]{1,0:T(8,128)(2,1)} %collective-permute-done.18, bf16[4,128,2048]{2,1,0:T(8,128)(2,1)S(1)} %add_convert_fusion), kind=kLoop, calls=%fused_computation.8 | loop fusion | flops 1572864 | bytes 2097152 | tf_op jit(solution)/shard_map/broadcast_in_dim | solution.py:262
  175.4 0.0 collective-permute-done.20
  175.4 1.5 fusion.8
  (27 shorter events, 0.3 us)
Async XLA Ops:
  0.6 11.8 %collective-permute-start = (bf16[1,16,2048]{2,1,0:T(8,128)(2,1)}, bf16[1,16,2048]{2,1,0:T(8,128)(2,1)S(1)}, u32[]{:S(2)}, u32[]{:S(2)}) collective-permute-start(bf16[1,16,2048]{2,1,0:T(8,128)(2,1)} %param.8), channel_id=1, source_target_pairs={{0,8},{8,16},{16,24},{24,32},{32,40},{40,48},{48,56},{56,64},{64,7... | collective-permute-start | bytes 196616 | tf_op jit(solution)/shard_map/ppermute | solution.py:19
  13.3 24.8 %collective-permute-start.4 = (bf16[128,2048]{1,0:T(8,128)(2,1)}, bf16[128,2048]{1,0:T(8,128)(2,1)S(1)}, u32[]{:S(2)}, u32[]{:S(2)}) collective-permute-start(bf16[128,2048]{1,0:T(8,128)(2,1)} %bitcast.61), channel_id=1, source_target_pairs={{0,2},{1,3},{2,4},{3,5},{4,6},{5,7},{8,10},{9,11},{10,12},{11,13},... | collective-permute-start | bytes 1572872 | tf_op jit(solution)/shard_map/ppermute | solution.py:152
  19.1 25.4 %collective-permute-start.5 = (bf16[128,2048]{1,0:T(8,128)(2,1)}, bf16[128,2048]{1,0:T(8,128)(2,1)S(1)}, u32[]{:S(2)}, u32[]{:S(2)}) collective-permute-start(bf16[128,2048]{1,0:T(8,128)(2,1)} %bitcast.62), channel_id=1, source_target_pairs={{0,6},{1,7},{2,0},{3,1},{8,14},{9,15},{10,8},{11,9},{16,22},{17,23... | collective-permute-start | bytes 1572872 | tf_op jit(solution)/shard_map/ppermute | solution.py:152
  24.3 9.0 %collective-permute-start.1 = (bf16[2,16,2048]{2,1,0:T(8,128)(2,1)S(1)}, bf16[2,16,2048]{2,1,0:T(8,128)(2,1)S(1)}, u32[]{:S(2)}, u32[]{:S(2)}) collective-permute-start(bf16[2,16,2048]{2,1,0:T(8,128)(2,1)S(1)} %pad_maximum_fusion.6), channel_id=1, source_target_pairs={{0,16},{8,24},{16,32},{24,40},{32,48},{40,56},{48,64},{56,72},{64,... | collective-permute-start | bytes 393224 | tf_op jit(solution)/shard_map/ppermute | solution.py:19
  26.3 10.1 %collective-permute-start.2 = (bf16[2,16,2048]{2,1,0:T(8,128)(2,1)S(1)}, bf16[2,16,2048]{2,1,0:T(8,128)(2,1)S(1)}, u32[]{:S(2)}, u32[]{:S(2)}) collective-permute-start(bf16[2,16,2048]{2,1,0:T(8,128)(2,1)S(1)} %pad_maximum_fusion.6), channel_id=1, source_target_pairs={{0,32},{8,40},{16,48},{24,56},{32,64},{40,72},{48,80},{56,88},{64,... | collective-permute-start | bytes 393224 | tf_op jit(solution)/shard_map/ppermute | solution.py:19
  28.2 9.9 %collective-permute-start.3 = (bf16[2,16,2048]{2,1,0:T(8,128)(2,1)S(1)}, bf16[2,16,2048]{2,1,0:T(8,128)(2,1)S(1)}, u32[]{:S(2)}, u32[]{:S(2)}) collective-permute-start(bf16[2,16,2048]{2,1,0:T(8,128)(2,1)S(1)} %pad_maximum_fusion.6), channel_id=1, source_target_pairs={{0,48},{8,56},{16,64},{24,72},{32,80},{40,88},{48,96},{56,104},{64... | collective-permute-start | bytes 393224 | tf_op jit(solution)/shard_map/ppermute | solution.py:19
  38.1 10.7 %copy-start.1 = (bf16[128,2048]{1,0:T(8,128)(2,1)}, bf16[128,2048]{1,0:T(8,128)(2,1)S(1)}, u32[]{:S(2)}) copy-start(bf16[128,2048]{1,0:T(8,128)(2,1)S(1)} %collective-permute-done.4.refs_5_.refs_13_) | copy-start | bytes 1572868
  44.7 26.1 %collective-permute-start.9 = (bf16[256,2048]{1,0:T(8,128)(2,1)S(1)}, bf16[256,2048]{1,0:T(8,128)(2,1)}, u32[]{:S(2)}, u32[]{:S(2)}) collective-permute-start(bf16[256,2048]{1,0:T(8,128)(2,1)S(1)} %pad_maximum_fusion), channel_id=1, source_target_pairs={{0,1},{1,0},{2,3},{3,2},{4,5},{5,4},{6,7},{7,6},{8,9},{9,8},{10,11... | collective-permute-start | bytes 3145736 | tf_op jit(solution)/shard_map/ppermute | solution.py:152
  48.8 24.4 %copy-start.7 = (s32[1,3]{1,0:T(1,128)S(1)}, s32[1,3]{1,0:T(1,128)}, u32[]{:S(2)}) copy-start(s32[1,3]{1,0:T(1,128)} %param.10) | copy-start | bytes 40
  48.9 26.2 %copy-start.2 = (bf16[16,2048]{1,0:T(8,128)(2,1)}, bf16[16,2048]{1,0:T(8,128)(2,1)S(1)}, u32[]{:S(2)}) copy-start(bf16[16,2048]{1,0:T(8,128)(2,1)S(1)} %fusion.9.refs_0_.refs_8_) | copy-start | bytes 196612
  49.0 21.5 %collective-permute-start.6 = (bf16[80,2048]{1,0:T(8,128)(2,1)S(1)}, bf16[80,2048]{1,0:T(8,128)(2,1)S(1)}, u32[]{:S(2)}, u32[]{:S(2)}) collective-permute-start(bf16[80,2048]{1,0:T(8,128)(2,1)S(1)} %get-tuple-element.72), channel_id=1, source_target_pairs={{0,2},{1,3},{2,4},{3,5},{4,6},{5,7},{6,0},{7,1},{8,10},{9,11},{10,... | collective-permute-start | bytes 983048 | tf_op jit(solution)/shard_map/ppermute | solution.py:152
  51.0 19.8 %collective-permute-start.7 = (bf16[80,2048]{1,0:T(8,128)(2,1)S(1)}, bf16[80,2048]{1,0:T(8,128)(2,1)S(1)}, u32[]{:S(2)}, u32[]{:S(2)}) collective-permute-start(bf16[80,2048]{1,0:T(8,128)(2,1)S(1)} %get-tuple-element.71), channel_id=1, source_target_pairs={{0,6},{1,7},{2,0},{3,1},{4,2},{5,3},{6,4},{7,5},{8,14},{9,15},{10,... | collective-permute-start | bytes 983048 | tf_op jit(solution)/shard_map/ppermute | solution.py:152
  56.4 14.1 %collective-permute-start.8 = (bf16[16,2048]{1,0:T(8,128)(2,1)S(1)}, bf16[16,2048]{1,0:T(8,128)(2,1)S(1)}, u32[]{:S(2)}, u32[]{:S(2)}) collective-permute-start(bf16[16,2048]{1,0:T(8,128)(2,1)S(1)} %fusion.9.refs_0_.refs_8_), channel_id=1, source_target_pairs={{0,4},{1,5},{2,6},{3,7},{4,0},{5,1},{6,2},{7,3},{8,12},{9,13},{10,... | collective-permute-start | bytes 196616 | tf_op jit(solution)/shard_map/ppermute | solution.py:152
  70.5 4.6 %copy-start.5 = (bf16[16,2048]{1,0:T(8,128)(2,1)}, bf16[16,2048]{1,0:T(8,128)(2,1)S(1)}, u32[]{:S(2)}) copy-start(bf16[16,2048]{1,0:T(8,128)(2,1)S(1)} %collective-permute-done.8.refs_1_.refs_9_) | copy-start | bytes 196612
  70.5 4.6 %copy-start.3 = (bf16[80,2048]{1,0:T(8,128)(2,1)}, bf16[80,2048]{1,0:T(8,128)(2,1)S(1)}, u32[]{:S(2)}) copy-start(bf16[80,2048]{1,0:T(8,128)(2,1)S(1)} %collective-permute-done.6.refs_2_.refs_10_) | copy-start | bytes 983044
  70.8 4.3 %copy-start.4 = (bf16[80,2048]{1,0:T(8,128)(2,1)}, bf16[80,2048]{1,0:T(8,128)(2,1)S(1)}, u32[]{:S(2)}) copy-start(bf16[80,2048]{1,0:T(8,128)(2,1)S(1)} %collective-permute-done.7.refs_3_.refs_11_) | copy-start | bytes 983044
  70.9 4.2 %collective-permute-start.10 = (bf16[192,2048]{1,0:T(8,128)(2,1)S(1)}, bf16[192,2048]{1,0:T(8,128)(2,1)S(1)}, u32[]{:S(2)}, u32[]{:S(2)}) collective-permute-start(bf16[192,2048]{1,0:T(8,128)(2,1)S(1)} %pad_maximum_fusion.1), channel_id=1, source_target_pairs={{0,1},{1,0},{2,3},{3,2},{4,5},{5,4},{6,7},{7,6},{8,9},{9,8},{10,11... | collective-permute-start | bytes 2359304 | tf_op jit(solution)/shard_map/ppermute | solution.py:152
  75.1 0.9 copy-start.6
  95.0 5.9 %collective-permute-start.11 = (bf16[448,2048]{1,0:T(8,128)(2,1)}, bf16[448,2048]{1,0:T(8,128)(2,1)S(1)}, u32[]{:S(2)}, u32[]{:S(2)}) collective-permute-start(bf16[448,2048]{1,0:T(8,128)(2,1)} %get-tuple-element.43), channel_id=1, source_target_pairs={{0,1},{1,0},{2,3},{3,2},{4,5},{5,4},{6,7},{7,6},{8,9},{9,8},{10,11... | collective-permute-start | bytes 5505032 | tf_op jit(solution)/shard_map/ppermute | solution.py:152
  100.9 1.5 copy-start
  103.1 23.3 %collective-permute-start.12 = (bf16[80,2048]{1,0:T(8,128)(2,1)S(1)}, bf16[80,2048]{1,0:T(8,128)(2,1)S(1)}, u32[]{:S(2)}, u32[]{:S(2)}) collective-permute-start(bf16[80,2048]{1,0:T(8,128)(2,1)S(1)} %pad_maximum_fusion.4), channel_id=1, source_target_pairs={{0,6},{1,7},{2,0},{3,1},{4,2},{5,3},{6,4},{7,5},{8,14},{9,15},{10,... | collective-permute-start | bytes 983048 | tf_op jit(solution)/shard_map/ppermute | solution.py:152
  107.8 18.6 %collective-permute-start.13 = (bf16[80,2048]{1,0:T(8,128)(2,1)S(1)}, bf16[80,2048]{1,0:T(8,128)(2,1)S(1)}, u32[]{:S(2)}, u32[]{:S(2)}) collective-permute-start(bf16[80,2048]{1,0:T(8,128)(2,1)S(1)} %pad_maximum_fusion.5), channel_id=1, source_target_pairs={{0,2},{1,3},{2,4},{3,5},{4,6},{5,7},{6,0},{7,1},{8,10},{9,11},{10,... | collective-permute-start | bytes 983048 | tf_op jit(solution)/shard_map/ppermute | solution.py:152
  110.5 15.9 %collective-permute-start.14 = (bf16[16,2048]{1,0:T(8,128)(2,1)S(1)}, bf16[16,2048]{1,0:T(8,128)(2,1)S(1)}, u32[]{:S(2)}, u32[]{:S(2)}) collective-permute-start(bf16[16,2048]{1,0:T(8,128)(2,1)S(1)} %get-tuple-element.63), channel_id=1, source_target_pairs={{0,4},{1,5},{2,6},{3,7},{4,0},{5,1},{6,2},{7,3},{8,12},{9,13},{10,... | collective-permute-start | bytes 196616 | tf_op jit(solution)/shard_map/ppermute | solution.py:152
  127.2 23.2 %collective-permute-start.15 = (bf16[2,16,2048]{2,1,0:T(8,128)(2,1)}, bf16[2,16,2048]{2,1,0:T(8,128)(2,1)S(1)}, u32[]{:S(2)}, u32[]{:S(2)}) collective-permute-start(bf16[2,16,2048]{2,1,0:T(8,128)(2,1)} %pad_maximum_fusion.7), channel_id=1, source_target_pairs={{0,496},{8,504},{16,0},{24,8},{32,16},{40,24},{48,32},{56,40},{64,... | collective-permute-start | bytes 393224 | tf_op jit(solution)/shard_map/ppermute | solution.py:19
  137.1 23.3 %collective-permute-start.18 = (bf16[128,2048]{1,0:T(8,128)(2,1)S(1)}, bf16[128,2048]{1,0:T(8,128)(2,1)}, u32[]{:S(2)}, u32[]{:S(2)}) collective-permute-start(bf16[128,2048]{1,0:T(8,128)(2,1)S(1)} %add_convert_fusion.2), channel_id=1, source_target_pairs={{2,0},{3,1},{4,2},{5,3},{6,4},{7,5},{10,8},{11,9},{12,10},{13,11},... | collective-permute-start | bytes 1572872 | tf_op jit(solution)/shard_map/ppermute | solution.py:152
  138.5 21.9 %collective-permute-start.19 = (bf16[128,2048]{1,0:T(8,128)(2,1)S(1)}, bf16[128,2048]{1,0:T(8,128)(2,1)}, u32[]{:S(2)}, u32[]{:S(2)}) collective-permute-start(bf16[128,2048]{1,0:T(8,128)(2,1)S(1)} %add_convert_fusion.1), channel_id=1, source_target_pairs={{6,0},{7,1},{0,2},{1,3},{14,8},{15,9},{8,10},{9,11},{22,16},{23,17... | collective-permute-start | bytes 1572872 | tf_op jit(solution)/shard_map/ppermute | solution.py:152
  144.0 9.2 %collective-permute-start.16 = (bf16[2,16,2048]{2,1,0:T(8,128)(2,1)}, bf16[2,16,2048]{2,1,0:T(8,128)(2,1)S(1)}, u32[]{:S(2)}, u32[]{:S(2)}) collective-permute-start(bf16[2,16,2048]{2,1,0:T(8,128)(2,1)} %pad_maximum_fusion.8), channel_id=1, source_target_pairs={{0,480},{8,488},{16,496},{24,504},{32,0},{40,8},{48,16},{56,24},{6... | collective-permute-start | bytes 393224 | tf_op jit(solution)/shard_map/ppermute | solution.py:19
  147.1 8.2 %collective-permute-start.17 = (bf16[2,16,2048]{2,1,0:T(8,128)(2,1)}, bf16[2,16,2048]{2,1,0:T(8,128)(2,1)}, u32[]{:S(2)}, u32[]{:S(2)}) collective-permute-start(bf16[2,16,2048]{2,1,0:T(8,128)(2,1)} %pad_maximum_fusion.9), channel_id=1, source_target_pairs={{0,464},{8,472},{16,480},{24,488},{32,496},{40,504},{48,0},{56,8},... | collective-permute-start | bytes 393224 | tf_op jit(solution)/shard_map/ppermute | solution.py:19
  161.2 14.1 %collective-permute-start.20 = (bf16[16,2048]{1,0:T(8,128)(2,1)S(1)}, bf16[16,2048]{1,0:T(8,128)(2,1)S(1)}, u32[]{:S(2)}, u32[]{:S(2)}) collective-permute-start(bf16[16,2048]{1,0:T(8,128)(2,1)S(1)} %fusion.4), channel_id=1, source_target_pairs={{0,504},{8,0},{16,8},{24,16},{32,24},{40,32},{48,40},{56,48},{64,5... | collective-permute-start | bytes 196616 | tf_op jit(solution)/shard_map/ppermute | solution.py:19

commit v4 on v2

--- a/solution.py
+++ b/solution.py
@@ -24,8 +24,8 @@
     return jnp.concatenate([block[:, h * HD : (h + 1) * HD] for h in range(heads)], axis=0)
 
 
-def attention_kernel(span, info, q_ref, g_ref, k_ref, v_ref, pk_ref, pv_ref, start_ref,
-                     dq_ref, keep_ref, give_ref, dp_ref, bias):
+def attention_kernel(span, n_seq, info, q_ref, g_ref, k_ref, v_ref, pk_ref, pv_ref, start_ref,
+                     dq_ref, dkv_ref, pkeep_ref, pgive_ref, bias):
     rows = q_ref.shape[0]
     heads = q_ref.shape[1] // HD
     plen = pk_ref.shape[0]
@@ -34,6 +34,10 @@
     scale = HD ** -0.5
     me = info[0]
     head = pl.program_id(0)
+    slot = plen // n_seq
+    chips = n_seq // 2
+    chip = lax.div(me, 2)
+    odd = lax.rem(me, 2) == 1
 
     @pl.when(head == 0)
     def _():
@@ -42,6 +46,7 @@
         q_ids = own + lax.broadcasted_iota(jnp.int32, (window, rows), 1)
         seen = (k_ids >= start_ref[...]) & (k_ids <= q_ids)
         bias[...] = jnp.where(seen, 0.0, NEG)
+        dkv_ref[...] = jnp.zeros_like(dkv_ref)
 
     near = [
         pl.ds(pl.multiple_of(jnp.maximum(me - back, 0) * rows, rows), rows)
@@ -73,14 +78,17 @@
     for part, base in ((d_key, 0), (d_value, half)):
         part = part.astype(jnp.bfloat16)
         columns = pl.ds(pl.multiple_of(base + head * HD, HD), HD)
-        dp_ref[:, columns] = part[:plen]
-        for back in range(span + 1):
-            block = part[plen + (span - back) * rows : plen + (span - back + 1) * rows]
-            into = (keep_ref, give_ref)[back % 2]
-            into[back // 2, :, columns] = block
-
-
-def attend(q_rows, grad_rows, kv, prompt, q_start, me, span):
+        for i, at in enumerate(near):
+            dkv_ref[at, columns] = part[plen + i * rows : plen + (i + 1) * rows]
+        for c in range(chips):
+            first = part[2 * c * slot : (2 * c + 1) * slot]
+            second = part[(2 * c + 1) * slot : (2 * c + 2) * slot]
+            back = pl.multiple_of(lax.rem(chip - c + chips, chips) * slot, slot)
+            pkeep_ref[pl.ds(back, slot), columns] = jnp.where(odd, second, first)
+            pgive_ref[pl.ds(back, slot), columns] = jnp.where(odd, first, second)
+
+
+def attend(q_rows, grad_rows, kv, prompt, q_start, me, span, n_seq):
     rows, columns = q_rows.shape
     total, width = kv.shape
     plen = prompt.shape[0]
@@ -89,9 +97,8 @@
     at = lambda n, col: pl.BlockSpec((n, col), lambda g, s: (0, g))
     later = lambda n: pl.BlockSpec((n, HD), lambda g, s: (0, KVH + g))
     pairs = (span + 1) * rows + plen
-    kept, given = span // 2 + 1, (span + 1) // 2
     return pl.pallas_call(
-        functools.partial(attention_kernel, span),
+        functools.partial(attention_kernel, span, n_seq),
         grid_spec=pltpu.PrefetchScalarGridSpec(
             num_scalar_prefetch=1,
             grid=(KVH,),
@@ -106,17 +113,17 @@
             ],
             out_specs=[
                 at(rows, group),
-                pl.BlockSpec((kept, rows, width), lambda g, s: (0, 0, 0)),
-                pl.BlockSpec((given, rows, width), lambda g, s: (0, 0, 0)),
-                pl.BlockSpec((plen, width), lambda g, s: (0, 0)),
+                pl.BlockSpec((total, width), lambda g, s: (0, 0)),
+                pl.BlockSpec((plen // 2, width), lambda g, s: (0, 0)),
+                pl.BlockSpec((plen // 2, width), lambda g, s: (0, 0)),
             ],
             scratch_shapes=[pltpu.VMEM(((span + 1) * rows, rows), jnp.float32)],
         ),
         out_shape=[
             jax.ShapeDtypeStruct((rows, columns), bf16),
-            jax.ShapeDtypeStruct((kept, rows, width), bf16),
-            jax.ShapeDtypeStruct((given, rows, width), bf16),
-            jax.ShapeDtypeStruct((plen, width), bf16),
+            jax.ShapeDtypeStruct((total, width), bf16),
+            jax.ShapeDtypeStruct((plen // 2, width), bf16),
+            jax.ShapeDtypeStruct((plen // 2, width), bf16),
         ],
         compiler_params=pltpu.CompilerParams(vmem_limit_bytes=56 * 1024 * 1024),
         cost_estimate=pl.CostEstimate(
@@ -134,32 +141,49 @@
     return total.astype(jnp.bfloat16)
 
 
-def gradients_home(keep, give, me_seq):
+def added(*parts):
+    total = parts[0].astype(jnp.float32)
+    for part in parts[1:]:
+        total = total + part.astype(jnp.float32)
+    return total.astype(jnp.bfloat16)
+
+
+def along_seq(value, pairs):
+    return lax.ppermute(value, "seq", pairs)
+
+
+def prompt_for(prompt, offset):
+    by1 = passed_along(prompt, "dp", 1)
+    pair = jnp.concatenate([prompt, by1])
+    pairs = [passed_along(pair, "dp", step) for step in range(2, SPREAD, 2)]
+    window = jnp.concatenate([pair, *pairs])
+    chosen = lax.dynamic_index_in_dim(window, offset, 0, keepdims=False)
+    return lax.all_gather(chosen, "seq", axis=0, tiled=True)
+
+
+def prompt_home_sum(keep, give, offset):
     n = lax.axis_size("seq")
-    rows = keep.shape[1]
-    cut = rows // 2
-    odd = jnp.mod(me_seq, 2) == 1
-    got = lax.ppermute(give, "seq", [(i, i ^ 1) for i in range(n)])
-    none = jnp.zeros_like(got[:1])
-    sums = added(
-        jnp.concatenate([keep, none]),
-        jnp.where(odd, jnp.concatenate([none, got]), jnp.concatenate([got, none])),
-    )
-    own, one, two, three = sums[0], sums[1], sums[2], sums[3]
-    back = lax.ppermute(two[:cut], "seq", [(i, i - 2) for i in range(4, n)])
-    ahead = lax.ppermute(two[cut:], "seq", [(i, (i + 2) % n) for i in range(4, n)])
-    zero = jnp.zeros_like(back)
-    one = added(one, jnp.concatenate([back, zero]))
-    three = added(three, jnp.concatenate([zero, ahead]))
-    from_next = lax.ppermute(one, "seq", [(i, i - 2) for i in range(2, n)])
-    from_last = lax.ppermute(three, "seq", [(i, (i + 2) % n) for i in (n - 2, n - 1, 0, 1)])
-    return added(own, from_next, from_last)
+    slot = keep.shape[0] // (n // 2)
+    total = added(keep, along_seq(give, [(i, i ^ 1) for i in range(n)]))
+    mine, to_behind, to_across, to_ahead = [total[i * slot : (i + 1) * slot] for i in range(4)]
+    parts = [
+        along_seq(to_across, [(i, (i + 4) % n) for i in range(n)]),
+        along_seq(to_behind, [(i, (i - 2) % n) for i in range(n)]),
+        along_seq(to_ahead, [(i, (i + 2) % n) for i in range(n)]),
+    ]
+    total = added(mine, *parts)
+    left = [jnp.where(offset == i, total, jnp.zeros((), total.dtype)) for i in range(SPREAD)]
+    pairs = [
+        passed_along(jnp.stack(left[step : step + 2]), "dp", -step)
+        for step in range(2, SPREAD, 2)
+    ]
+    by1 = passed_along(added(left[1], *[pair[1] for pair in pairs]), "dp", -1)
+    return added(left[0], by1, *[pair[0] for pair in pairs])
 
 
 def on_device(queries, resp_kv, prompt_kv, d_out, resp_lengths, prompt_home):
     q_rows = queries[0]
     own_kv = resp_kv[0]
-    own_prompt = prompt_kv[0]
     grad_rows = d_out[0]
     rows = q_rows.shape[0]
     n_seq = lax.axis_size("seq")
@@ -170,33 +194,18 @@
     offset = jnp.mod(me_dp - prompt_home[0], n_dp)
 
     kv = lax.all_gather(own_kv, "seq", axis=0, tiled=True)
-
-    window = own_prompt[None]
-    reach = 1
-    while reach < SPREAD:
-        window = jnp.concatenate([window, passed_along(window, "dp", reach)], axis=0)
-        reach *= 2
-    chosen = lax.dynamic_index_in_dim(window, offset, 0, keepdims=False)
-    prompt = lax.all_gather(chosen, "seq", axis=0, tiled=True)
+    prompt = prompt_for(prompt_kv, offset)
 
     lengths = resp_lengths[0]
     starts = jnp.cumsum(lengths) - lengths
     q_ids = me_seq * rows + jnp.arange(rows, dtype=jnp.int32)
     q_start = jnp.max(jnp.where(starts[None, :] <= q_ids[:, None], starts[None, :], 0), axis=1)
-    d_query, keep, give, d_prompt = attend(
-        q_rows, grad_rows, kv, prompt, q_start, me_seq, span
+    d_query, d_near, keep, give = attend(
+        q_rows, grad_rows, kv, prompt, q_start, me_seq, span, n_seq
     )
-    prompt_grad = lax.psum_scatter(d_prompt, "seq", scatter_dimension=0, tiled=True)
-    d_kv = gradients_home(keep, give, me_seq)
-
-    slots = jnp.arange(SPREAD, dtype=jnp.int32)[:, None, None]
-    held = jnp.where(slots == offset, prompt_grad[None], jnp.zeros((), prompt_grad.dtype))
-    reach = SPREAD // 2
-    while reach > 0:
-        arrived = passed_along(held[reach:], "dp", -reach)
-        held = (held[:reach].astype(jnp.float32) + arrived.astype(jnp.float32)).astype(held.dtype)
-        reach //= 2
-    return (d_query[None], d_kv[None], held)
+    d_kv = lax.psum_scatter(d_near, "seq", scatter_dimension=0, tiled=True)
+    d_prompt = prompt_home_sum(keep, give, offset)
+    return (d_query[None], d_kv[None], d_prompt[None])
 
 
 def solution(mesh):

time: 199 us -> 167 us (0.84); the launches traced: 198 us -> 164 us
  waiting for transfers between devices: 85.3 us -> 52 us
  other arithmetic: 7.49 us -> 3 us
    reduce_scatter x1, waiting for transfers between devices: 36.7 us -> 7.22 us  [on_device(): d_kv = lax.psum_scatter(d_near, 'seq', scatter_dimension=0, tiled=True)]
    ppermute x5 -> x4, waiting for transfers between devices: 19.7 us -> 8.16 us  [along_seq(): return lax.ppermute(value, 'seq', pairs)]
    all_gather x1, waiting for transfers between devices: 6.17 us -> 13.4 us  [on_device(): kv = lax.all_gather(own_kv, 'seq', axis=0, tiled=True)]
    ppermute x6 -> x8, starting transfers between devices: 28.1 us -> 31.4 us  [passed_along(): lax.ppermute(value, axis, [(i, (i + by) % peers) for i in range(peers)])]
    ppermute x5 -> x4, starting transfers between devices: 14.6 us -> 13.1 us  [along_seq(): return lax.ppermute(value, 'seq', pairs)]
    ppermute x6 -> x8, waiting for transfers between devices: 22 us -> 22.5 us  [passed_along(): lax.ppermute(value, axis, [(i, (i + by) % peers) for i in range(peers)])]
  transfers between devices with their start and end apart: 13 -> 14, of which waited for: 10 -> 12; matrix products, arithmetic and copies ran while one was open for 3% -> 2% of each run, Pallas kernels for 0% -> 0%
where the time goes in v4:
time: 167 us; the launch traced here: 164 us
  waiting for transfers between devices  52 us (31%)
  starting transfers between devices  44.6 us (27%)
  blocking collectives  28.4 us (17%)
  Pallas kernels  19.2 us (11%)
  between operations  14.9 us (9%)
  other arithmetic  3 us (2%)
  local copies, waits for them, and re-layouts  1.83 us (1%)
    ppermute x8, starting transfers between devices, passed_along(): lax.ppermute(value, axis, [(i, (i + by) % peers) for i in range(peers)])  31.4 us
    all_gather x1, blocking collectives, prompt_for(): return lax.all_gather(chosen, 'seq', axis=0, tiled=True)  28.4 us
    ppermute x8, waiting for transfers between devices, passed_along(): lax.ppermute(value, axis, [(i, (i + by) % peers) for i in range(peers)])  22.5 us
    pallas_call x1, Pallas kernels, attend(): pl.pallas_call(functools.partial(attention_kernel, span, n_seq), grid_spe...  19.2 us
    all_gather x1, waiting for transfers between devices, on_device(): kv = lax.all_gather(own_kv, 'seq', axis=0, tiled=True)  13.4 us
    ppermute x4, starting transfers between devices, along_seq(): return lax.ppermute(value, 'seq', pairs)  13.1 us
    ppermute x4, waiting for transfers between devices, along_seq(): return lax.ppermute(value, 'seq', pairs)  8.16 us
    reduce_scatter x1, waiting for transfers between devices, on_device(): d_kv = lax.psum_scatter(d_near, 'seq', scatter_dimension=0, tiled=True)  7.22 us
  transfers between devices with their start and end apart: 14, of which 12 were waited for; matrix products, arithmetic and copies ran while one was open for 2% of the time, Pallas kernels for 0%

profile of v4, /device:TPU:1, one launch (start us, length us, event | category | flops | bytes accessed | tf_op | source)
XLA Modules:
  0.0 164.0 jit_solution(13918497508164004307)
XLA Ops:
  7.2 0.0 all-gather.4.cloned.1.call-start
  7.2 0.7 all-gather.4.cloned.1.call-update
  7.9 0.0 reduce-scatter.2.cloned.1.call-start
  7.9 4.8 %collective-permute-start = (bf16[1,16,2048]{2,1,0:T(8,128)(2,1)}, bf16[1,16,2048]{2,1,0:T(8,128)(2,1)S(1)}, u32[]{:S(2)}, u32[]{:S(2)}) collective-permute-start(bf16[1,16,2048]{2,1,0:T(8,128)(2,1)} %param.8), channel_id=1, source_target_pairs={{0,8},{8,16},{16,24},{24,32},{32,40},{40,48},{48,56},{56,64},{64,7... | collective-permute-start | bytes 196616 | tf_op jit(solution)/shard_map/ppermute | solution.py:19
  12.8 0.8 reduce-window_clone.1
  13.6 0.8 constant_dynamic-update-slice_fusion.1
  14.5 0.7 subtract_bitcast_fusion
  15.1 4.6 %collective-permute-done = bf16[1,16,2048]{2,1,0:T(8,128)(2,1)S(1)} collective-permute-done((bf16[1,16,2048]{2,1,0:T(8,128)(2,1)}, bf16[1,16,2048]{2,1,0:T(8,128)(2,1)S(1)}, u32[]{:S(2)}, u32[]{:S(2)}) %collective-permute-start) | collective-permute-done | bytes 65568 | tf_op jit(solution)/shard_map/ppermute | solution.py:19
  19.7 1.9 %collective-permute-start.1 = (bf16[2,16,2048]{2,1,0:T(8,128)(2,1)S(1)}, bf16[2,16,2048]{2,1,0:T(8,128)(2,1)S(1)}, u32[]{:S(2)}, u32[]{:S(2)}) collective-permute-start(bf16[2,16,2048]{2,1,0:T(8,128)(2,1)S(1)} %get-tuple-element.21), channel_id=1, source_target_pairs={{0,16},{8,24},{16,32},{24,40},{32,48},{40,56},{48,64},{56,72},{64,... | collective-permute-start | bytes 393224 | tf_op jit(solution)/shard_map/ppermute | solution.py:19
  22.4 0.6 select_reduce_fusion
  23.0 1.9 %collective-permute-start.2 = (bf16[2,16,2048]{2,1,0:T(8,128)(2,1)S(1)}, bf16[2,16,2048]{2,1,0:T(8,128)(2,1)S(1)}, u32[]{:S(2)}, u32[]{:S(2)}) collective-permute-start(bf16[2,16,2048]{2,1,0:T(8,128)(2,1)S(1)} %get-tuple-element.21), channel_id=1, source_target_pairs={{0,32},{8,40},{16,48},{24,56},{32,64},{40,72},{48,80},{56,88},{64,... | collective-permute-start | bytes 393224 | tf_op jit(solution)/shard_map/ppermute | solution.py:19
  24.9 3.1 %collective-permute-start.3 = (bf16[2,16,2048]{2,1,0:T(8,128)(2,1)S(1)}, bf16[2,16,2048]{2,1,0:T(8,128)(2,1)S(1)}, u32[]{:S(2)}, u32[]{:S(2)}) collective-permute-start(bf16[2,16,2048]{2,1,0:T(8,128)(2,1)S(1)} %get-tuple-element.21), channel_id=1, source_target_pairs={{0,48},{8,56},{16,64},{24,72},{32,80},{40,88},{48,96},{56,104},{64... | collective-permute-start | bytes 393224 | tf_op jit(solution)/shard_map/ppermute | solution.py:19
  28.0 0.8 collective-permute-done.1
  28.8 3.5 %collective-permute-done.2 = bf16[2,16,2048]{2,1,0:T(8,128)(2,1)S(1)} collective-permute-done((bf16[2,16,2048]{2,1,0:T(8,128)(2,1)S(1)}, bf16[2,16,2048]{2,1,0:T(8,128)(2,1)S(1)}, u32[]{:S(2)}, u32[]{:S(2)}) %collective-permute-start.2) | collective-permute-done | bytes 131104 | tf_op jit(solution)/shard_map/ppermute | solution.py:19
  32.3 2.5 %collective-permute-done.3 = bf16[2,16,2048]{2,1,0:T(8,128)(2,1)S(1)} collective-permute-done((bf16[2,16,2048]{2,1,0:T(8,128)(2,1)S(1)}, bf16[2,16,2048]{2,1,0:T(8,128)(2,1)S(1)}, u32[]{:S(2)}, u32[]{:S(2)}) %collective-permute-start.3) | collective-permute-done | bytes 131104 | tf_op jit(solution)/shard_map/ppermute | solution.py:19
  34.8 28.4 %all-gather.1 = bf16[1,128,2048]{2,1,0:T(8,128)(2,1)} all-gather(bf16[1,16,2048]{2,1,0:T(8,128)(2,1)S(1)} %constant_dynamic-slice_fusion), channel_id=3, replica_groups=mesh['dp'=64,'seq'=8] {'seq'}, dimensions={1}, use_global_device_ids=true | all-gather | bytes 589824 | tf_op jit(solution)/shard_map/all_gather | solution.py:161
  63.2 13.4 %all-gather.4.cloned.1.call-done = bf16[1,1024,2048]{2,1,0:T(8,128)(2,1)} async-done(((bf16[1,128,2048]{2,1,0:T(8,128)(2,1)}), bf16[1,1024,2048]{2,1,0:T(8,128)(2,1)}) %all-gather.4.cloned.1.call-update) | async-done | bytes 4194320 | tf_op jit(solution)/shard_map/all_gather | solution.py:196
  76.6 19.2 %shard_map.85 = (bf16[128,4096]{1,0:T(8,128)(2,1)}, bf16[1024,2048]{1,0:T(8,128)(2,1)}, bf16[64,2048]{1,0:T(8,128)(2,1)}, bf16[64,2048]{1,0:T(8,128)(2,1)}) custom-call(s32[1]{0:T(128)} %bitcast.info, bf16[128,4096]{1,0:T(8,128)(2,1)} %bitcast.60, bf16[128,4096]{1,0:T(8,128)(2,1)} %bitcast.61, bf16[1024,2048]{1,0:T(8,128)(2,1)} %bitcast.58, ...), custom_call_target="tpu_custom_call" | custom-call | flops 4697620480 | bytes 12582912 | tf_op jit(solution)/shard_map/pallas_call | solution.py:100
  95.8 0.0 copy-start.1
  95.8 0.0 copy-start
  95.8 0.0 reduce-scatter.2.cloned.1.call-update
  95.8 0.9 copy-done.1
  96.7 2.2 %collective-permute-start.4 = (bf16[64,2048]{1,0:T(8,128)(2,1)S(1)}, bf16[64,2048]{1,0:T(8,128)(2,1)S(1)}, u32[]{:S(2)}, u32[]{:S(2)}) collective-permute-start(bf16[64,2048]{1,0:T(8,128)(2,1)S(1)} %copy-done.1), channel_id=1, source_target_pairs={{0,1},{1,0},{2,3},{3,2},{4,5},{5,4},{6,7},{7,6},{8,9},{9,8},{10,11... | collective-permute-start | bytes 786440 | tf_op jit(solution)/shard_map/ppermute | solution.py:152
  98.9 1.3 collective-permute-done.4
  100.2 0.0 copy-done
  100.2 0.1 add_convert_fusion
  100.3 4.2 %collective-permute-start.5 = (bf16[16,2048]{1,0:T(8,128)(2,1)S(1)}, bf16[16,2048]{1,0:T(8,128)(2,1)S(1)}, u32[]{:S(2)}, u32[]{:S(2)}) collective-permute-start(bf16[16,2048]{1,0:T(8,128)(2,1)S(1)} %get-tuple-element.13), channel_id=1, source_target_pairs={{0,4},{1,5},{2,6},{3,7},{4,0},{5,1},{6,2},{7,3},{8,12},{9,13},{10,... | collective-permute-start | bytes 196616 | tf_op jit(solution)/shard_map/ppermute | solution.py:152
  104.5 4.8 %collective-permute-start.6 = (bf16[16,2048]{1,0:T(8,128)(2,1)S(1)}, bf16[16,2048]{1,0:T(8,128)(2,1)S(1)}, u32[]{:S(2)}, u32[]{:S(2)}) collective-permute-start(bf16[16,2048]{1,0:T(8,128)(2,1)S(1)} %get-tuple-element.15), channel_id=1, source_target_pairs={{0,6},{1,7},{2,0},{3,1},{4,2},{5,3},{6,4},{7,5},{8,14},{9,15},{10,... | collective-permute-start | bytes 196616 | tf_op jit(solution)/shard_map/ppermute | solution.py:152
  109.3 1.9 %collective-permute-start.7 = (bf16[16,2048]{1,0:T(8,128)(2,1)S(1)}, bf16[16,2048]{1,0:T(8,128)(2,1)S(1)}, u32[]{:S(2)}, u32[]{:S(2)}) collective-permute-start(bf16[16,2048]{1,0:T(8,128)(2,1)S(1)} %get-tuple-element.14), channel_id=1, source_target_pairs={{0,2},{1,3},{2,4},{3,5},{4,6},{5,7},{6,0},{7,1},{8,10},{9,11},{10,... | collective-permute-start | bytes 196616 | tf_op jit(solution)/shard_map/ppermute | solution.py:152
  111.2 0.0 collective-permute-done.5
  111.3 3.7 %collective-permute-done.6 = bf16[16,2048]{1,0:T(8,128)(2,1)S(1)} collective-permute-done((bf16[16,2048]{1,0:T(8,128)(2,1)S(1)}, bf16[16,2048]{1,0:T(8,128)(2,1)S(1)}, u32[]{:S(2)}, u32[]{:S(2)}) %collective-permute-start.6) | collective-permute-done | bytes 65568 | tf_op jit(solution)/shard_map/ppermute | solution.py:152
  115.0 3.2 %collective-permute-done.7 = bf16[16,2048]{1,0:T(8,128)(2,1)S(1)} collective-permute-done((bf16[16,2048]{1,0:T(8,128)(2,1)S(1)}, bf16[16,2048]{1,0:T(8,128)(2,1)S(1)}, u32[]{:S(2)}, u32[]{:S(2)}) %collective-permute-start.7) | collective-permute-done | bytes 65568 | tf_op jit(solution)/shard_map/ppermute | solution.py:152
  118.3 7.2 %collective-permute-start.8 = (bf16[2,16,2048]{2,1,0:T(8,128)(2,1)S(1)}, bf16[2,16,2048]{2,1,0:T(8,128)(2,1)S(1)}, u32[]{:S(2)}, u32[]{:S(2)}) collective-permute-start(bf16[2,16,2048]{2,1,0:T(8,128)(2,1)S(1)} %pad_maximum_fusion), channel_id=1, source_target_pairs={{0,496},{8,504},{16,0},{24,8},{32,16},{40,24},{48,32},{56,40},{64,... | collective-permute-start | bytes 393224 | tf_op jit(solution)/shard_map/ppermute | solution.py:19
  125.5 2.7 %collective-permute-start.9 = (bf16[2,16,2048]{2,1,0:T(8,128)(2,1)S(1)}, bf16[2,16,2048]{2,1,0:T(8,128)(2,1)S(1)}, u32[]{:S(2)}, u32[]{:S(2)}) collective-permute-start(bf16[2,16,2048]{2,1,0:T(8,128)(2,1)S(1)} %pad_maximum_fusion.1), channel_id=1, source_target_pairs={{0,480},{8,488},{16,496},{24,504},{32,0},{40,8},{48,16},{56,24},{6... | collective-permute-start | bytes 393224 | tf_op jit(solution)/shard_map/ppermute | solution.py:19
  128.2 3.3 %collective-permute-start.10 = (bf16[2,16,2048]{2,1,0:T(8,128)(2,1)S(1)}, bf16[2,16,2048]{2,1,0:T(8,128)(2,1)S(1)}, u32[]{:S(2)}, u32[]{:S(2)}) collective-permute-start(bf16[2,16,2048]{2,1,0:T(8,128)(2,1)S(1)} %pad_maximum_fusion.2), channel_id=1, source_target_pairs={{0,464},{8,472},{16,480},{24,488},{32,496},{40,504},{48,0},{56,8},... | collective-permute-start | bytes 393224 | tf_op jit(solution)/shard_map/ppermute | solution.py:19
  131.5 0.0 collective-permute-done.8
  131.5 3.0 %collective-permute-done.9 = bf16[2,16,2048]{2,1,0:T(8,128)(2,1)S(1)} collective-permute-done((bf16[2,16,2048]{2,1,0:T(8,128)(2,1)S(1)}, bf16[2,16,2048]{2,1,0:T(8,128)(2,1)S(1)}, u32[]{:S(2)}, u32[]{:S(2)}) %collective-permute-start.9) | collective-permute-done | bytes 131104 | tf_op jit(solution)/shard_map/ppermute | solution.py:19
  134.5 1.4 collective-permute-done.10
  136.0 6.5 %collective-permute-start.11 = (bf16[16,2048]{1,0:T(8,128)(2,1)S(1)}, bf16[16,2048]{1,0:T(8,128)(2,1)S(1)}, u32[]{:S(2)}, u32[]{:S(2)}) collective-permute-start(bf16[16,2048]{1,0:T(8,128)(2,1)S(1)} %fusion.1), channel_id=1, source_target_pairs={{0,504},{8,0},{16,8},{24,16},{32,24},{40,32},{48,40},{56,48},{64,5... | collective-permute-start | bytes 196616 | tf_op jit(solution)/shard_map/ppermute | solution.py:19
  142.5 6.7 %collective-permute-done.11 = bf16[16,2048]{1,0:T(8,128)(2,1)S(1)} collective-permute-done((bf16[16,2048]{1,0:T(8,128)(2,1)S(1)}, bf16[16,2048]{1,0:T(8,128)(2,1)S(1)}, u32[]{:S(2)}, u32[]{:S(2)}) %collective-permute-start.11) | collective-permute-done | bytes 65568 | tf_op jit(solution)/shard_map/ppermute | solution.py:19
  149.2 0.7 fusion.2
  149.9 7.2 %reduce-scatter.2.cloned.1.call-done = bf16[128,2048]{1,0:T(8,128)(2,1)} async-done(((bf16[1024,2048]{1,0:T(8,128)(2,1)}), bf16[128,2048]{1,0:T(8,128)(2,1)}) %reduce-scatter.2.cloned.1.call-update) | async-done | bytes 524304 | tf_op jit(solution)/shard_map/reduce_scatter | solution.py:206
  (13 shorter events, 0.2 us)
Async XLA Ops:
  7.2 69.4 %all-gather.4.cloned.1.call-start = ((), (), s32[]{:S(2)}) async-start(), calls=%async_computation.2 | async-start | bytes 4718592 | tf_op jit(solution)/shard_map/all_gather | solution.py:196
  7.9 149.2 %reduce-scatter.2.cloned.1.call-start = ((), (), s32[]{:S(2)}) async-start(), calls=%async_computation.1 | async-start | bytes 4718592 | tf_op jit(solution)/shard_map/reduce_scatter | solution.py:206
  7.9 11.8 %collective-permute-start = (bf16[1,16,2048]{2,1,0:T(8,128)(2,1)}, bf16[1,16,2048]{2,1,0:T(8,128)(2,1)S(1)}, u32[]{:S(2)}, u32[]{:S(2)}) collective-permute-start(bf16[1,16,2048]{2,1,0:T(8,128)(2,1)} %param.8), channel_id=1, source_target_pairs={{0,8},{8,16},{16,24},{24,32},{32,40},{40,48},{48,56},{56,64},{64,7... | collective-permute-start | bytes 196616 | tf_op jit(solution)/shard_map/ppermute | solution.py:19
  19.7 9.0 %collective-permute-start.1 = (bf16[2,16,2048]{2,1,0:T(8,128)(2,1)S(1)}, bf16[2,16,2048]{2,1,0:T(8,128)(2,1)S(1)}, u32[]{:S(2)}, u32[]{:S(2)}) collective-permute-start(bf16[2,16,2048]{2,1,0:T(8,128)(2,1)S(1)} %get-tuple-element.21), channel_id=1, source_target_pairs={{0,16},{8,24},{16,32},{24,40},{32,48},{40,56},{48,64},{56,72},{64,... | collective-permute-start | bytes 393224 | tf_op jit(solution)/shard_map/ppermute | solution.py:19
  23.0 9.3 %collective-permute-start.2 = (bf16[2,16,2048]{2,1,0:T(8,128)(2,1)S(1)}, bf16[2,16,2048]{2,1,0:T(8,128)(2,1)S(1)}, u32[]{:S(2)}, u32[]{:S(2)}) collective-permute-start(bf16[2,16,2048]{2,1,0:T(8,128)(2,1)S(1)} %get-tuple-element.21), channel_id=1, source_target_pairs={{0,32},{8,40},{16,48},{24,56},{32,64},{40,72},{48,80},{56,88},{64,... | collective-permute-start | bytes 393224 | tf_op jit(solution)/shard_map/ppermute | solution.py:19
  24.9 9.9 %collective-permute-start.3 = (bf16[2,16,2048]{2,1,0:T(8,128)(2,1)S(1)}, bf16[2,16,2048]{2,1,0:T(8,128)(2,1)S(1)}, u32[]{:S(2)}, u32[]{:S(2)}) collective-permute-start(bf16[2,16,2048]{2,1,0:T(8,128)(2,1)S(1)} %get-tuple-element.21), channel_id=1, source_target_pairs={{0,48},{8,56},{16,64},{24,72},{32,80},{40,88},{48,96},{56,104},{64... | collective-permute-start | bytes 393224 | tf_op jit(solution)/shard_map/ppermute | solution.py:19
  95.8 0.9 copy-start.1
  95.8 4.4 %copy-start = (bf16[64,2048]{1,0:T(8,128)(2,1)S(1)}, bf16[64,2048]{1,0:T(8,128)(2,1)}, u32[]{:S(2)}) copy-start(bf16[64,2048]{1,0:T(8,128)(2,1)} %get-tuple-element.9) | copy-start | bytes 786436
  96.7 3.4 %collective-permute-start.4 = (bf16[64,2048]{1,0:T(8,128)(2,1)S(1)}, bf16[64,2048]{1,0:T(8,128)(2,1)S(1)}, u32[]{:S(2)}, u32[]{:S(2)}) collective-permute-start(bf16[64,2048]{1,0:T(8,128)(2,1)S(1)} %copy-done.1), channel_id=1, source_target_pairs={{0,1},{1,0},{2,3},{3,2},{4,5},{5,4},{6,7},{7,6},{8,9},{9,8},{10,11... | collective-permute-start | bytes 786440 | tf_op jit(solution)/shard_map/ppermute | solution.py:152
  100.3 11.0 %collective-permute-start.5 = (bf16[16,2048]{1,0:T(8,128)(2,1)S(1)}, bf16[16,2048]{1,0:T(8,128)(2,1)S(1)}, u32[]{:S(2)}, u32[]{:S(2)}) collective-permute-start(bf16[16,2048]{1,0:T(8,128)(2,1)S(1)} %get-tuple-element.13), channel_id=1, source_target_pairs={{0,4},{1,5},{2,6},{3,7},{4,0},{5,1},{6,2},{7,3},{8,12},{9,13},{10,... | collective-permute-start | bytes 196616 | tf_op jit(solution)/shard_map/ppermute | solution.py:152
  104.5 10.5 %collective-permute-start.6 = (bf16[16,2048]{1,0:T(8,128)(2,1)S(1)}, bf16[16,2048]{1,0:T(8,128)(2,1)S(1)}, u32[]{:S(2)}, u32[]{:S(2)}) collective-permute-start(bf16[16,2048]{1,0:T(8,128)(2,1)S(1)} %get-tuple-element.15), channel_id=1, source_target_pairs={{0,6},{1,7},{2,0},{3,1},{4,2},{5,3},{6,4},{7,5},{8,14},{9,15},{10,... | collective-permute-start | bytes 196616 | tf_op jit(solution)/shard_map/ppermute | solution.py:152
  109.3 8.9 %collective-permute-start.7 = (bf16[16,2048]{1,0:T(8,128)(2,1)S(1)}, bf16[16,2048]{1,0:T(8,128)(2,1)S(1)}, u32[]{:S(2)}, u32[]{:S(2)}) collective-permute-start(bf16[16,2048]{1,0:T(8,128)(2,1)S(1)} %get-tuple-element.14), channel_id=1, source_target_pairs={{0,2},{1,3},{2,4},{3,5},{4,6},{5,7},{6,0},{7,1},{8,10},{9,11},{10,... | collective-permute-start | bytes 196616 | tf_op jit(solution)/shard_map/ppermute | solution.py:152
  118.3 13.2 %collective-permute-start.8 = (bf16[2,16,2048]{2,1,0:T(8,128)(2,1)S(1)}, bf16[2,16,2048]{2,1,0:T(8,128)(2,1)S(1)}, u32[]{:S(2)}, u32[]{:S(2)}) collective-permute-start(bf16[2,16,2048]{2,1,0:T(8,128)(2,1)S(1)} %pad_maximum_fusion), channel_id=1, source_target_pairs={{0,496},{8,504},{16,0},{24,8},{32,16},{40,24},{48,32},{56,40},{64,... | collective-permute-start | bytes 393224 | tf_op jit(solution)/shard_map/ppermute | solution.py:19
  125.5 9.0 %collective-permute-start.9 = (bf16[2,16,2048]{2,1,0:T(8,128)(2,1)S(1)}, bf16[2,16,2048]{2,1,0:T(8,128)(2,1)S(1)}, u32[]{:S(2)}, u32[]{:S(2)}) collective-permute-start(bf16[2,16,2048]{2,1,0:T(8,128)(2,1)S(1)} %pad_maximum_fusion.1), channel_id=1, source_target_pairs={{0,480},{8,488},{16,496},{24,504},{32,0},{40,8},{48,16},{56,24},{6... | collective-permute-start | bytes 393224 | tf_op jit(solution)/shard_map/ppermute | solution.py:19
  128.2 7.7 %collective-permute-start.10 = (bf16[2,16,2048]{2,1,0:T(8,128)(2,1)S(1)}, bf16[2,16,2048]{2,1,0:T(8,128)(2,1)S(1)}, u32[]{:S(2)}, u32[]{:S(2)}) collective-permute-start(bf16[2,16,2048]{2,1,0:T(8,128)(2,1)S(1)} %pad_maximum_fusion.2), channel_id=1, source_target_pairs={{0,464},{8,472},{16,480},{24,488},{32,496},{40,504},{48,0},{56,8},... | collective-permute-start | bytes 393224 | tf_op jit(solution)/shard_map/ppermute | solution.py:19
  136.0 13.3 %collective-permute-start.11 = (bf16[16,2048]{1,0:T(8,128)(2,1)S(1)}, bf16[16,2048]{1,0:T(8,128)(2,1)S(1)}, u32[]{:S(2)}, u32[]{:S(2)}) collective-permute-start(bf16[16,2048]{1,0:T(8,128)(2,1)S(1)} %fusion.1), channel_id=1, source_target_pairs={{0,504},{8,0},{16,8},{24,16},{32,24},{40,32},{48,40},{56,48},{64,5... | collective-permute-start | bytes 196616 | tf_op jit(solution)/shard_map/ppermute | solution.py:19
Sparse Core Ops, SparseCore 0:
  10.1 66.3 all-gather.3
  96.0 61.1 reduce-scatter.1

commit v5 on v3

--- a/solution.py
+++ b/solution.py
@@ -162,24 +162,25 @@
     tied = lax.optimization_barrier
 
     by1 = passed_along(prompt, "dp", 1)
+    top2 = along_seq(own[:cut], [(i, i + 2) for i in range(n - 2)])
+    low6 = along_seq(own[cut:], [(i, (i - 2) % n) for i in range(4)])
+    low, top2 = tied((own[cut:], top2))
+    top, low6 = tied((own[:cut], low6))
+    low2 = along_seq(low, [(i, i + 2) for i in range(n - 2)])
+    top6 = along_seq(top, [(1, n - 1)])
     pair = jnp.concatenate([prompt, by1])
-    pair, own = tied((pair, own))
-    two = along_seq(own, [(i, i + 2) for i in range(n - 2)])
-    six = along_seq(own, [(i, (i - 2) % n) for i in range(4)])
     pairs = [passed_along(pair, "dp", step) for step in range(2, SPREAD, 2)]
-    *pairs, two, six = tied((*pairs, two, six))
-    top2, low6 = two[:cut], six[cut:]
+    *pairs, top2, low6 = tied((*pairs, top2, low6))
 
     window = jnp.concatenate([pair, *pairs])
     chosen = lax.dynamic_index_in_dim(window, offset, 0, keepdims=False)
     from_last = along_seq(jnp.concatenate([top2, chosen]), ahead)
     from_next = along_seq(jnp.concatenate([low6, chosen]), behind)
     from_across = along_seq(chosen, across)
+    two = jnp.concatenate([top2, low2])
+    six = jnp.concatenate([top6, low6])
     near = jnp.concatenate([jnp.where(odd, two, own), jnp.where(odd, six, two)])
     got_near = along_seq(near, swap)
-    from_last, from_next, from_across, chosen, got_near = tied(
-        (from_last, from_next, from_across, chosen, got_near)
-    )
     got_far = along_seq(jnp.concatenate([from_last, from_next, chosen, from_across]), swap)
     return [chosen, from_across, from_last, from_next, own, two, got_near, got_far]
 
@@ -211,28 +212,26 @@
     from_next = along_seq(jnp.concatenate([two[:cut], to_behind]), behind)
     from_last = along_seq(jnp.concatenate([two[cut:], to_ahead]), ahead)
     from_across = along_seq(to_across, across)
-    from_next, from_last, from_across, one, three = tied(
-        (from_next, from_last, from_across, one, three)
-    )
+    low1 = along_seq(one[cut:], [(i, i - 2) for i in range(2, n)])
+    top3 = along_seq(three[:cut], [(n - 1, 1)])
+    from_next, from_last, from_across = tied((from_next, from_last, from_across))
 
     prompt = added(mine, from_next[cut:], from_last[cut:], from_across)
     none = jnp.zeros((), prompt.dtype)
     left = [jnp.where(offset == i, prompt, none) for i in range(SPREAD)]
-    zero = jnp.zeros_like(prompt, shape=(cut,) + prompt.shape[1:])
     passing = (me >= n - 2) | (me < 2)
-    one = added(one, jnp.concatenate([from_next[:cut], zero]))
-    three = added(
-        three, jnp.concatenate([zero, jnp.where(passing, from_last[:cut], none)])
-    )
-    from_next = along_seq(one, [(i, i - 2) for i in range(2, n)])
-    from_last = along_seq(three, [(i, (i + 2) % n) for i in (n - 2, n - 1, 0, 1)])
+    top_one = added(one[:cut], from_next[:cut])
+    low_three = added(three[cut:], jnp.where(passing, from_last[:cut], none))
+    top_one, low_three, low1, top3 = tied((top_one, low_three, low1, top3))
     pairs = [
         passed_along(jnp.stack(left[step : step + 2]), "dp", -step)
         for step in range(2, SPREAD, 2)
     ]
-    *pairs, from_next, from_last = tied((*pairs, from_next, from_last))
+    top1 = along_seq(top_one, [(i, i - 2) for i in range(2, n)])
+    low3 = along_seq(low_three, [(i, (i + 2) % n) for i in (n - 2, n - 1, 0, 1)])
+    *pairs, top1, low3 = tied((*pairs, top1, low3))
     by1 = passed_along(added(left[1], *[pair[1] for pair in pairs]), "dp", -1)
-    d_kv = added(own, from_next, from_last)
+    d_kv = added(own, jnp.concatenate([top1, low1]), jnp.concatenate([top3, low3]))
     return d_kv, added(left[0], by1, *[pair[0] for pair in pairs])
 
 

time: 178 us -> 163 us (0.916)
  waiting for transfers between devices: 55.2 us -> 41.1 us
  local copies, waits for them, and re-layouts: 1.44 us -> 4.23 us
  starting transfers between devices: 88.8 us -> 86.5 us
    ppermute x8, starting transfers between devices: 39.8 us -> 29.1 us  [passed_along(): lax.ppermute(value, axis, [(i, (i + by) % peers) for i in range(peers)])]
    ppermute x8, waiting for transfers between devices: 17.9 us -> 8.72 us  [passed_along(): lax.ppermute(value, axis, [(i, (i + by) % peers) for i in range(peers)])]
    ppermute x13 -> x17, starting transfers between devices: 49 us -> 57.4 us  [along_seq(): return lax.ppermute(value, 'seq', pairs)]
    ppermute x13 -> x17, waiting for transfers between devices: 37.3 us -> 32.4 us  [along_seq(): return lax.ppermute(value, 'seq', pairs)]
    broadcast_in_dim x2 -> x1, other arithmetic: 3.76 us -> 0.68 us  [on_device(): return (d_query[None], d_kv[None], d_prompt[None])]
    convert_element_type x5, other arithmetic: 2.79 us -> 5.05 us  [added(): return total.astype(jnp.bfloat16)]
    slice x4 -> x2, local copies, waits for them, and re-layouts: 0.1 us -> 1.95 us  [the longest x1 1.07 us: rounds_in(): top2 = along_seq(own[:cut], [(i, i + 2) for i in range(n - 2)])]
  transfers between devices with their start and end apart: 21 -> 25, of which waited for: 13 -> 10; matrix products, arithmetic and copies ran while one was open for 3% -> 5% of each run, Pallas kernels for 0% -> 0%
where the time goes in v5:
time: 163 us; the launch traced here: 162 us
  starting transfers between devices  86.5 us (53%)
  waiting for transfers between devices  41.1 us (25%)
  Pallas kernels  19 us (12%)
  other arithmetic  9.39 us (6%)
  local copies, waits for them, and re-layouts  4.23 us (3%)
  between operations  1.86 us (1%)
    ppermute x17, starting transfers between devices, along_seq(): return lax.ppermute(value, 'seq', pairs)  57.4 us
    ppermute x17, waiting for transfers between devices, along_seq(): return lax.ppermute(value, 'seq', pairs)  32.4 us
    ppermute x8, starting transfers between devices, passed_along(): lax.ppermute(value, axis, [(i, (i + by) % peers) for i in range(peers)])  29.1 us
    pallas_call x1, Pallas kernels, attend(): pl.pallas_call(functools.partial(attention_kernel, span, n_seq), grid_spe...  19 us
    ppermute x8, waiting for transfers between devices, passed_along(): lax.ppermute(value, axis, [(i, (i + by) % peers) for i in range(peers)])  8.72 us
    convert_element_type x5, other arithmetic, added(): return total.astype(jnp.bfloat16)  5.05 us
  transfers between devices with their start and end apart: 25, of which 10 were waited for; matrix products, arithmetic and copies ran while one was open for 5% of the time, Pallas kernels for 0%

profile of v5, /device:TPU:1, one launch (start us, length us, event | category | flops | bytes accessed | tf_op | source)
XLA Modules:
  0.0 162.0 jit_solution(4078723927005960898)
XLA Ops:
  0.6 4.8 %collective-permute-start = (bf16[1,16,2048]{2,1,0:T(8,128)(2,1)}, bf16[1,16,2048]{2,1,0:T(8,128)(2,1)S(1)}, u32[]{:S(2)}, u32[]{:S(2)}) collective-permute-start(bf16[1,16,2048]{2,1,0:T(8,128)(2,1)} %param.8), channel_id=1, source_target_pairs={{0,8},{8,16},{16,24},{24,32},{32,40},{40,48},{48,56},{56,64},{64,7... | collective-permute-start | bytes 196616 | tf_op jit(solution)/shard_map/ppermute | solution.py:19
  5.5 1.1 slice_bitcast_fusion.6
  6.5 0.0 copy-start
  6.6 6.0 %collective-permute-start.4 = (bf16[64,2048]{1,0:T(8,128)(2,1)S(1)}, bf16[64,2048]{1,0:T(8,128)(2,1)S(1)}, u32[]{:S(2)}, u32[]{:S(2)}) collective-permute-start(bf16[64,2048]{1,0:T(8,128)(2,1)S(1)} %get-tuple-element.36), channel_id=1, source_target_pairs={{0,2},{1,3},{2,4},{3,5},{4,6},{5,7},{8,10},{9,11},{10,12},{11,13},... | collective-permute-start | bytes 786440 | tf_op jit(solution)/shard_map/ppermute | solution.py:152
  12.5 5.2 %collective-permute-start.5 = (bf16[64,2048]{1,0:T(8,128)(2,1)S(1)}, bf16[64,2048]{1,0:T(8,128)(2,1)S(1)}, u32[]{:S(2)}, u32[]{:S(2)}) collective-permute-start(bf16[64,2048]{1,0:T(8,128)(2,1)S(1)} %get-tuple-element.35), channel_id=1, source_target_pairs={{0,6},{1,7},{2,0},{3,1},{8,14},{9,15},{10,8},{11,9},{16,22},{17,23... | collective-permute-start | bytes 786440 | tf_op jit(solution)/shard_map/ppermute | solution.py:152
  17.7 0.9 constant_dynamic-update-slice_fusion.1
  18.6 0.0 collective-permute-done
  18.6 4.4 %collective-permute-start.3 = (bf16[2,16,2048]{2,1,0:T(8,128)(2,1)S(1)}, bf16[2,16,2048]{2,1,0:T(8,128)(2,1)S(1)}, u32[]{:S(2)}, u32[]{:S(2)}) collective-permute-start(bf16[2,16,2048]{2,1,0:T(8,128)(2,1)S(1)} %get-tuple-element.75), channel_id=1, source_target_pairs={{0,48},{8,56},{16,64},{24,72},{32,80},{40,88},{48,96},{56,104},{64... | collective-permute-start | bytes 393224 | tf_op jit(solution)/shard_map/ppermute | solution.py:19
  23.0 3.4 %collective-permute-start.2 = (bf16[2,16,2048]{2,1,0:T(8,128)(2,1)S(1)}, bf16[2,16,2048]{2,1,0:T(8,128)(2,1)S(1)}, u32[]{:S(2)}, u32[]{:S(2)}) collective-permute-start(bf16[2,16,2048]{2,1,0:T(8,128)(2,1)S(1)} %get-tuple-element.75), channel_id=1, source_target_pairs={{0,32},{8,40},{16,48},{24,56},{32,64},{40,72},{48,80},{56,88},{64,... | collective-permute-start | bytes 393224 | tf_op jit(solution)/shard_map/ppermute | solution.py:19
  26.5 2.5 %collective-permute-start.1 = (bf16[2,16,2048]{2,1,0:T(8,128)(2,1)S(1)}, bf16[2,16,2048]{2,1,0:T(8,128)(2,1)S(1)}, u32[]{:S(2)}, u32[]{:S(2)}) collective-permute-start(bf16[2,16,2048]{2,1,0:T(8,128)(2,1)S(1)} %get-tuple-element.75), channel_id=1, source_target_pairs={{0,16},{8,24},{16,32},{24,40},{32,48},{40,56},{48,64},{56,72},{64,... | collective-permute-start | bytes 393224 | tf_op jit(solution)/shard_map/ppermute | solution.py:19
  29.7 0.0 collective-permute-done.4
  29.7 2.2 %collective-permute-start.9 = (bf16[64,2048]{1,0:T(8,128)(2,1)S(1)}, bf16[64,2048]{1,0:T(8,128)(2,1)S(1)}, u32[]{:S(2)}, u32[]{:S(2)}) collective-permute-start(bf16[64,2048]{1,0:T(8,128)(2,1)S(1)} %get-tuple-element.35), channel_id=1, source_target_pairs={{0,2},{1,3},{2,4},{3,5},{4,6},{5,7},{8,10},{9,11},{10,12},{11,13},... | collective-permute-start | bytes 786440 | tf_op jit(solution)/shard_map/ppermute | solution.py:152
  31.9 0.0 collective-permute-done.5
  31.9 2.6 %collective-permute-start.10 = (bf16[64,2048]{1,0:T(8,128)(2,1)S(1)}, bf16[64,2048]{1,0:T(8,128)(2,1)S(1)}, u32[]{:S(2)}, u32[]{:S(2)}) collective-permute-start(bf16[64,2048]{1,0:T(8,128)(2,1)S(1)} %get-tuple-element.36), channel_id=1, source_target_pairs={{1,7},{9,15},{17,23},{25,31},{33,39},{41,47},{49,55},{57,63},{65,7... | collective-permute-start | bytes 786440 | tf_op jit(solution)/shard_map/ppermute | solution.py:152
  34.5 1.3 collective-permute-done.1
  35.9 0.0 copy-start.3
  35.9 3.4 %collective-permute-start.6 = (bf16[16,2048]{1,0:T(8,128)(2,1)S(1)}, bf16[16,2048]{1,0:T(8,128)(2,1)S(1)}, u32[]{:S(2)}, u32[]{:S(2)}) collective-permute-start(bf16[16,2048]{1,0:T(8,128)(2,1)S(1)} %dynamic-slice_bitcast_fusion.refs_0_.refs_8_), channel_id=1, source_target_pairs={{0,4},{1,5},{2,6},{3,7},{4,0},{5,1},{6,2},{7,3},{8,12},{9,13},{10,... | collective-permute-start | bytes 196616 | tf_op jit(solution)/shard_map/ppermute | solution.py:152
  39.3 0.1 pad_maximum_fusion.2
  39.4 4.0 %collective-permute-start.8 = (bf16[80,2048]{1,0:T(8,128)(2,1)S(1)}, bf16[80,2048]{1,0:T(8,128)(2,1)S(1)}, u32[]{:S(2)}, u32[]{:S(2)}) collective-permute-start(bf16[80,2048]{1,0:T(8,128)(2,1)S(1)} %get-tuple-element.73), channel_id=1, source_target_pairs={{0,6},{1,7},{2,0},{3,1},{4,2},{5,3},{6,4},{7,5},{8,14},{9,15},{10,... | collective-permute-start | bytes 983048 | tf_op jit(solution)/shard_map/ppermute | solution.py:152
  43.4 2.2 %collective-permute-start.7 = (bf16[80,2048]{1,0:T(8,128)(2,1)S(1)}, bf16[80,2048]{1,0:T(8,128)(2,1)S(1)}, u32[]{:S(2)}, u32[]{:S(2)}) collective-permute-start(bf16[80,2048]{1,0:T(8,128)(2,1)S(1)} %get-tuple-element.74), channel_id=1, source_target_pairs={{0,2},{1,3},{2,4},{3,5},{4,6},{5,7},{6,0},{7,1},{8,10},{9,11},{10,... | collective-permute-start | bytes 983048 | tf_op jit(solution)/shard_map/ppermute | solution.py:152
  45.6 0.0 copy-start.2
  45.7 0.3 broadcast_select_fusion
  46.0 0.0 copy-start.10
  46.0 0.1 pad_maximum_fusion
  46.1 0.3 copy-done.2
  46.4 5.4 %collective-permute-start.11 = (bf16[256,2048]{1,0:T(8,128)(2,1)S(1)}, bf16[256,2048]{1,0:T(8,128)(2,1)}, u32[]{:S(2)}, u32[]{:S(2)}) collective-permute-start(bf16[256,2048]{1,0:T(8,128)(2,1)S(1)} %pad_maximum_fusion), channel_id=1, source_target_pairs={{0,1},{1,0},{2,3},{3,2},{4,5},{5,4},{6,7},{7,6},{8,9},{9,8},{10,11... | collective-permute-start | bytes 3145736 | tf_op jit(solution)/shard_map/ppermute | solution.py:152
  51.8 7.4 %collective-permute-done.8.refs_3_.refs_11_ = bf16[80,2048]{1,0:T(8,128)(2,1)S(1)} collective-permute-done((bf16[80,2048]{1,0:T(8,128)(2,1)S(1)}, bf16[80,2048]{1,0:T(8,128)(2,1)S(1)}, u32[]{:S(2)}, u32[]{:S(2)}) %collective-permute-start.8) | collective-permute-done | bytes 327712 | tf_op jit(solution)/shard_map/ppermute | solution.py:152
  59.2 0.1 pad_maximum_fusion.1
  59.3 3.5 %collective-permute-start.12 = (bf16[192,2048]{1,0:T(8,128)(2,1)S(1)}, bf16[192,2048]{1,0:T(8,128)(2,1)}, u32[]{:S(2)}, u32[]{:S(2)}) collective-permute-start(bf16[192,2048]{1,0:T(8,128)(2,1)S(1)} %pad_maximum_fusion.1), channel_id=1, source_target_pairs={{0,1},{1,0},{2,3},{3,2},{4,5},{5,4},{6,7},{7,6},{8,9},{9,8},{10,11... | collective-permute-start | bytes 2359304 | tf_op jit(solution)/shard_map/ppermute | solution.py:152
  62.8 0.2 reduce-window_clone.1
  63.0 0.6 select_reduce_fusion
  63.6 1.2 collective-permute-done.12.refs_7_.refs_15_
  64.8 19.0 %shard_map.85 = (bf16[128,4096]{1,0:T(8,128)(2,1)}, bf16[3,128,2048]{2,1,0:T(8,128)(2,1)}, bf16[448,2048]{1,0:T(8,128)(2,1)}, bf16[64,2048]{1,0:T(8,128)(2,1)}) custom-call(s32[1]{0:T(128)} %bitcast.info, bf16[128,4096]{1,0:T(8,128)(2,1)} %bitcast.78, bf16[128,4096]{1,0:T(8,128)(2,1)} %bitcast.79, s32[1,128]{1,0:T(1,128)} %bitcast.81, ...), custom_call_target="tpu_custom_call" | custom-call | flops 4697620480 | bytes 12582912 | tf_op jit(solution)/shard_map/pallas_call | solution.py:109
  83.8 2.3 %collective-permute-start.13 = (bf16[448,2048]{1,0:T(8,128)(2,1)}, bf16[448,2048]{1,0:T(8,128)(2,1)S(1)}, u32[]{:S(2)}, u32[]{:S(2)}) collective-permute-start(bf16[448,2048]{1,0:T(8,128)(2,1)} %get-tuple-element.39), channel_id=1, source_target_pairs={{0,1},{1,0},{2,3},{3,2},{4,5},{5,4},{6,7},{7,6},{8,9},{9,8},{10,11... | collective-permute-start | bytes 5505032 | tf_op jit(solution)/shard_map/ppermute | solution.py:152
  86.1 3.6 %collective-permute-done.13 = bf16[448,2048]{1,0:T(8,128)(2,1)S(1)} collective-permute-done((bf16[448,2048]{1,0:T(8,128)(2,1)}, bf16[448,2048]{1,0:T(8,128)(2,1)S(1)}, u32[]{:S(2)}, u32[]{:S(2)}) %collective-permute-start.13) | collective-permute-done | bytes 1835040 | tf_op jit(solution)/shard_map/ppermute | solution.py:152
  89.7 1.1 add_convert_fusion.2
  90.9 0.1 slice.137
  91.0 0.2 copy-done.1
  91.2 0.6 add_convert_fusion
  91.8 0.9 slice_bitcast_fusion
  92.7 4.5 %collective-permute-start.14 = (bf16[80,2048]{1,0:T(8,128)(2,1)S(1)}, bf16[80,2048]{1,0:T(8,128)(2,1)S(1)}, u32[]{:S(2)}, u32[]{:S(2)}) collective-permute-start(bf16[80,2048]{1,0:T(8,128)(2,1)S(1)} %pad_maximum_fusion.4), channel_id=1, source_target_pairs={{0,6},{1,7},{2,0},{3,1},{4,2},{5,3},{6,4},{7,5},{8,14},{9,15},{10,... | collective-permute-start | bytes 983048 | tf_op jit(solution)/shard_map/ppermute | solution.py:152
  97.3 1.9 %collective-permute-start.15 = (bf16[80,2048]{1,0:T(8,128)(2,1)S(1)}, bf16[80,2048]{1,0:T(8,128)(2,1)}, u32[]{:S(2)}, u32[]{:S(2)}) collective-permute-start(bf16[80,2048]{1,0:T(8,128)(2,1)S(1)} %pad_maximum_fusion.5), channel_id=1, source_target_pairs={{0,2},{1,3},{2,4},{3,5},{4,6},{5,7},{6,0},{7,1},{8,10},{9,11},{10,... | collective-permute-start | bytes 983048 | tf_op jit(solution)/shard_map/ppermute | solution.py:152
  99.2 5.5 %collective-permute-start.16 = (bf16[16,2048]{1,0:T(8,128)(2,1)S(1)}, bf16[16,2048]{1,0:T(8,128)(2,1)S(1)}, u32[]{:S(2)}, u32[]{:S(2)}) collective-permute-start(bf16[16,2048]{1,0:T(8,128)(2,1)S(1)} %get-tuple-element.65), channel_id=1, source_target_pairs={{0,4},{1,5},{2,6},{3,7},{4,0},{5,1},{6,2},{7,3},{8,12},{9,13},{10,... | collective-permute-start | bytes 196616 | tf_op jit(solution)/shard_map/ppermute | solution.py:152
  104.7 1.3 collective-permute-start.21
  106.0 1.3 collective-permute-start.20
  107.3 3.9 %collective-permute-done.16 = bf16[16,2048]{1,0:T(8,128)(2,1)S(1)} collective-permute-done((bf16[16,2048]{1,0:T(8,128)(2,1)S(1)}, bf16[16,2048]{1,0:T(8,128)(2,1)S(1)}, u32[]{:S(2)}, u32[]{:S(2)}) %collective-permute-start.16) | collective-permute-done | bytes 65568 | tf_op jit(solution)/shard_map/ppermute | solution.py:152
  111.2 0.6 copy-done.9
  111.8 1.1 fusion
  112.9 10.6 %collective-permute-done.21 = bf16[64,2048]{1,0:T(8,128)(2,1)S(1)} collective-permute-done((bf16[64,2048]{1,0:T(8,128)(2,1)}, bf16[64,2048]{1,0:T(8,128)(2,1)S(1)}, u32[]{:S(2)}, u32[]{:S(2)}) %collective-permute-start.21) | collective-permute-done | bytes 262176 | tf_op jit(solution)/shard_map/ppermute | solution.py:152
  123.5 5.8 %collective-permute-done.20 = bf16[64,2048]{1,0:T(8,128)(2,1)S(1)} collective-permute-done((bf16[64,2048]{1,0:T(8,128)(2,1)}, bf16[64,2048]{1,0:T(8,128)(2,1)S(1)}, u32[]{:S(2)}, u32[]{:S(2)}) %collective-permute-start.20) | collective-permute-done | bytes 262176 | tf_op jit(solution)/shard_map/ppermute | solution.py:152
  129.3 1.3 collective-permute-start.22
  130.5 4.9 %collective-permute-start.23 = (bf16[64,2048]{1,0:T(8,128)(2,1)S(1)}, bf16[64,2048]{1,0:T(8,128)(2,1)}, u32[]{:S(2)}, u32[]{:S(2)}) collective-permute-start(bf16[64,2048]{1,0:T(8,128)(2,1)S(1)} %get-tuple-element.45), channel_id=1, source_target_pairs={{6,0},{7,1},{0,2},{1,3},{14,8},{15,9},{8,10},{9,11},{22,16},{23,17... | collective-permute-start | bytes 786440 | tf_op jit(solution)/shard_map/ppermute | solution.py:152
  135.4 0.9 select_bitcast_fusion.1
  136.4 4.9 %collective-permute-start.17 = (bf16[2,16,2048]{2,1,0:T(8,128)(2,1)S(1)}, bf16[2,16,2048]{2,1,0:T(8,128)(2,1)S(1)}, u32[]{:S(2)}, u32[]{:S(2)}) collective-permute-start(bf16[2,16,2048]{2,1,0:T(8,128)(2,1)S(1)} %pad_maximum_fusion.6), channel_id=1, source_target_pairs={{0,496},{8,504},{16,0},{24,8},{32,16},{40,24},{48,32},{56,40},{64,... | collective-permute-start | bytes 393224 | tf_op jit(solution)/shard_map/ppermute | solution.py:19
  141.3 0.7 pad_maximum_fusion.7
  142.0 2.5 %collective-permute-start.18 = (bf16[2,16,2048]{2,1,0:T(8,128)(2,1)}, bf16[2,16,2048]{2,1,0:T(8,128)(2,1)S(1)}, u32[]{:S(2)}, u32[]{:S(2)}) collective-permute-start(bf16[2,16,2048]{2,1,0:T(8,128)(2,1)} %pad_maximum_fusion.7), channel_id=1, source_target_pairs={{0,480},{8,488},{16,496},{24,504},{32,0},{40,8},{48,16},{56,24},{6... | collective-permute-start | bytes 393224 | tf_op jit(solution)/shard_map/ppermute | solution.py:19
  144.5 0.7 pad_maximum_fusion.8
  145.1 2.6 %collective-permute-start.19 = (bf16[2,16,2048]{2,1,0:T(8,128)(2,1)}, bf16[2,16,2048]{2,1,0:T(8,128)(2,1)S(1)}, u32[]{:S(2)}, u32[]{:S(2)}) collective-permute-start(bf16[2,16,2048]{2,1,0:T(8,128)(2,1)} %pad_maximum_fusion.8), channel_id=1, source_target_pairs={{0,464},{8,472},{16,480},{24,488},{32,496},{40,504},{48,0},{56,8},... | collective-permute-start | bytes 393224 | tf_op jit(solution)/shard_map/ppermute | solution.py:19
  147.8 1.6 collective-permute-done.18
  149.4 3.5 %collective-permute-done.19 = bf16[2,16,2048]{2,1,0:T(8,128)(2,1)S(1)} collective-permute-done((bf16[2,16,2048]{2,1,0:T(8,128)(2,1)}, bf16[2,16,2048]{2,1,0:T(8,128)(2,1)S(1)}, u32[]{:S(2)}, u32[]{:S(2)}) %collective-permute-start.19) | collective-permute-done | bytes 131104 | tf_op jit(solution)/shard_map/ppermute | solution.py:19
  152.9 3.9 %collective-permute-start.24 = (bf16[16,2048]{1,0:T(8,128)(2,1)S(1)}, bf16[16,2048]{1,0:T(8,128)(2,1)S(1)}, u32[]{:S(2)}, u32[]{:S(2)}) collective-permute-start(bf16[16,2048]{1,0:T(8,128)(2,1)S(1)} %fusion.3), channel_id=1, source_target_pairs={{0,504},{8,0},{16,8},{24,16},{32,24},{40,32},{48,40},{56,48},{64,5... | collective-permute-start | bytes 196616 | tf_op jit(solution)/shard_map/ppermute | solution.py:19
  156.9 2.1 %add_convert_fusion.1 = bf16[1,128,2048]{2,1,0:T(8,128)(2,1)} fusion(bf16[4,128,2048]{2,1,0:T(8,128)(2,1)S(1)} %add_convert_fusion, bf16[1,64,2048]{2,1,0:T(8,128)(2,1)} %bitcast.76, bf16[1,64,2048]{2,1,0:T(8,128)(2,1)S(1)} %bitcast.77, bf16[1,64,2048]{2,1,0:T(8,128)(2,1)} %bitcast.27, bf16[1,64,2048]{2,1,0:T(8,128)(2,1)} %bitcast.75), kind=kLoop, calls=%fused_computation.2 | loop fusion | flops 3145728 | bytes 2097152 | tf_op jit(solution)/shard_map/convert_element_type | solution.py:148
  159.0 2.3 %collective-permute-done.24 = bf16[16,2048]{1,0:T(8,128)(2,1)S(1)} collective-permute-done((bf16[16,2048]{1,0:T(8,128)(2,1)S(1)}, bf16[16,2048]{1,0:T(8,128)(2,1)S(1)}, u32[]{:S(2)}, u32[]{:S(2)}) %collective-permute-start.24) | collective-permute-done | bytes 65568 | tf_op jit(solution)/shard_map/ppermute | solution.py:19
  161.4 0.7 fusion.4
  (42 shorter events, 0.3 us)
Async XLA Ops:
  0.6 18.0 %collective-permute-start = (bf16[1,16,2048]{2,1,0:T(8,128)(2,1)}, bf16[1,16,2048]{2,1,0:T(8,128)(2,1)S(1)}, u32[]{:S(2)}, u32[]{:S(2)}) collective-permute-start(bf16[1,16,2048]{2,1,0:T(8,128)(2,1)} %param.8), channel_id=1, source_target_pairs={{0,8},{8,16},{16,24},{24,32},{32,40},{40,48},{48,56},{56,64},{64,7... | collective-permute-start | bytes 196616 | tf_op jit(solution)/shard_map/ppermute | solution.py:19
  6.5 39.1 %copy-start = (bf16[1,128,2048]{2,1,0:T(8,128)(2,1)S(1)}, bf16[1,128,2048]{2,1,0:T(8,128)(2,1)}, u32[]{:S(2)}) copy-start(bf16[1,128,2048]{2,1,0:T(8,128)(2,1)} %param.7) | copy-start | bytes 1572868
  6.6 23.1 %collective-permute-start.4 = (bf16[64,2048]{1,0:T(8,128)(2,1)S(1)}, bf16[64,2048]{1,0:T(8,128)(2,1)S(1)}, u32[]{:S(2)}, u32[]{:S(2)}) collective-permute-start(bf16[64,2048]{1,0:T(8,128)(2,1)S(1)} %get-tuple-element.36), channel_id=1, source_target_pairs={{0,2},{1,3},{2,4},{3,5},{4,6},{5,7},{8,10},{9,11},{10,12},{11,13},... | collective-permute-start | bytes 786440 | tf_op jit(solution)/shard_map/ppermute | solution.py:152
  12.5 19.4 %collective-permute-start.5 = (bf16[64,2048]{1,0:T(8,128)(2,1)S(1)}, bf16[64,2048]{1,0:T(8,128)(2,1)S(1)}, u32[]{:S(2)}, u32[]{:S(2)}) collective-permute-start(bf16[64,2048]{1,0:T(8,128)(2,1)S(1)} %get-tuple-element.35), channel_id=1, source_target_pairs={{0,6},{1,7},{2,0},{3,1},{8,14},{9,15},{10,8},{11,9},{16,22},{17,23... | collective-permute-start | bytes 786440 | tf_op jit(solution)/shard_map/ppermute | solution.py:152
  18.6 15.9 %collective-permute-start.3 = (bf16[2,16,2048]{2,1,0:T(8,128)(2,1)S(1)}, bf16[2,16,2048]{2,1,0:T(8,128)(2,1)S(1)}, u32[]{:S(2)}, u32[]{:S(2)}) collective-permute-start(bf16[2,16,2048]{2,1,0:T(8,128)(2,1)S(1)} %get-tuple-element.75), channel_id=1, source_target_pairs={{0,48},{8,56},{16,64},{24,72},{32,80},{40,88},{48,96},{56,104},{64... | collective-permute-start | bytes 393224 | tf_op jit(solution)/shard_map/ppermute | solution.py:19
  23.0 11.5 %collective-permute-start.2 = (bf16[2,16,2048]{2,1,0:T(8,128)(2,1)S(1)}, bf16[2,16,2048]{2,1,0:T(8,128)(2,1)S(1)}, u32[]{:S(2)}, u32[]{:S(2)}) collective-permute-start(bf16[2,16,2048]{2,1,0:T(8,128)(2,1)S(1)} %get-tuple-element.75), channel_id=1, source_target_pairs={{0,32},{8,40},{16,48},{24,56},{32,64},{40,72},{48,80},{56,88},{64,... | collective-permute-start | bytes 393224 | tf_op jit(solution)/shard_map/ppermute | solution.py:19
  26.5 9.4 %collective-permute-start.1 = (bf16[2,16,2048]{2,1,0:T(8,128)(2,1)S(1)}, bf16[2,16,2048]{2,1,0:T(8,128)(2,1)S(1)}, u32[]{:S(2)}, u32[]{:S(2)}) collective-permute-start(bf16[2,16,2048]{2,1,0:T(8,128)(2,1)S(1)} %get-tuple-element.75), channel_id=1, source_target_pairs={{0,16},{8,24},{16,32},{24,40},{32,48},{40,56},{48,64},{56,72},{64,... | collective-permute-start | bytes 393224 | tf_op jit(solution)/shard_map/ppermute | solution.py:19
  29.7 15.9 %collective-permute-start.9 = (bf16[64,2048]{1,0:T(8,128)(2,1)S(1)}, bf16[64,2048]{1,0:T(8,128)(2,1)S(1)}, u32[]{:S(2)}, u32[]{:S(2)}) collective-permute-start(bf16[64,2048]{1,0:T(8,128)(2,1)S(1)} %get-tuple-element.35), channel_id=1, source_target_pairs={{0,2},{1,3},{2,4},{3,5},{4,6},{5,7},{8,10},{9,11},{10,12},{11,13},... | collective-permute-start | bytes 786440 | tf_op jit(solution)/shard_map/ppermute | solution.py:152
  31.9 13.7 %collective-permute-start.10 = (bf16[64,2048]{1,0:T(8,128)(2,1)S(1)}, bf16[64,2048]{1,0:T(8,128)(2,1)S(1)}, u32[]{:S(2)}, u32[]{:S(2)}) collective-permute-start(bf16[64,2048]{1,0:T(8,128)(2,1)S(1)} %get-tuple-element.36), channel_id=1, source_target_pairs={{1,7},{9,15},{17,23},{25,31},{33,39},{41,47},{49,55},{57,63},{65,7... | collective-permute-start | bytes 786440 | tf_op jit(solution)/shard_map/ppermute | solution.py:152
  35.9 23.3 %copy-start.3 = (bf16[16,2048]{1,0:T(8,128)(2,1)}, bf16[16,2048]{1,0:T(8,128)(2,1)S(1)}, u32[]{:S(2)}) copy-start(bf16[16,2048]{1,0:T(8,128)(2,1)S(1)} %dynamic-slice_bitcast_fusion.refs_0_.refs_8_) | copy-start | bytes 196612
  35.9 15.9 %collective-permute-start.6 = (bf16[16,2048]{1,0:T(8,128)(2,1)S(1)}, bf16[16,2048]{1,0:T(8,128)(2,1)S(1)}, u32[]{:S(2)}, u32[]{:S(2)}) collective-permute-start(bf16[16,2048]{1,0:T(8,128)(2,1)S(1)} %dynamic-slice_bitcast_fusion.refs_0_.refs_8_), channel_id=1, source_target_pairs={{0,4},{1,5},{2,6},{3,7},{4,0},{5,1},{6,2},{7,3},{8,12},{9,13},{10,... | collective-permute-start | bytes 196616 | tf_op jit(solution)/shard_map/ppermute | solution.py:152
  39.4 19.8 %collective-permute-start.8 = (bf16[80,2048]{1,0:T(8,128)(2,1)S(1)}, bf16[80,2048]{1,0:T(8,128)(2,1)S(1)}, u32[]{:S(2)}, u32[]{:S(2)}) collective-permute-start(bf16[80,2048]{1,0:T(8,128)(2,1)S(1)} %get-tuple-element.73), channel_id=1, source_target_pairs={{0,6},{1,7},{2,0},{3,1},{4,2},{5,3},{6,4},{7,5},{8,14},{9,15},{10,... | collective-permute-start | bytes 983048 | tf_op jit(solution)/shard_map/ppermute | solution.py:152
  43.4 15.8 %collective-permute-start.7 = (bf16[80,2048]{1,0:T(8,128)(2,1)S(1)}, bf16[80,2048]{1,0:T(8,128)(2,1)S(1)}, u32[]{:S(2)}, u32[]{:S(2)}) collective-permute-start(bf16[80,2048]{1,0:T(8,128)(2,1)S(1)} %get-tuple-element.74), channel_id=1, source_target_pairs={{0,2},{1,3},{2,4},{3,5},{4,6},{5,7},{6,0},{7,1},{8,10},{9,11},{10,... | collective-permute-start | bytes 983048 | tf_op jit(solution)/shard_map/ppermute | solution.py:152
  45.6 0.8 copy-start.2
  46.0 16.8 %copy-start.10 = (s32[1,3]{1,0:T(1,128)S(1)}, s32[1,3]{1,0:T(1,128)}, u32[]{:S(2)}) copy-start(s32[1,3]{1,0:T(1,128)} %param.10) | copy-start | bytes 40
  46.4 18.4 %collective-permute-start.11 = (bf16[256,2048]{1,0:T(8,128)(2,1)S(1)}, bf16[256,2048]{1,0:T(8,128)(2,1)}, u32[]{:S(2)}, u32[]{:S(2)}) collective-permute-start(bf16[256,2048]{1,0:T(8,128)(2,1)S(1)} %pad_maximum_fusion), channel_id=1, source_target_pairs={{0,1},{1,0},{2,3},{3,2},{4,5},{5,4},{6,7},{7,6},{8,9},{9,8},{10,11... | collective-permute-start | bytes 3145736 | tf_op jit(solution)/shard_map/ppermute | solution.py:152
  51.8 13.0 %copy-start.8 = (bf16[16,2048]{1,0:T(8,128)(2,1)}, bf16[16,2048]{1,0:T(8,128)(2,1)S(1)}, u32[]{:S(2)}) copy-start(bf16[16,2048]{1,0:T(8,128)(2,1)S(1)} %collective-permute-done.6.refs_1_.refs_9_) | copy-start | bytes 196612
  59.2 5.7 %copy-start.4 = (bf16[80,2048]{1,0:T(8,128)(2,1)}, bf16[80,2048]{1,0:T(8,128)(2,1)S(1)}, u32[]{:S(2)}) copy-start(bf16[80,2048]{1,0:T(8,128)(2,1)S(1)} %collective-permute-done.8.refs_3_.refs_11_) | copy-start | bytes 983044
  59.2 5.7 %copy-start.5 = (bf16[80,2048]{1,0:T(8,128)(2,1)}, bf16[80,2048]{1,0:T(8,128)(2,1)S(1)}, u32[]{:S(2)}) copy-start(bf16[80,2048]{1,0:T(8,128)(2,1)S(1)} %collective-permute-done.7.refs_2_.refs_10_) | copy-start | bytes 983044
  59.3 5.6 %collective-permute-start.12 = (bf16[192,2048]{1,0:T(8,128)(2,1)S(1)}, bf16[192,2048]{1,0:T(8,128)(2,1)}, u32[]{:S(2)}, u32[]{:S(2)}) collective-permute-start(bf16[192,2048]{1,0:T(8,128)(2,1)S(1)} %pad_maximum_fusion.1), channel_id=1, source_target_pairs={{0,1},{1,0},{2,3},{3,2},{4,5},{5,4},{6,7},{7,6},{8,9},{9,8},{10,11... | collective-permute-start | bytes 2359304 | tf_op jit(solution)/shard_map/ppermute | solution.py:152
  83.8 5.9 %collective-permute-start.13 = (bf16[448,2048]{1,0:T(8,128)(2,1)}, bf16[448,2048]{1,0:T(8,128)(2,1)S(1)}, u32[]{:S(2)}, u32[]{:S(2)}) collective-permute-start(bf16[448,2048]{1,0:T(8,128)(2,1)} %get-tuple-element.39), channel_id=1, source_target_pairs={{0,1},{1,0},{2,3},{3,2},{4,5},{5,4},{6,7},{7,6},{8,9},{9,8},{10,11... | collective-permute-start | bytes 5505032 | tf_op jit(solution)/shard_map/ppermute | solution.py:152
  89.7 1.5 copy-start.1
  92.7 18.4 %collective-permute-start.14 = (bf16[80,2048]{1,0:T(8,128)(2,1)S(1)}, bf16[80,2048]{1,0:T(8,128)(2,1)S(1)}, u32[]{:S(2)}, u32[]{:S(2)}) collective-permute-start(bf16[80,2048]{1,0:T(8,128)(2,1)S(1)} %pad_maximum_fusion.4), channel_id=1, source_target_pairs={{0,6},{1,7},{2,0},{3,1},{4,2},{5,3},{6,4},{7,5},{8,14},{9,15},{10,... | collective-permute-start | bytes 983048 | tf_op jit(solution)/shard_map/ppermute | solution.py:152
  97.3 14.5 %collective-permute-start.15 = (bf16[80,2048]{1,0:T(8,128)(2,1)S(1)}, bf16[80,2048]{1,0:T(8,128)(2,1)}, u32[]{:S(2)}, u32[]{:S(2)}) collective-permute-start(bf16[80,2048]{1,0:T(8,128)(2,1)S(1)} %pad_maximum_fusion.5), channel_id=1, source_target_pairs={{0,2},{1,3},{2,4},{3,5},{4,6},{5,7},{6,0},{7,1},{8,10},{9,11},{10,... | collective-permute-start | bytes 983048 | tf_op jit(solution)/shard_map/ppermute | solution.py:152
  99.2 12.0 %collective-permute-start.16 = (bf16[16,2048]{1,0:T(8,128)(2,1)S(1)}, bf16[16,2048]{1,0:T(8,128)(2,1)S(1)}, u32[]{:S(2)}, u32[]{:S(2)}) collective-permute-start(bf16[16,2048]{1,0:T(8,128)(2,1)S(1)} %get-tuple-element.65), channel_id=1, source_target_pairs={{0,4},{1,5},{2,6},{3,7},{4,0},{5,1},{6,2},{7,3},{8,12},{9,13},{10,... | collective-permute-start | bytes 196616 | tf_op jit(solution)/shard_map/ppermute | solution.py:152
  104.7 18.8 %collective-permute-start.21 = (bf16[64,2048]{1,0:T(8,128)(2,1)}, bf16[64,2048]{1,0:T(8,128)(2,1)S(1)}, u32[]{:S(2)}, u32[]{:S(2)}) collective-permute-start(bf16[64,2048]{1,0:T(8,128)(2,1)} %get-tuple-element.55), channel_id=1, source_target_pairs={{7,1},{15,9},{23,17},{31,25},{39,33},{47,41},{55,49},{63,57},{71,6... | collective-permute-start | bytes 786440 | tf_op jit(solution)/shard_map/ppermute | solution.py:152
  106.0 23.3 %collective-permute-start.20 = (bf16[64,2048]{1,0:T(8,128)(2,1)}, bf16[64,2048]{1,0:T(8,128)(2,1)S(1)}, u32[]{:S(2)}, u32[]{:S(2)}) collective-permute-start(bf16[64,2048]{1,0:T(8,128)(2,1)} %get-tuple-element.56), channel_id=1, source_target_pairs={{2,0},{3,1},{4,2},{5,3},{6,4},{7,5},{10,8},{11,9},{12,10},{13,11},... | collective-permute-start | bytes 786440 | tf_op jit(solution)/shard_map/ppermute | solution.py:152
  111.2 0.6 copy-start.9
  123.5 21.7 %copy-start.6 = (bf16[64,2048]{1,0:T(8,128)(2,1)}, bf16[64,2048]{1,0:T(8,128)(2,1)S(1)}, u32[]{:S(2)}) copy-start(bf16[64,2048]{1,0:T(8,128)(2,1)S(1)} %collective-permute-done.21) | copy-start | bytes 786436
  129.3 15.9 %copy-start.7 = (bf16[64,2048]{1,0:T(8,128)(2,1)}, bf16[64,2048]{1,0:T(8,128)(2,1)S(1)}, u32[]{:S(2)}) copy-start(bf16[64,2048]{1,0:T(8,128)(2,1)S(1)} %collective-permute-done.20) | copy-start | bytes 786436
  129.3 23.6 %collective-permute-start.22 = (bf16[64,2048]{1,0:T(8,128)(2,1)S(1)}, bf16[64,2048]{1,0:T(8,128)(2,1)S(1)}, u32[]{:S(2)}, u32[]{:S(2)}) collective-permute-start(bf16[64,2048]{1,0:T(8,128)(2,1)S(1)} %get-tuple-element.44), channel_id=1, source_target_pairs={{2,0},{3,1},{4,2},{5,3},{6,4},{7,5},{10,8},{11,9},{12,10},{13,11},... | collective-permute-start | bytes 786440 | tf_op jit(solution)/shard_map/ppermute | solution.py:152
  130.5 22.4 %collective-permute-start.23 = (bf16[64,2048]{1,0:T(8,128)(2,1)S(1)}, bf16[64,2048]{1,0:T(8,128)(2,1)}, u32[]{:S(2)}, u32[]{:S(2)}) collective-permute-start(bf16[64,2048]{1,0:T(8,128)(2,1)S(1)} %get-tuple-element.45), channel_id=1, source_target_pairs={{6,0},{7,1},{0,2},{1,3},{14,8},{15,9},{8,10},{9,11},{22,16},{23,17... | collective-permute-start | bytes 786440 | tf_op jit(solution)/shard_map/ppermute | solution.py:152
  136.4 11.3 %collective-permute-start.17 = (bf16[2,16,2048]{2,1,0:T(8,128)(2,1)S(1)}, bf16[2,16,2048]{2,1,0:T(8,128)(2,1)S(1)}, u32[]{:S(2)}, u32[]{:S(2)}) collective-permute-start(bf16[2,16,2048]{2,1,0:T(8,128)(2,1)S(1)} %pad_maximum_fusion.6), channel_id=1, source_target_pairs={{0,496},{8,504},{16,0},{24,8},{32,16},{40,24},{48,32},{56,40},{64,... | collective-permute-start | bytes 393224 | tf_op jit(solution)/shard_map/ppermute | solution.py:19
  142.0 7.4 %collective-permute-start.18 = (bf16[2,16,2048]{2,1,0:T(8,128)(2,1)}, bf16[2,16,2048]{2,1,0:T(8,128)(2,1)S(1)}, u32[]{:S(2)}, u32[]{:S(2)}) collective-permute-start(bf16[2,16,2048]{2,1,0:T(8,128)(2,1)} %pad_maximum_fusion.7), channel_id=1, source_target_pairs={{0,480},{8,488},{16,496},{24,504},{32,0},{40,8},{48,16},{56,24},{6... | collective-permute-start | bytes 393224 | tf_op jit(solution)/shard_map/ppermute | solution.py:19
  145.1 7.8 %collective-permute-start.19 = (bf16[2,16,2048]{2,1,0:T(8,128)(2,1)}, bf16[2,16,2048]{2,1,0:T(8,128)(2,1)S(1)}, u32[]{:S(2)}, u32[]{:S(2)}) collective-permute-start(bf16[2,16,2048]{2,1,0:T(8,128)(2,1)} %pad_maximum_fusion.8), channel_id=1, source_target_pairs={{0,464},{8,472},{16,480},{24,488},{32,496},{40,504},{48,0},{56,8},... | collective-permute-start | bytes 393224 | tf_op jit(solution)/shard_map/ppermute | solution.py:19
  152.9 8.4 %collective-permute-start.24 = (bf16[16,2048]{1,0:T(8,128)(2,1)S(1)}, bf16[16,2048]{1,0:T(8,128)(2,1)S(1)}, u32[]{:S(2)}, u32[]{:S(2)}) collective-permute-start(bf16[16,2048]{1,0:T(8,128)(2,1)S(1)} %fusion.3), channel_id=1, source_target_pairs={{0,504},{8,0},{16,8},{24,16},{32,24},{40,32},{48,40},{56,48},{64,5... | collective-permute-start | bytes 196616 | tf_op jit(solution)/shard_map/ppermute | solution.py:19

commit v6 on v5

--- a/solution.py
+++ b/solution.py
@@ -11,6 +11,7 @@
 HD = 128
 SPREAD = 8
 NEG = -1e30
+UNIT = 2
 LOG2E = 1.4426950408889634
 
 
@@ -28,7 +29,7 @@
     key_refs, value_refs = refs[:8], refs[8:16]
     dq_ref, keep_ref, give_ref, pkeep_ref, bias = refs[16:]
     rows = q_ref.shape[0]
-    heads = q_ref.shape[1] // HD
+    heads = q_ref.shape[1] // HD // UNIT
     slot = key_refs[0].shape[0]
     plen = slot * n_seq
     odd = lax.rem(info[0], 2) == 1
@@ -46,77 +47,81 @@
         seen = (k_ids >= start_ref[...]) & (k_ids <= q_ids)
         bias[...] = jnp.where(seen, 0.0, NEG)
 
-    def laid_out(refs):
-        mine, across, last, next_, own, two, got_near, got_far = [ref[...] for ref in refs]
-        cut = rows // 2
-        far = cut + slot
-        four = [last[:cut], next_[:cut]]
-        other4 = jnp.concatenate([got_far[:cut], got_far[far : far + cut]], axis=0)
-        other3 = got_near[rows:]
-        blocks = [mine, last[cut:], across, next_[cut:]]
-        blocks += [got_far[2 * far : 2 * far + slot], got_far[cut:far]]
-        blocks += [got_far[2 * far + slot :], got_far[far + cut : 2 * far]]
-        blocks += [jnp.where(odd, other4, other3), *four, jnp.where(odd, other3, other4)]
-        blocks += [two, got_near[:rows], own]
-        return jnp.concatenate(blocks, axis=0)
-
-    keys = laid_out(key_refs)
-    values = laid_out(value_refs)
-    q_rows = stacked(q_ref[...])
-    g_rows = stacked(g_ref[...])
-    nt = (((1,), (1,)), ((), ()))
-    nn = (((1,), (0,)), ((), ()))
-    tn = (((0,), (0,)), ((), ()))
-    scores = lax.dot_general(keys, q_rows, nt, preferred_element_type=jnp.float32)
-    shade = jnp.concatenate([bias[...]] * heads, axis=1)
-    scores = jnp.concatenate([scores[:plen], scores[plen:] + shade], axis=0)
-    top = jnp.max(scores, axis=0, keepdims=True)
-    expo = jnp.exp2((scores - top) * (scale * LOG2E))
-    weights = expo * (1.0 / jnp.sum(expo, axis=0, keepdims=True))
-    d_weights = lax.dot_general(values, g_rows, nt, preferred_element_type=jnp.float32)
-    delta = jnp.sum(weights * d_weights, axis=0, keepdims=True)
-    d_scores = (weights * (d_weights - delta)).astype(jnp.bfloat16)
-    weights_b = weights.astype(jnp.bfloat16)
-    d_value = lax.dot_general(weights_b, g_rows, nn, preferred_element_type=jnp.float32)
-    d_key = lax.dot_general(d_scores, q_rows, nn, preferred_element_type=jnp.float32) * scale
-    d_query = lax.dot_general(d_scores, keys, tn, preferred_element_type=jnp.float32) * scale
-    d_query = d_query.astype(jnp.bfloat16)
-    for h in range(heads):
-        dq_ref[:, h * HD : (h + 1) * HD] = d_query[h * rows : (h + 1) * rows]
-    given = (span + 1) // 2 * rows
-    for part, base in ((d_key, 0), (d_value, half)):
-        part = part.astype(jnp.bfloat16)
-        columns = pl.ds(pl.multiple_of(base + head * HD, HD), HD)
-        for back in range(span + 1):
-            block = part[plen + (span - back) * rows : plen + (span - back + 1) * rows]
-            if back % 2 == 0:
-                keep_ref[back // 2, :, columns] = block
-            else:
-                give_ref[back // 2 * rows : (back // 2 + 1) * rows, columns] = block
-        pkeep_ref[:, columns] = part[: plen // 2]
-        give_ref[given:, columns] = part[plen // 2 : plen]
+    def one(u):
+        def laid_out(refs):
+            mine, across, last, next_, own, two, got_near, got_far = [ref[:, u * HD : (u + 1) * HD] for ref in refs]
+            cut = rows // 2
+            far = cut + slot
+            four = [last[:cut], next_[:cut]]
+            other4 = jnp.concatenate([got_far[:cut], got_far[far : far + cut]], axis=0)
+            other3 = got_near[rows:]
+            blocks = [mine, last[cut:], across, next_[cut:]]
+            blocks += [got_far[2 * far : 2 * far + slot], got_far[cut:far]]
+            blocks += [got_far[2 * far + slot :], got_far[far + cut : 2 * far]]
+            blocks += [jnp.where(odd, other4, other3), *four, jnp.where(odd, other3, other4)]
+            blocks += [two, got_near[:rows], own]
+            return jnp.concatenate(blocks, axis=0)
+
+        keys = laid_out(key_refs)
+        values = laid_out(value_refs)
+        q_rows = stacked(q_ref[:, u * heads * HD : (u + 1) * heads * HD])
+        g_rows = stacked(g_ref[:, u * heads * HD : (u + 1) * heads * HD])
+        nt = (((1,), (1,)), ((), ()))
+        nn = (((1,), (0,)), ((), ()))
+        tn = (((0,), (0,)), ((), ()))
+        scores = lax.dot_general(keys, q_rows, nt, preferred_element_type=jnp.float32)
+        shade = jnp.concatenate([bias[...]] * heads, axis=1)
+        scores = jnp.concatenate([scores[:plen], scores[plen:] + shade], axis=0)
+        top = jnp.max(scores, axis=0, keepdims=True)
+        expo = jnp.exp2((scores - top) * (scale * LOG2E))
+        weights = expo * (1.0 / jnp.sum(expo, axis=0, keepdims=True))
+        d_weights = lax.dot_general(values, g_rows, nt, preferred_element_type=jnp.float32)
+        delta = jnp.sum(weights * d_weights, axis=0, keepdims=True)
+        d_scores = (weights * (d_weights - delta)).astype(jnp.bfloat16)
+        weights_b = weights.astype(jnp.bfloat16)
+        d_value = lax.dot_general(weights_b, g_rows, nn, preferred_element_type=jnp.float32)
+        d_key = lax.dot_general(d_scores, q_rows, nn, preferred_element_type=jnp.float32) * scale
+        d_query = lax.dot_general(d_scores, keys, tn, preferred_element_type=jnp.float32) * scale
+        d_query = d_query.astype(jnp.bfloat16)
+        for h in range(heads):
+            dq_ref[:, (u * heads + h) * HD : (u * heads + h + 1) * HD] = d_query[h * rows : (h + 1) * rows]
+        given = (span + 1) // 2 * rows
+        for part, base in ((d_key, 0), (d_value, half)):
+            part = part.astype(jnp.bfloat16)
+            columns = pl.ds(pl.multiple_of(base + (head * UNIT + u) * HD, HD), HD)
+            for back in range(span + 1):
+                block = part[plen + (span - back) * rows : plen + (span - back + 1) * rows]
+                if back % 2 == 0:
+                    keep_ref[back // 2, :, columns] = block
+                else:
+                    give_ref[back // 2 * rows : (back // 2 + 1) * rows, columns] = block
+            pkeep_ref[:, columns] = part[: plen // 2]
+            give_ref[given:, columns] = part[plen // 2 : plen]
+
+    for u in range(UNIT):
+        one(u)
 
 
 def attend(q_rows, grad_rows, kv, q_start, me, span, n_seq):
     rows, columns = q_rows.shape
     plen, width = n_seq * kv[0].shape[0], kv[0].shape[1]
-    group = columns // KVH
+    group = columns // KVH * UNIT
     bf16 = jnp.bfloat16
     at = lambda n, col: pl.BlockSpec((n, col), lambda g, s: (0, g))
-    later = lambda n: pl.BlockSpec((n, HD), lambda g, s: (0, KVH + g))
+    later = lambda n: pl.BlockSpec((n, UNIT * HD), lambda g, s: (0, KVH // UNIT + g))
     pairs = (span + 1) * rows + plen
     kept, given = span // 2 + 1, (span + 1) // 2
     return pl.pallas_call(
         functools.partial(attention_kernel, span, n_seq),
         grid_spec=pltpu.PrefetchScalarGridSpec(
             num_scalar_prefetch=1,
-            grid=(KVH,),
+            grid=(KVH // UNIT,),
             in_specs=[
                 at(rows, group),
                 at(rows, group),
                 pl.BlockSpec((1, rows), lambda g, s: (0, 0)),
             ]
-            + [at(x.shape[0], HD) for x in kv]
+            + [at(x.shape[0], UNIT * HD) for x in kv]
             + [later(x.shape[0]) for x in kv],
             out_specs=[
                 at(rows, group),
@@ -222,11 +227,9 @@
     passing = (me >= n - 2) | (me < 2)
     top_one = added(one[:cut], from_next[:cut])
     low_three = added(three[cut:], jnp.where(passing, from_last[:cut], none))
-    top_one, low_three, low1, top3 = tied((top_one, low_three, low1, top3))
-    pairs = [
-        passed_along(jnp.stack(left[step : step + 2]), "dp", -step)
-        for step in range(2, SPREAD, 2)
-    ]
+    stacks = [jnp.stack(left[step : step + 2]) for step in range(2, SPREAD, 2)]
+    pairs = [passed_along(x, "dp", -step) for x, step in zip(stacks, range(2, SPREAD, 2))]
+    top_one, low_three, low1, top3, pairs[0] = tied((top_one, low_three, low1, top3, pairs[0]))
     top1 = along_seq(top_one, [(i, i - 2) for i in range(2, n)])
     low3 = along_seq(low_three, [(i, (i + 2) % n) for i in (n - 2, n - 1, 0, 1)])
     *pairs, top1, low3 = tied((*pairs, top1, low3))

time: 163 us -> 163 us (level); the launches traced: 162 us -> 160 us
  waiting for transfers between devices: 41.1 us -> 19.7 us
  starting transfers between devices: 86.5 us -> 106 us
    ppermute x8, starting transfers between devices: 29.1 us -> 48.2 us  [passed_along(): lax.ppermute(value, axis, [(i, (i + by) % peers) for i in range(peers)])]
    ppermute x17, waiting for transfers between devices: 32.4 us -> 16.1 us  [along_seq(): return lax.ppermute(value, 'seq', pairs)]
    ppermute x8, waiting for transfers between devices: 8.72 us -> 3.64 us  [passed_along(): lax.ppermute(value, axis, [(i, (i + by) % peers) for i in range(peers)])]
  transfers between devices with their start and end apart: 25 -> 25, of which waited for: 10 -> 6; matrix products, arithmetic and copies ran while one was open for 5% -> 5% of each run, Pallas kernels for 0% -> 0%
where the time goes in v6:
time: 163 us; the launch traced here: 160 us
  starting transfers between devices  106 us (65%)
  waiting for transfers between devices  19.7 us (12%)
  Pallas kernels  17.6 us (11%)
  other arithmetic  11 us (7%)
  local copies, waits for them, and re-layouts  3.63 us (2%)
  between operations  1.9 us (1%)
    ppermute x17, starting transfers between devices, along_seq(): return lax.ppermute(value, 'seq', pairs)  58 us
    ppermute x8, starting transfers between devices, passed_along(): lax.ppermute(value, axis, [(i, (i + by) % peers) for i in range(peers)])  48.2 us
    pallas_call x1, Pallas kernels, attend(): pl.pallas_call(functools.partial(attention_kernel, span, n_seq), grid_spe...  17.6 us
    ppermute x17, waiting for transfers between devices, along_seq(): return lax.ppermute(value, 'seq', pairs)  16.1 us
    convert_element_type x5, other arithmetic, added(): return total.astype(jnp.bfloat16)  5.84 us
    ppermute x8, waiting for transfers between devices, passed_along(): lax.ppermute(value, axis, [(i, (i + by) % peers) for i in range(peers)])  3.64 us
  transfers between devices with their start and end apart: 25, of which 6 were waited for; matrix products, arithmetic and copies ran while one was open for 5% of the time, Pallas kernels for 0%

profile of v6, /device:TPU:1, one launch (start us, length us, event | category | flops | bytes accessed | tf_op | source)
XLA Modules:
  0.0 159.9 jit_solution(2275584147672293103)
XLA Ops:
  0.6 4.8 %collective-permute-start = (bf16[1,16,2048]{2,1,0:T(8,128)(2,1)}, bf16[1,16,2048]{2,1,0:T(8,128)(2,1)S(1)}, u32[]{:S(2)}, u32[]{:S(2)}) collective-permute-start(bf16[1,16,2048]{2,1,0:T(8,128)(2,1)} %param.8), channel_id=1, source_target_pairs={{0,8},{8,16},{16,24},{24,32},{32,40},{40,48},{48,56},{56,64},{64,7... | collective-permute-start | bytes 196616 | tf_op jit(solution)/shard_map/ppermute | solution.py:20
  5.5 1.1 slice_bitcast_fusion.6
  6.5 0.0 copy-start
  6.6 6.0 %collective-permute-start.4 = (bf16[64,2048]{1,0:T(8,128)(2,1)S(1)}, bf16[64,2048]{1,0:T(8,128)(2,1)S(1)}, u32[]{:S(2)}, u32[]{:S(2)}) collective-permute-start(bf16[64,2048]{1,0:T(8,128)(2,1)S(1)} %get-tuple-element.37), channel_id=1, source_target_pairs={{0,2},{1,3},{2,4},{3,5},{4,6},{5,7},{8,10},{9,11},{10,12},{11,13},... | collective-permute-start | bytes 786440 | tf_op jit(solution)/shard_map/ppermute | solution.py:157
  12.5 5.2 %collective-permute-start.5 = (bf16[64,2048]{1,0:T(8,128)(2,1)S(1)}, bf16[64,2048]{1,0:T(8,128)(2,1)S(1)}, u32[]{:S(2)}, u32[]{:S(2)}) collective-permute-start(bf16[64,2048]{1,0:T(8,128)(2,1)S(1)} %get-tuple-element.36), channel_id=1, source_target_pairs={{0,6},{1,7},{2,0},{3,1},{8,14},{9,15},{10,8},{11,9},{16,22},{17,23... | collective-permute-start | bytes 786440 | tf_op jit(solution)/shard_map/ppermute | solution.py:157
  17.7 0.9 constant_dynamic-update-slice_fusion.1
  18.6 0.0 collective-permute-done
  18.6 4.4 %collective-permute-start.3 = (bf16[2,16,2048]{2,1,0:T(8,128)(2,1)S(1)}, bf16[2,16,2048]{2,1,0:T(8,128)(2,1)S(1)}, u32[]{:S(2)}, u32[]{:S(2)}) collective-permute-start(bf16[2,16,2048]{2,1,0:T(8,128)(2,1)S(1)} %get-tuple-element.77), channel_id=1, source_target_pairs={{0,48},{8,56},{16,64},{24,72},{32,80},{40,88},{48,96},{56,104},{64... | collective-permute-start | bytes 393224 | tf_op jit(solution)/shard_map/ppermute | solution.py:20
  23.0 3.4 %collective-permute-start.2 = (bf16[2,16,2048]{2,1,0:T(8,128)(2,1)S(1)}, bf16[2,16,2048]{2,1,0:T(8,128)(2,1)S(1)}, u32[]{:S(2)}, u32[]{:S(2)}) collective-permute-start(bf16[2,16,2048]{2,1,0:T(8,128)(2,1)S(1)} %get-tuple-element.77), channel_id=1, source_target_pairs={{0,32},{8,40},{16,48},{24,56},{32,64},{40,72},{48,80},{56,88},{64,... | collective-permute-start | bytes 393224 | tf_op jit(solution)/shard_map/ppermute | solution.py:20
  26.5 2.5 %collective-permute-start.1 = (bf16[2,16,2048]{2,1,0:T(8,128)(2,1)S(1)}, bf16[2,16,2048]{2,1,0:T(8,128)(2,1)S(1)}, u32[]{:S(2)}, u32[]{:S(2)}) collective-permute-start(bf16[2,16,2048]{2,1,0:T(8,128)(2,1)S(1)} %get-tuple-element.77), channel_id=1, source_target_pairs={{0,16},{8,24},{16,32},{24,40},{32,48},{40,56},{48,64},{56,72},{64,... | collective-permute-start | bytes 393224 | tf_op jit(solution)/shard_map/ppermute | solution.py:20
  29.7 0.0 collective-permute-done.4
  29.7 2.2 %collective-permute-start.9 = (bf16[64,2048]{1,0:T(8,128)(2,1)S(1)}, bf16[64,2048]{1,0:T(8,128)(2,1)S(1)}, u32[]{:S(2)}, u32[]{:S(2)}) collective-permute-start(bf16[64,2048]{1,0:T(8,128)(2,1)S(1)} %get-tuple-element.36), channel_id=1, source_target_pairs={{0,2},{1,3},{2,4},{3,5},{4,6},{5,7},{8,10},{9,11},{10,12},{11,13},... | collective-permute-start | bytes 786440 | tf_op jit(solution)/shard_map/ppermute | solution.py:157
  31.9 0.0 collective-permute-done.5
  31.9 2.6 %collective-permute-start.10 = (bf16[64,2048]{1,0:T(8,128)(2,1)S(1)}, bf16[64,2048]{1,0:T(8,128)(2,1)S(1)}, u32[]{:S(2)}, u32[]{:S(2)}) collective-permute-start(bf16[64,2048]{1,0:T(8,128)(2,1)S(1)} %get-tuple-element.37), channel_id=1, source_target_pairs={{1,7},{9,15},{17,23},{25,31},{33,39},{41,47},{49,55},{57,63},{65,7... | collective-permute-start | bytes 786440 | tf_op jit(solution)/shard_map/ppermute | solution.py:157
  34.5 0.0 collective-permute-done.2
  34.5 1.3 collective-permute-done.1
  35.9 0.0 copy-start.3
  35.9 3.4 %collective-permute-start.6 = (bf16[16,2048]{1,0:T(8,128)(2,1)S(1)}, bf16[16,2048]{1,0:T(8,128)(2,1)S(1)}, u32[]{:S(2)}, u32[]{:S(2)}) collective-permute-start(bf16[16,2048]{1,0:T(8,128)(2,1)S(1)} %dynamic-slice_bitcast_fusion.refs_0_.refs_8_), channel_id=1, source_target_pairs={{0,4},{1,5},{2,6},{3,7},{4,0},{5,1},{6,2},{7,3},{8,12},{9,13},{10,... | collective-permute-start | bytes 196616 | tf_op jit(solution)/shard_map/ppermute | solution.py:157
  39.3 0.1 pad_maximum_fusion.2
  39.4 4.0 %collective-permute-start.8 = (bf16[80,2048]{1,0:T(8,128)(2,1)S(1)}, bf16[80,2048]{1,0:T(8,128)(2,1)S(1)}, u32[]{:S(2)}, u32[]{:S(2)}) collective-permute-start(bf16[80,2048]{1,0:T(8,128)(2,1)S(1)} %get-tuple-element.75), channel_id=1, source_target_pairs={{0,6},{1,7},{2,0},{3,1},{4,2},{5,3},{6,4},{7,5},{8,14},{9,15},{10,... | collective-permute-start | bytes 983048 | tf_op jit(solution)/shard_map/ppermute | solution.py:157
  43.4 2.2 %collective-permute-start.7 = (bf16[80,2048]{1,0:T(8,128)(2,1)S(1)}, bf16[80,2048]{1,0:T(8,128)(2,1)S(1)}, u32[]{:S(2)}, u32[]{:S(2)}) collective-permute-start(bf16[80,2048]{1,0:T(8,128)(2,1)S(1)} %get-tuple-element.76), channel_id=1, source_target_pairs={{0,2},{1,3},{2,4},{3,5},{4,6},{5,7},{6,0},{7,1},{8,10},{9,11},{10,... | collective-permute-start | bytes 983048 | tf_op jit(solution)/shard_map/ppermute | solution.py:157
  45.6 0.0 copy-start.2
  45.7 0.3 broadcast_select_fusion
  46.0 0.0 copy-start.10
  46.0 0.1 pad_maximum_fusion
  46.1 0.4 copy-done.2
  46.4 5.4 %collective-permute-start.11 = (bf16[256,2048]{1,0:T(8,128)(2,1)S(1)}, bf16[256,2048]{1,0:T(8,128)(2,1)}, u32[]{:S(2)}, u32[]{:S(2)}) collective-permute-start(bf16[256,2048]{1,0:T(8,128)(2,1)S(1)} %pad_maximum_fusion), channel_id=1, source_target_pairs={{0,1},{1,0},{2,3},{3,2},{4,5},{5,4},{6,7},{7,6},{8,9},{9,8},{10,11... | collective-permute-start | bytes 3145736 | tf_op jit(solution)/shard_map/ppermute | solution.py:157
  51.8 7.4 %collective-permute-done.8.refs_3_.refs_11_ = bf16[80,2048]{1,0:T(8,128)(2,1)S(1)} collective-permute-done((bf16[80,2048]{1,0:T(8,128)(2,1)S(1)}, bf16[80,2048]{1,0:T(8,128)(2,1)S(1)}, u32[]{:S(2)}, u32[]{:S(2)}) %collective-permute-start.8) | collective-permute-done | bytes 327712 | tf_op jit(solution)/shard_map/ppermute | solution.py:157
  59.2 0.0 collective-permute-done.7.refs_2_.refs_10_
  59.2 0.1 pad_maximum_fusion.1
  59.3 3.5 %collective-permute-start.12 = (bf16[192,2048]{1,0:T(8,128)(2,1)S(1)}, bf16[192,2048]{1,0:T(8,128)(2,1)}, u32[]{:S(2)}, u32[]{:S(2)}) collective-permute-start(bf16[192,2048]{1,0:T(8,128)(2,1)S(1)} %pad_maximum_fusion.1), channel_id=1, source_target_pairs={{0,1},{1,0},{2,3},{3,2},{4,5},{5,4},{6,7},{7,6},{8,9},{9,8},{10,11... | collective-permute-start | bytes 2359304 | tf_op jit(solution)/shard_map/ppermute | solution.py:157
  62.8 0.2 reduce-window_clone.1
  63.0 0.6 select_reduce_fusion
  63.6 1.2 collective-permute-done.12.refs_7_.refs_15_
  64.8 17.6 %shard_map.85 = (bf16[128,4096]{1,0:T(8,128)(2,1)}, bf16[3,128,2048]{2,1,0:T(8,128)(2,1)}, bf16[448,2048]{1,0:T(8,128)(2,1)}, bf16[64,2048]{1,0:T(8,128)(2,1)}) custom-call(s32[1]{0:T(128)} %bitcast.info, bf16[128,4096]{1,0:T(8,128)(2,1)} %bitcast.78, bf16[128,4096]{1,0:T(8,128)(2,1)} %bitcast.79, s32[1,128]{1,0:T(1,128)} %bitcast.81, ...), custom_call_target="tpu_custom_call" | custom-call | flops 4697620480 | bytes 12582912 | tf_op jit(solution)/shard_map/pallas_call | solution.py:114
  82.4 2.3 %collective-permute-start.13 = (bf16[448,2048]{1,0:T(8,128)(2,1)}, bf16[448,2048]{1,0:T(8,128)(2,1)S(1)}, u32[]{:S(2)}, u32[]{:S(2)}) collective-permute-start(bf16[448,2048]{1,0:T(8,128)(2,1)} %get-tuple-element.40), channel_id=1, source_target_pairs={{0,1},{1,0},{2,3},{3,2},{4,5},{5,4},{6,7},{7,6},{8,9},{9,8},{10,11... | collective-permute-start | bytes 5505032 | tf_op jit(solution)/shard_map/ppermute | solution.py:157
  84.7 3.6 %collective-permute-done.13 = bf16[448,2048]{1,0:T(8,128)(2,1)S(1)} collective-permute-done((bf16[448,2048]{1,0:T(8,128)(2,1)}, bf16[448,2048]{1,0:T(8,128)(2,1)S(1)}, u32[]{:S(2)}, u32[]{:S(2)}) %collective-permute-start.13) | collective-permute-done | bytes 1835040 | tf_op jit(solution)/shard_map/ppermute | solution.py:157
  88.3 1.1 add_convert_fusion.2
  89.5 0.1 slice.137
  89.6 0.2 copy-done.1
  89.8 0.6 add_convert_fusion
  90.4 0.9 slice_bitcast_fusion
  91.3 4.5 %collective-permute-start.14 = (bf16[80,2048]{1,0:T(8,128)(2,1)S(1)}, bf16[80,2048]{1,0:T(8,128)(2,1)S(1)}, u32[]{:S(2)}, u32[]{:S(2)}) collective-permute-start(bf16[80,2048]{1,0:T(8,128)(2,1)S(1)} %pad_maximum_fusion.4), channel_id=1, source_target_pairs={{0,6},{1,7},{2,0},{3,1},{4,2},{5,3},{6,4},{7,5},{8,14},{9,15},{10,... | collective-permute-start | bytes 983048 | tf_op jit(solution)/shard_map/ppermute | solution.py:157
  95.9 1.9 %collective-permute-start.15 = (bf16[80,2048]{1,0:T(8,128)(2,1)S(1)}, bf16[80,2048]{1,0:T(8,128)(2,1)}, u32[]{:S(2)}, u32[]{:S(2)}) collective-permute-start(bf16[80,2048]{1,0:T(8,128)(2,1)S(1)} %pad_maximum_fusion.5), channel_id=1, source_target_pairs={{0,2},{1,3},{2,4},{3,5},{4,6},{5,7},{6,0},{7,1},{8,10},{9,11},{10,... | collective-permute-start | bytes 983048 | tf_op jit(solution)/shard_map/ppermute | solution.py:157
  97.8 5.5 %collective-permute-start.16 = (bf16[16,2048]{1,0:T(8,128)(2,1)S(1)}, bf16[16,2048]{1,0:T(8,128)(2,1)S(1)}, u32[]{:S(2)}, u32[]{:S(2)}) collective-permute-start(bf16[16,2048]{1,0:T(8,128)(2,1)S(1)} %get-tuple-element.67), channel_id=1, source_target_pairs={{0,4},{1,5},{2,6},{3,7},{4,0},{5,1},{6,2},{7,3},{8,12},{9,13},{10,... | collective-permute-start | bytes 196616 | tf_op jit(solution)/shard_map/ppermute | solution.py:157
  103.3 1.3 collective-permute-start.18
  104.6 1.3 collective-permute-start.17
  105.9 3.9 %collective-permute-done.16 = bf16[16,2048]{1,0:T(8,128)(2,1)S(1)} collective-permute-done((bf16[16,2048]{1,0:T(8,128)(2,1)S(1)}, bf16[16,2048]{1,0:T(8,128)(2,1)S(1)}, u32[]{:S(2)}, u32[]{:S(2)}) %collective-permute-start.16) | collective-permute-done | bytes 65568 | tf_op jit(solution)/shard_map/ppermute | solution.py:157
  109.8 1.1 fusion
  110.9 0.9 select_bitcast_fusion.1
  111.8 15.2 %collective-permute-start.19 = (bf16[2,16,2048]{2,1,0:T(8,128)(2,1)S(1)}, bf16[2,16,2048]{2,1,0:T(8,128)(2,1)S(1)}, u32[]{:S(2)}, u32[]{:S(2)}) collective-permute-start(bf16[2,16,2048]{2,1,0:T(8,128)(2,1)S(1)} %pad_maximum_fusion.6), channel_id=1, source_target_pairs={{0,496},{8,504},{16,0},{24,8},{32,16},{40,24},{48,32},{56,40},{64,... | collective-permute-start | bytes 393224 | tf_op jit(solution)/shard_map/ppermute | solution.py:20
  127.0 0.7 pad_maximum_fusion.7
  127.7 1.9 %collective-permute-start.20 = (bf16[2,16,2048]{2,1,0:T(8,128)(2,1)}, bf16[2,16,2048]{2,1,0:T(8,128)(2,1)S(1)}, u32[]{:S(2)}, u32[]{:S(2)}) collective-permute-start(bf16[2,16,2048]{2,1,0:T(8,128)(2,1)} %pad_maximum_fusion.7), channel_id=1, source_target_pairs={{0,480},{8,488},{16,496},{24,504},{32,0},{40,8},{48,16},{56,24},{6... | collective-permute-start | bytes 393224 | tf_op jit(solution)/shard_map/ppermute | solution.py:20
  129.6 0.0 collective-permute-done.17
  129.6 0.0 collective-permute-done.19
  129.6 1.3 collective-permute-start.22
  130.9 5.5 %collective-permute-start.23 = (bf16[64,2048]{1,0:T(8,128)(2,1)S(1)}, bf16[64,2048]{1,0:T(8,128)(2,1)S(1)}, u32[]{:S(2)}, u32[]{:S(2)}) collective-permute-start(bf16[64,2048]{1,0:T(8,128)(2,1)S(1)} %get-tuple-element.47), channel_id=1, source_target_pairs={{6,0},{7,1},{0,2},{1,3},{14,8},{15,9},{8,10},{9,11},{22,16},{23,17... | collective-permute-start | bytes 786440 | tf_op jit(solution)/shard_map/ppermute | solution.py:157
  136.4 0.7 pad_maximum_fusion.8
  137.1 5.0 %collective-permute-start.21 = (bf16[2,16,2048]{2,1,0:T(8,128)(2,1)}, bf16[2,16,2048]{2,1,0:T(8,128)(2,1)}, u32[]{:S(2)}, u32[]{:S(2)}) collective-permute-start(bf16[2,16,2048]{2,1,0:T(8,128)(2,1)} %pad_maximum_fusion.8), channel_id=1, source_target_pairs={{0,464},{8,472},{16,480},{24,488},{32,496},{40,504},{48,0},{56,8},... | collective-permute-start | bytes 393224 | tf_op jit(solution)/shard_map/ppermute | solution.py:20
  142.2 2.3 %collective-permute-done.21 = bf16[2,16,2048]{2,1,0:T(8,128)(2,1)} collective-permute-done((bf16[2,16,2048]{2,1,0:T(8,128)(2,1)}, bf16[2,16,2048]{2,1,0:T(8,128)(2,1)}, u32[]{:S(2)}, u32[]{:S(2)}) %collective-permute-start.21) | collective-permute-done | bytes 131104 | tf_op jit(solution)/shard_map/ppermute | solution.py:20
  144.5 0.9 fusion.3
  145.4 10.9 %collective-permute-start.24 = (bf16[16,2048]{1,0:T(8,128)(2,1)S(1)}, bf16[16,2048]{1,0:T(8,128)(2,1)S(1)}, u32[]{:S(2)}, u32[]{:S(2)}) collective-permute-start(bf16[16,2048]{1,0:T(8,128)(2,1)S(1)} %fusion.3), channel_id=1, source_target_pairs={{0,504},{8,0},{16,8},{24,16},{32,24},{40,32},{48,40},{56,48},{64,5... | collective-permute-start | bytes 196616 | tf_op jit(solution)/shard_map/ppermute | solution.py:20
  156.3 2.1 %add_convert_fusion.1 = bf16[1,128,2048]{2,1,0:T(8,128)(2,1)} fusion(bf16[4,128,2048]{2,1,0:T(8,128)(2,1)S(1)} %add_convert_fusion, bf16[1,64,2048]{2,1,0:T(8,128)(2,1)} %bitcast.25, bf16[1,64,2048]{2,1,0:T(8,128)(2,1)S(1)} %bitcast.76, bf16[1,64,2048]{2,1,0:T(8,128)(2,1)S(1)} %bitcast.77, bf16[1,64,2048]{2,1,0:T(8,128)(2,1)} %bitcast.75), kind=kLoop, calls=%fused_computation.2 | loop fusion | flops 3145728 | bytes 2097152 | tf_op jit(solution)/shard_map/convert_element_type | solution.py:153
  158.4 1.5 fusion.4
  (42 shorter events, 0.3 us)
Async XLA Ops:
  0.6 18.0 %collective-permute-start = (bf16[1,16,2048]{2,1,0:T(8,128)(2,1)}, bf16[1,16,2048]{2,1,0:T(8,128)(2,1)S(1)}, u32[]{:S(2)}, u32[]{:S(2)}) collective-permute-start(bf16[1,16,2048]{2,1,0:T(8,128)(2,1)} %param.8), channel_id=1, source_target_pairs={{0,8},{8,16},{16,24},{24,32},{32,40},{40,48},{48,56},{56,64},{64,7... | collective-permute-start | bytes 196616 | tf_op jit(solution)/shard_map/ppermute | solution.py:20
  6.5 39.1 %copy-start = (bf16[1,128,2048]{2,1,0:T(8,128)(2,1)S(1)}, bf16[1,128,2048]{2,1,0:T(8,128)(2,1)}, u32[]{:S(2)}) copy-start(bf16[1,128,2048]{2,1,0:T(8,128)(2,1)} %param.7) | copy-start | bytes 1572868
  6.6 23.1 %collective-permute-start.4 = (bf16[64,2048]{1,0:T(8,128)(2,1)S(1)}, bf16[64,2048]{1,0:T(8,128)(2,1)S(1)}, u32[]{:S(2)}, u32[]{:S(2)}) collective-permute-start(bf16[64,2048]{1,0:T(8,128)(2,1)S(1)} %get-tuple-element.37), channel_id=1, source_target_pairs={{0,2},{1,3},{2,4},{3,5},{4,6},{5,7},{8,10},{9,11},{10,12},{11,13},... | collective-permute-start | bytes 786440 | tf_op jit(solution)/shard_map/ppermute | solution.py:157
  12.5 19.4 %collective-permute-start.5 = (bf16[64,2048]{1,0:T(8,128)(2,1)S(1)}, bf16[64,2048]{1,0:T(8,128)(2,1)S(1)}, u32[]{:S(2)}, u32[]{:S(2)}) collective-permute-start(bf16[64,2048]{1,0:T(8,128)(2,1)S(1)} %get-tuple-element.36), channel_id=1, source_target_pairs={{0,6},{1,7},{2,0},{3,1},{8,14},{9,15},{10,8},{11,9},{16,22},{17,23... | collective-permute-start | bytes 786440 | tf_op jit(solution)/shard_map/ppermute | solution.py:157
  18.6 15.9 %collective-permute-start.3 = (bf16[2,16,2048]{2,1,0:T(8,128)(2,1)S(1)}, bf16[2,16,2048]{2,1,0:T(8,128)(2,1)S(1)}, u32[]{:S(2)}, u32[]{:S(2)}) collective-permute-start(bf16[2,16,2048]{2,1,0:T(8,128)(2,1)S(1)} %get-tuple-element.77), channel_id=1, source_target_pairs={{0,48},{8,56},{16,64},{24,72},{32,80},{40,88},{48,96},{56,104},{64... | collective-permute-start | bytes 393224 | tf_op jit(solution)/shard_map/ppermute | solution.py:20
  23.0 11.5 %collective-permute-start.2 = (bf16[2,16,2048]{2,1,0:T(8,128)(2,1)S(1)}, bf16[2,16,2048]{2,1,0:T(8,128)(2,1)S(1)}, u32[]{:S(2)}, u32[]{:S(2)}) collective-permute-start(bf16[2,16,2048]{2,1,0:T(8,128)(2,1)S(1)} %get-tuple-element.77), channel_id=1, source_target_pairs={{0,32},{8,40},{16,48},{24,56},{32,64},{40,72},{48,80},{56,88},{64,... | collective-permute-start | bytes 393224 | tf_op jit(solution)/shard_map/ppermute | solution.py:20
  26.5 9.4 %collective-permute-start.1 = (bf16[2,16,2048]{2,1,0:T(8,128)(2,1)S(1)}, bf16[2,16,2048]{2,1,0:T(8,128)(2,1)S(1)}, u32[]{:S(2)}, u32[]{:S(2)}) collective-permute-start(bf16[2,16,2048]{2,1,0:T(8,128)(2,1)S(1)} %get-tuple-element.77), channel_id=1, source_target_pairs={{0,16},{8,24},{16,32},{24,40},{32,48},{40,56},{48,64},{56,72},{64,... | collective-permute-start | bytes 393224 | tf_op jit(solution)/shard_map/ppermute | solution.py:20
  29.7 15.9 %collective-permute-start.9 = (bf16[64,2048]{1,0:T(8,128)(2,1)S(1)}, bf16[64,2048]{1,0:T(8,128)(2,1)S(1)}, u32[]{:S(2)}, u32[]{:S(2)}) collective-permute-start(bf16[64,2048]{1,0:T(8,128)(2,1)S(1)} %get-tuple-element.36), channel_id=1, source_target_pairs={{0,2},{1,3},{2,4},{3,5},{4,6},{5,7},{8,10},{9,11},{10,12},{11,13},... | collective-permute-start | bytes 786440 | tf_op jit(solution)/shard_map/ppermute | solution.py:157
  31.9 13.7 %collective-permute-start.10 = (bf16[64,2048]{1,0:T(8,128)(2,1)S(1)}, bf16[64,2048]{1,0:T(8,128)(2,1)S(1)}, u32[]{:S(2)}, u32[]{:S(2)}) collective-permute-start(bf16[64,2048]{1,0:T(8,128)(2,1)S(1)} %get-tuple-element.37), channel_id=1, source_target_pairs={{1,7},{9,15},{17,23},{25,31},{33,39},{41,47},{49,55},{57,63},{65,7... | collective-permute-start | bytes 786440 | tf_op jit(solution)/shard_map/ppermute | solution.py:157
  35.9 23.3 %copy-start.3 = (bf16[16,2048]{1,0:T(8,128)(2,1)}, bf16[16,2048]{1,0:T(8,128)(2,1)S(1)}, u32[]{:S(2)}) copy-start(bf16[16,2048]{1,0:T(8,128)(2,1)S(1)} %dynamic-slice_bitcast_fusion.refs_0_.refs_8_) | copy-start | bytes 196612
  35.9 15.9 %collective-permute-start.6 = (bf16[16,2048]{1,0:T(8,128)(2,1)S(1)}, bf16[16,2048]{1,0:T(8,128)(2,1)S(1)}, u32[]{:S(2)}, u32[]{:S(2)}) collective-permute-start(bf16[16,2048]{1,0:T(8,128)(2,1)S(1)} %dynamic-slice_bitcast_fusion.refs_0_.refs_8_), channel_id=1, source_target_pairs={{0,4},{1,5},{2,6},{3,7},{4,0},{5,1},{6,2},{7,3},{8,12},{9,13},{10,... | collective-permute-start | bytes 196616 | tf_op jit(solution)/shard_map/ppermute | solution.py:157
  39.4 19.8 %collective-permute-start.8 = (bf16[80,2048]{1,0:T(8,128)(2,1)S(1)}, bf16[80,2048]{1,0:T(8,128)(2,1)S(1)}, u32[]{:S(2)}, u32[]{:S(2)}) collective-permute-start(bf16[80,2048]{1,0:T(8,128)(2,1)S(1)} %get-tuple-element.75), channel_id=1, source_target_pairs={{0,6},{1,7},{2,0},{3,1},{4,2},{5,3},{6,4},{7,5},{8,14},{9,15},{10,... | collective-permute-start | bytes 983048 | tf_op jit(solution)/shard_map/ppermute | solution.py:157
  43.4 15.8 %collective-permute-start.7 = (bf16[80,2048]{1,0:T(8,128)(2,1)S(1)}, bf16[80,2048]{1,0:T(8,128)(2,1)S(1)}, u32[]{:S(2)}, u32[]{:S(2)}) collective-permute-start(bf16[80,2048]{1,0:T(8,128)(2,1)S(1)} %get-tuple-element.76), channel_id=1, source_target_pairs={{0,2},{1,3},{2,4},{3,5},{4,6},{5,7},{6,0},{7,1},{8,10},{9,11},{10,... | collective-permute-start | bytes 983048 | tf_op jit(solution)/shard_map/ppermute | solution.py:157
  45.6 0.8 copy-start.2
  46.0 16.8 %copy-start.10 = (s32[1,3]{1,0:T(1,128)S(1)}, s32[1,3]{1,0:T(1,128)}, u32[]{:S(2)}) copy-start(s32[1,3]{1,0:T(1,128)} %param.10) | copy-start | bytes 40
  46.4 18.4 %collective-permute-start.11 = (bf16[256,2048]{1,0:T(8,128)(2,1)S(1)}, bf16[256,2048]{1,0:T(8,128)(2,1)}, u32[]{:S(2)}, u32[]{:S(2)}) collective-permute-start(bf16[256,2048]{1,0:T(8,128)(2,1)S(1)} %pad_maximum_fusion), channel_id=1, source_target_pairs={{0,1},{1,0},{2,3},{3,2},{4,5},{5,4},{6,7},{7,6},{8,9},{9,8},{10,11... | collective-permute-start | bytes 3145736 | tf_op jit(solution)/shard_map/ppermute | solution.py:157
  51.8 13.0 %copy-start.9 = (bf16[16,2048]{1,0:T(8,128)(2,1)}, bf16[16,2048]{1,0:T(8,128)(2,1)S(1)}, u32[]{:S(2)}) copy-start(bf16[16,2048]{1,0:T(8,128)(2,1)S(1)} %collective-permute-done.6.refs_1_.refs_9_) | copy-start | bytes 196612
  59.2 5.7 %copy-start.4 = (bf16[80,2048]{1,0:T(8,128)(2,1)}, bf16[80,2048]{1,0:T(8,128)(2,1)S(1)}, u32[]{:S(2)}) copy-start(bf16[80,2048]{1,0:T(8,128)(2,1)S(1)} %collective-permute-done.8.refs_3_.refs_11_) | copy-start | bytes 983044
  59.2 5.7 %copy-start.5 = (bf16[80,2048]{1,0:T(8,128)(2,1)}, bf16[80,2048]{1,0:T(8,128)(2,1)S(1)}, u32[]{:S(2)}) copy-start(bf16[80,2048]{1,0:T(8,128)(2,1)S(1)} %collective-permute-done.7.refs_2_.refs_10_) | copy-start | bytes 983044
  59.3 5.6 %collective-permute-start.12 = (bf16[192,2048]{1,0:T(8,128)(2,1)S(1)}, bf16[192,2048]{1,0:T(8,128)(2,1)}, u32[]{:S(2)}, u32[]{:S(2)}) collective-permute-start(bf16[192,2048]{1,0:T(8,128)(2,1)S(1)} %pad_maximum_fusion.1), channel_id=1, source_target_pairs={{0,1},{1,0},{2,3},{3,2},{4,5},{5,4},{6,7},{7,6},{8,9},{9,8},{10,11... | collective-permute-start | bytes 2359304 | tf_op jit(solution)/shard_map/ppermute | solution.py:157
  82.4 5.9 %collective-permute-start.13 = (bf16[448,2048]{1,0:T(8,128)(2,1)}, bf16[448,2048]{1,0:T(8,128)(2,1)S(1)}, u32[]{:S(2)}, u32[]{:S(2)}) collective-permute-start(bf16[448,2048]{1,0:T(8,128)(2,1)} %get-tuple-element.40), channel_id=1, source_target_pairs={{0,1},{1,0},{2,3},{3,2},{4,5},{5,4},{6,7},{7,6},{8,9},{9,8},{10,11... | collective-permute-start | bytes 5505032 | tf_op jit(solution)/shard_map/ppermute | solution.py:157
  88.3 1.5 copy-start.1
  91.3 18.4 %collective-permute-start.14 = (bf16[80,2048]{1,0:T(8,128)(2,1)S(1)}, bf16[80,2048]{1,0:T(8,128)(2,1)S(1)}, u32[]{:S(2)}, u32[]{:S(2)}) collective-permute-start(bf16[80,2048]{1,0:T(8,128)(2,1)S(1)} %pad_maximum_fusion.4), channel_id=1, source_target_pairs={{0,6},{1,7},{2,0},{3,1},{4,2},{5,3},{6,4},{7,5},{8,14},{9,15},{10,... | collective-permute-start | bytes 983048 | tf_op jit(solution)/shard_map/ppermute | solution.py:157
  95.9 13.9 %collective-permute-start.15 = (bf16[80,2048]{1,0:T(8,128)(2,1)S(1)}, bf16[80,2048]{1,0:T(8,128)(2,1)}, u32[]{:S(2)}, u32[]{:S(2)}) collective-permute-start(bf16[80,2048]{1,0:T(8,128)(2,1)S(1)} %pad_maximum_fusion.5), channel_id=1, source_target_pairs={{0,2},{1,3},{2,4},{3,5},{4,6},{5,7},{6,0},{7,1},{8,10},{9,11},{10,... | collective-permute-start | bytes 983048 | tf_op jit(solution)/shard_map/ppermute | solution.py:157
  97.8 12.0 %collective-permute-start.16 = (bf16[16,2048]{1,0:T(8,128)(2,1)S(1)}, bf16[16,2048]{1,0:T(8,128)(2,1)S(1)}, u32[]{:S(2)}, u32[]{:S(2)}) collective-permute-start(bf16[16,2048]{1,0:T(8,128)(2,1)S(1)} %get-tuple-element.67), channel_id=1, source_target_pairs={{0,4},{1,5},{2,6},{3,7},{4,0},{5,1},{6,2},{7,3},{8,12},{9,13},{10,... | collective-permute-start | bytes 196616 | tf_op jit(solution)/shard_map/ppermute | solution.py:157
  103.3 26.3 %collective-permute-start.18 = (bf16[64,2048]{1,0:T(8,128)(2,1)}, bf16[64,2048]{1,0:T(8,128)(2,1)S(1)}, u32[]{:S(2)}, u32[]{:S(2)}) collective-permute-start(bf16[64,2048]{1,0:T(8,128)(2,1)} %get-tuple-element.57), channel_id=1, source_target_pairs={{7,1},{15,9},{23,17},{31,25},{39,33},{47,41},{55,49},{63,57},{71,6... | collective-permute-start | bytes 786440 | tf_op jit(solution)/shard_map/ppermute | solution.py:157
  104.6 25.0 %collective-permute-start.17 = (bf16[64,2048]{1,0:T(8,128)(2,1)}, bf16[64,2048]{1,0:T(8,128)(2,1)}, u32[]{:S(2)}, u32[]{:S(2)}) collective-permute-start(bf16[64,2048]{1,0:T(8,128)(2,1)} %get-tuple-element.58), channel_id=1, source_target_pairs={{2,0},{3,1},{4,2},{5,3},{6,4},{7,5},{10,8},{11,9},{12,10},{13,11},... | collective-permute-start | bytes 786440 | tf_op jit(solution)/shard_map/ppermute | solution.py:157
  111.8 17.8 %collective-permute-start.19 = (bf16[2,16,2048]{2,1,0:T(8,128)(2,1)S(1)}, bf16[2,16,2048]{2,1,0:T(8,128)(2,1)S(1)}, u32[]{:S(2)}, u32[]{:S(2)}) collective-permute-start(bf16[2,16,2048]{2,1,0:T(8,128)(2,1)S(1)} %pad_maximum_fusion.6), channel_id=1, source_target_pairs={{0,496},{8,504},{16,0},{24,8},{32,16},{40,24},{48,32},{56,40},{64,... | collective-permute-start | bytes 393224 | tf_op jit(solution)/shard_map/ppermute | solution.py:20
  127.7 14.5 %collective-permute-start.20 = (bf16[2,16,2048]{2,1,0:T(8,128)(2,1)}, bf16[2,16,2048]{2,1,0:T(8,128)(2,1)S(1)}, u32[]{:S(2)}, u32[]{:S(2)}) collective-permute-start(bf16[2,16,2048]{2,1,0:T(8,128)(2,1)} %pad_maximum_fusion.7), channel_id=1, source_target_pairs={{0,480},{8,488},{16,496},{24,504},{32,0},{40,8},{48,16},{56,24},{6... | collective-permute-start | bytes 393224 | tf_op jit(solution)/shard_map/ppermute | solution.py:20
  129.6 7.5 %copy-start.6 = (bf16[64,2048]{1,0:T(8,128)(2,1)}, bf16[64,2048]{1,0:T(8,128)(2,1)S(1)}, u32[]{:S(2)}) copy-start(bf16[64,2048]{1,0:T(8,128)(2,1)S(1)} %collective-permute-done.18) | copy-start | bytes 786436
  129.6 7.5 %copy-start.7 = (bf16[2,16,2048]{2,1,0:T(8,128)(2,1)}, bf16[2,16,2048]{2,1,0:T(8,128)(2,1)S(1)}, u32[]{:S(2)}) copy-start(bf16[2,16,2048]{2,1,0:T(8,128)(2,1)S(1)} %collective-permute-done.19) | copy-start | bytes 393220
  129.6 14.9 %collective-permute-start.22 = (bf16[64,2048]{1,0:T(8,128)(2,1)S(1)}, bf16[64,2048]{1,0:T(8,128)(2,1)S(1)}, u32[]{:S(2)}, u32[]{:S(2)}) collective-permute-start(bf16[64,2048]{1,0:T(8,128)(2,1)S(1)} %get-tuple-element.46), channel_id=1, source_target_pairs={{2,0},{3,1},{4,2},{5,3},{6,4},{7,5},{10,8},{11,9},{12,10},{13,11},... | collective-permute-start | bytes 786440 | tf_op jit(solution)/shard_map/ppermute | solution.py:157
  130.9 13.6 %collective-permute-start.23 = (bf16[64,2048]{1,0:T(8,128)(2,1)S(1)}, bf16[64,2048]{1,0:T(8,128)(2,1)S(1)}, u32[]{:S(2)}, u32[]{:S(2)}) collective-permute-start(bf16[64,2048]{1,0:T(8,128)(2,1)S(1)} %get-tuple-element.47), channel_id=1, source_target_pairs={{6,0},{7,1},{0,2},{1,3},{14,8},{15,9},{8,10},{9,11},{22,16},{23,17... | collective-permute-start | bytes 786440 | tf_op jit(solution)/shard_map/ppermute | solution.py:157
  137.1 7.4 %collective-permute-start.21 = (bf16[2,16,2048]{2,1,0:T(8,128)(2,1)}, bf16[2,16,2048]{2,1,0:T(8,128)(2,1)}, u32[]{:S(2)}, u32[]{:S(2)}) collective-permute-start(bf16[2,16,2048]{2,1,0:T(8,128)(2,1)} %pad_maximum_fusion.8), channel_id=1, source_target_pairs={{0,464},{8,472},{16,480},{24,488},{32,496},{40,504},{48,0},{56,8},... | collective-permute-start | bytes 393224 | tf_op jit(solution)/shard_map/ppermute | solution.py:20
  142.2 16.2 %copy-start.8 = (bf16[2,16,2048]{2,1,0:T(8,128)(2,1)S(1)}, bf16[2,16,2048]{2,1,0:T(8,128)(2,1)}, u32[]{:S(2)}) copy-start(bf16[2,16,2048]{2,1,0:T(8,128)(2,1)} %copy-done.7) | copy-start | bytes 393220
  145.4 12.9 %collective-permute-start.24 = (bf16[16,2048]{1,0:T(8,128)(2,1)S(1)}, bf16[16,2048]{1,0:T(8,128)(2,1)S(1)}, u32[]{:S(2)}, u32[]{:S(2)}) collective-permute-start(bf16[16,2048]{1,0:T(8,128)(2,1)S(1)} %fusion.3), channel_id=1, source_target_pairs={{0,504},{8,0},{16,8},{24,16},{32,24},{40,32},{48,40},{56,48},{64,5... | collective-permute-start | bytes 196616 | tf_op jit(solution)/shard_map/ppermute | solution.py:20

commit v7 on v6

--- a/solution.py
+++ b/solution.py
@@ -232,7 +232,6 @@
     top_one, low_three, low1, top3, pairs[0] = tied((top_one, low_three, low1, top3, pairs[0]))
     top1 = along_seq(top_one, [(i, i - 2) for i in range(2, n)])
     low3 = along_seq(low_three, [(i, (i + 2) % n) for i in (n - 2, n - 1, 0, 1)])
-    *pairs, top1, low3 = tied((*pairs, top1, low3))
     by1 = passed_along(added(left[1], *[pair[1] for pair in pairs]), "dp", -1)
     d_kv = added(own, jnp.concatenate([top1, low1]), jnp.concatenate([top3, low3]))
     return d_kv, added(left[0], by1, *[pair[0] for pair in pairs])

time: 163 us -> 161 us (0.988)
  the two profiles are of different devices: /device:TPU:1 before, /device:TPU:68 now
where the time goes in v7:
time: 161 us; the launch traced here: 160 us
  starting transfers between devices  90.2 us (56%)
  waiting for transfers between devices  38.5 us (24%)
  Pallas kernels  17.6 us (11%)
  other arithmetic  7.95 us (5%)
  local copies, waits for them, and re-layouts  3.58 us (2%)
  between operations  1.87 us (1%)
    ppermute x17, starting transfers between devices, along_seq(): return lax.ppermute(value, 'seq', pairs)  53.6 us
    ppermute x8, starting transfers between devices, passed_along(): lax.ppermute(value, axis, [(i, (i + by) % peers) for i in range(peers)])  36.6 us
    ppermute x17, waiting for transfers between devices, along_seq(): return lax.ppermute(value, 'seq', pairs)  32.1 us
    pallas_call x1, Pallas kernels, attend(): pl.pallas_call(functools.partial(attention_kernel, span, n_seq), grid_spe...  17.6 us
    ppermute x8, waiting for transfers between devices, passed_along(): lax.ppermute(value, axis, [(i, (i + by) % peers) for i in range(peers)])  6.37 us
    convert_element_type x5, other arithmetic, added(): return total.astype(jnp.bfloat16)  4.97 us
  transfers between devices with their start and end apart: 25, of which 10 were waited for; matrix products, arithmetic and copies ran while one was open for 4% of the time, Pallas kernels for 0%

profile of v7, /device:TPU:68, one launch (start us, length us, event | category | flops | bytes accessed | tf_op | source)
XLA Modules:
  0.0 159.6 jit_solution(15679325763449052469)
XLA Ops:
  0.6 2.2 %collective-permute-start = (bf16[1,16,2048]{2,1,0:T(8,128)(2,1)}, bf16[1,16,2048]{2,1,0:T(8,128)(2,1)S(1)}, u32[]{:S(2)}, u32[]{:S(2)}) collective-permute-start(bf16[1,16,2048]{2,1,0:T(8,128)(2,1)} %param.8), channel_id=1, source_target_pairs={{0,8},{8,16},{16,24},{24,32},{32,40},{40,48},{48,56},{56,64},{64,7... | collective-permute-start | bytes 196616 | tf_op jit(solution)/shard_map/ppermute | solution.py:20
  2.8 1.1 slice_bitcast_fusion.6
  3.9 0.0 copy-start
  3.9 6.2 %collective-permute-start.4 = (bf16[64,2048]{1,0:T(8,128)(2,1)S(1)}, bf16[64,2048]{1,0:T(8,128)(2,1)S(1)}, u32[]{:S(2)}, u32[]{:S(2)}) collective-permute-start(bf16[64,2048]{1,0:T(8,128)(2,1)S(1)} %get-tuple-element.32), channel_id=1, source_target_pairs={{0,2},{1,3},{2,4},{3,5},{4,6},{5,7},{8,10},{9,11},{10,12},{11,13},... | collective-permute-start | bytes 786440 | tf_op jit(solution)/shard_map/ppermute | solution.py:157
  10.2 6.1 %collective-permute-start.5 = (bf16[64,2048]{1,0:T(8,128)(2,1)S(1)}, bf16[64,2048]{1,0:T(8,128)(2,1)S(1)}, u32[]{:S(2)}, u32[]{:S(2)}) collective-permute-start(bf16[64,2048]{1,0:T(8,128)(2,1)S(1)} %get-tuple-element.31), channel_id=1, source_target_pairs={{0,6},{1,7},{2,0},{3,1},{8,14},{9,15},{10,8},{11,9},{16,22},{17,23... | collective-permute-start | bytes 786440 | tf_op jit(solution)/shard_map/ppermute | solution.py:157
  16.3 0.9 constant_dynamic-update-slice_fusion.1
  17.1 0.0 collective-permute-done
  17.2 3.8 %collective-permute-start.3 = (bf16[2,16,2048]{2,1,0:T(8,128)(2,1)S(1)}, bf16[2,16,2048]{2,1,0:T(8,128)(2,1)S(1)}, u32[]{:S(2)}, u32[]{:S(2)}) collective-permute-start(bf16[2,16,2048]{2,1,0:T(8,128)(2,1)S(1)} %get-tuple-element.67), channel_id=1, source_target_pairs={{0,48},{8,56},{16,64},{24,72},{32,80},{40,88},{48,96},{56,104},{64... | collective-permute-start | bytes 393224 | tf_op jit(solution)/shard_map/ppermute | solution.py:20
  20.9 4.6 %collective-permute-start.2 = (bf16[2,16,2048]{2,1,0:T(8,128)(2,1)S(1)}, bf16[2,16,2048]{2,1,0:T(8,128)(2,1)S(1)}, u32[]{:S(2)}, u32[]{:S(2)}) collective-permute-start(bf16[2,16,2048]{2,1,0:T(8,128)(2,1)S(1)} %get-tuple-element.67), channel_id=1, source_target_pairs={{0,32},{8,40},{16,48},{24,56},{32,64},{40,72},{48,80},{56,88},{64,... | collective-permute-start | bytes 393224 | tf_op jit(solution)/shard_map/ppermute | solution.py:20
  25.6 2.8 %collective-permute-start.1 = (bf16[2,16,2048]{2,1,0:T(8,128)(2,1)S(1)}, bf16[2,16,2048]{2,1,0:T(8,128)(2,1)S(1)}, u32[]{:S(2)}, u32[]{:S(2)}) collective-permute-start(bf16[2,16,2048]{2,1,0:T(8,128)(2,1)S(1)} %get-tuple-element.67), channel_id=1, source_target_pairs={{0,16},{8,24},{16,32},{24,40},{32,48},{40,56},{48,64},{56,72},{64,... | collective-permute-start | bytes 393224 | tf_op jit(solution)/shard_map/ppermute | solution.py:20
  29.1 0.0 collective-permute-done.4
  29.1 2.5 %collective-permute-start.9 = (bf16[64,2048]{1,0:T(8,128)(2,1)S(1)}, bf16[64,2048]{1,0:T(8,128)(2,1)S(1)}, u32[]{:S(2)}, u32[]{:S(2)}) collective-permute-start(bf16[64,2048]{1,0:T(8,128)(2,1)S(1)} %get-tuple-element.31), channel_id=1, source_target_pairs={{0,2},{1,3},{2,4},{3,5},{4,6},{5,7},{8,10},{9,11},{10,12},{11,13},... | collective-permute-start | bytes 786440 | tf_op jit(solution)/shard_map/ppermute | solution.py:157
  31.6 0.7 collective-permute-start.10
  32.3 0.0 collective-permute-done.3
  32.3 0.2 collective-permute-done.1
  32.5 0.0 copy-start.3
  32.5 3.7 %collective-permute-start.6 = (bf16[16,2048]{1,0:T(8,128)(2,1)S(1)}, bf16[16,2048]{1,0:T(8,128)(2,1)S(1)}, u32[]{:S(2)}, u32[]{:S(2)}) collective-permute-start(bf16[16,2048]{1,0:T(8,128)(2,1)S(1)} %dynamic-slice_bitcast_fusion.refs_0_.refs_8_), channel_id=1, source_target_pairs={{0,4},{1,5},{2,6},{3,7},{4,0},{5,1},{6,2},{7,3},{8,12},{9,13},{10,... | collective-permute-start | bytes 196616 | tf_op jit(solution)/shard_map/ppermute | solution.py:157
  36.3 0.1 pad_maximum_fusion.2
  36.3 5.3 %collective-permute-start.8 = (bf16[80,2048]{1,0:T(8,128)(2,1)S(1)}, bf16[80,2048]{1,0:T(8,128)(2,1)S(1)}, u32[]{:S(2)}, u32[]{:S(2)}) collective-permute-start(bf16[80,2048]{1,0:T(8,128)(2,1)S(1)} %get-tuple-element.65), channel_id=1, source_target_pairs={{0,6},{1,7},{2,0},{3,1},{4,2},{5,3},{6,4},{7,5},{8,14},{9,15},{10,... | collective-permute-start | bytes 983048 | tf_op jit(solution)/shard_map/ppermute | solution.py:157
  41.6 1.9 %collective-permute-start.7 = (bf16[80,2048]{1,0:T(8,128)(2,1)S(1)}, bf16[80,2048]{1,0:T(8,128)(2,1)S(1)}, u32[]{:S(2)}, u32[]{:S(2)}) collective-permute-start(bf16[80,2048]{1,0:T(8,128)(2,1)S(1)} %get-tuple-element.66), channel_id=1, source_target_pairs={{0,2},{1,3},{2,4},{3,5},{4,6},{5,7},{6,0},{7,1},{8,10},{9,11},{10,... | collective-permute-start | bytes 983048 | tf_op jit(solution)/shard_map/ppermute | solution.py:157
  43.5 4.4 %collective-permute-done.9 = bf16[64,2048]{1,0:T(8,128)(2,1)S(1)} collective-permute-done((bf16[64,2048]{1,0:T(8,128)(2,1)S(1)}, bf16[64,2048]{1,0:T(8,128)(2,1)S(1)}, u32[]{:S(2)}, u32[]{:S(2)}) %collective-permute-start.9) | collective-permute-done | bytes 262176 | tf_op jit(solution)/shard_map/ppermute | solution.py:157
  48.0 0.0 copy-start.2
  48.0 0.3 broadcast_select_fusion
  48.3 0.0 copy-start.7
  48.3 0.1 pad_maximum_fusion
  48.4 0.3 copy-done.2
  48.8 1.9 %collective-permute-start.11 = (bf16[256,2048]{1,0:T(8,128)(2,1)S(1)}, bf16[256,2048]{1,0:T(8,128)(2,1)}, u32[]{:S(2)}, u32[]{:S(2)}) collective-permute-start(bf16[256,2048]{1,0:T(8,128)(2,1)S(1)} %pad_maximum_fusion), channel_id=1, source_target_pairs={{0,1},{1,0},{2,3},{3,2},{4,5},{5,4},{6,7},{7,6},{8,9},{9,8},{10,11... | collective-permute-start | bytes 3145736 | tf_op jit(solution)/shard_map/ppermute | solution.py:157
  50.7 2.1 %collective-permute-done.8.refs_3_.refs_11_ = bf16[80,2048]{1,0:T(8,128)(2,1)S(1)} collective-permute-done((bf16[80,2048]{1,0:T(8,128)(2,1)S(1)}, bf16[80,2048]{1,0:T(8,128)(2,1)S(1)}, u32[]{:S(2)}, u32[]{:S(2)}) %collective-permute-start.8) | collective-permute-done | bytes 327712 | tf_op jit(solution)/shard_map/ppermute | solution.py:157
  52.8 7.2 %collective-permute-done.7.refs_2_.refs_10_ = bf16[80,2048]{1,0:T(8,128)(2,1)S(1)} collective-permute-done((bf16[80,2048]{1,0:T(8,128)(2,1)S(1)}, bf16[80,2048]{1,0:T(8,128)(2,1)S(1)}, u32[]{:S(2)}, u32[]{:S(2)}) %collective-permute-start.7) | collective-permute-done | bytes 327712 | tf_op jit(solution)/shard_map/ppermute | solution.py:157
  60.0 0.1 pad_maximum_fusion.1
  60.1 1.9 %collective-permute-start.12 = (bf16[192,2048]{1,0:T(8,128)(2,1)S(1)}, bf16[192,2048]{1,0:T(8,128)(2,1)}, u32[]{:S(2)}, u32[]{:S(2)}) collective-permute-start(bf16[192,2048]{1,0:T(8,128)(2,1)S(1)} %pad_maximum_fusion.1), channel_id=1, source_target_pairs={{0,1},{1,0},{2,3},{3,2},{4,5},{5,4},{6,7},{7,6},{8,9},{9,8},{10,11... | collective-permute-start | bytes 2359304 | tf_op jit(solution)/shard_map/ppermute | solution.py:157
  62.0 0.2 reduce-window_clone.1
  62.2 0.6 select_reduce_fusion
  62.8 1.6 %collective-permute-done.12.refs_7_.refs_15_ = bf16[192,2048]{1,0:T(8,128)(2,1)} collective-permute-done((bf16[192,2048]{1,0:T(8,128)(2,1)S(1)}, bf16[192,2048]{1,0:T(8,128)(2,1)}, u32[]{:S(2)}, u32[]{:S(2)}) %collective-permute-start.12) | collective-permute-done | bytes 786464 | tf_op jit(solution)/shard_map/ppermute | solution.py:157
  64.4 17.6 %shard_map.85 = (bf16[128,4096]{1,0:T(8,128)(2,1)}, bf16[3,128,2048]{2,1,0:T(8,128)(2,1)}, bf16[448,2048]{1,0:T(8,128)(2,1)}, bf16[64,2048]{1,0:T(8,128)(2,1)}) custom-call(s32[1]{0:T(128)} %bitcast.info, bf16[128,4096]{1,0:T(8,128)(2,1)} %bitcast.85, bf16[128,4096]{1,0:T(8,128)(2,1)} %bitcast.86, s32[1,128]{1,0:T(1,128)} %bitcast.88, ...), custom_call_target="tpu_custom_call" | custom-call | flops 4697620480 | bytes 12582912 | tf_op jit(solution)/shard_map/pallas_call | solution.py:114
  82.0 2.0 %collective-permute-start.13 = (bf16[448,2048]{1,0:T(8,128)(2,1)}, bf16[448,2048]{1,0:T(8,128)(2,1)S(1)}, u32[]{:S(2)}, u32[]{:S(2)}) collective-permute-start(bf16[448,2048]{1,0:T(8,128)(2,1)} %get-tuple-element.35), channel_id=1, source_target_pairs={{0,1},{1,0},{2,3},{3,2},{4,5},{5,4},{6,7},{7,6},{8,9},{9,8},{10,11... | collective-permute-start | bytes 5505032 | tf_op jit(solution)/shard_map/ppermute | solution.py:157
  84.1 3.9 %collective-permute-done.13 = bf16[448,2048]{1,0:T(8,128)(2,1)S(1)} collective-permute-done((bf16[448,2048]{1,0:T(8,128)(2,1)}, bf16[448,2048]{1,0:T(8,128)(2,1)S(1)}, u32[]{:S(2)}, u32[]{:S(2)}) %collective-permute-start.13) | collective-permute-done | bytes 1835040 | tf_op jit(solution)/shard_map/ppermute | solution.py:157
  87.9 1.1 add_convert_fusion.2
  89.1 0.1 slice.137
  89.2 0.2 copy-done.1
  89.4 0.6 add_convert_fusion
  90.0 0.9 slice_bitcast_fusion
  90.9 2.5 %collective-permute-start.14 = (bf16[80,2048]{1,0:T(8,128)(2,1)S(1)}, bf16[80,2048]{1,0:T(8,128)(2,1)S(1)}, u32[]{:S(2)}, u32[]{:S(2)}) collective-permute-start(bf16[80,2048]{1,0:T(8,128)(2,1)S(1)} %pad_maximum_fusion.4), channel_id=1, source_target_pairs={{0,6},{1,7},{2,0},{3,1},{4,2},{5,3},{6,4},{7,5},{8,14},{9,15},{10,... | collective-permute-start | bytes 983048 | tf_op jit(solution)/shard_map/ppermute | solution.py:157
  93.5 4.2 %collective-permute-start.15 = (bf16[80,2048]{1,0:T(8,128)(2,1)S(1)}, bf16[80,2048]{1,0:T(8,128)(2,1)}, u32[]{:S(2)}, u32[]{:S(2)}) collective-permute-start(bf16[80,2048]{1,0:T(8,128)(2,1)S(1)} %pad_maximum_fusion.5), channel_id=1, source_target_pairs={{0,2},{1,3},{2,4},{3,5},{4,6},{5,7},{6,0},{7,1},{8,10},{9,11},{10,... | collective-permute-start | bytes 983048 | tf_op jit(solution)/shard_map/ppermute | solution.py:157
  97.7 5.2 %collective-permute-start.16 = (bf16[16,2048]{1,0:T(8,128)(2,1)S(1)}, bf16[16,2048]{1,0:T(8,128)(2,1)S(1)}, u32[]{:S(2)}, u32[]{:S(2)}) collective-permute-start(bf16[16,2048]{1,0:T(8,128)(2,1)S(1)} %get-tuple-element.57), channel_id=1, source_target_pairs={{0,4},{1,5},{2,6},{3,7},{4,0},{5,1},{6,2},{7,3},{8,12},{9,13},{10,... | collective-permute-start | bytes 196616 | tf_op jit(solution)/shard_map/ppermute | solution.py:157
  102.9 1.4 collective-permute-start.18
  104.3 1.3 collective-permute-start.17
  105.6 5.9 %collective-permute-done.16 = bf16[16,2048]{1,0:T(8,128)(2,1)S(1)} collective-permute-done((bf16[16,2048]{1,0:T(8,128)(2,1)S(1)}, bf16[16,2048]{1,0:T(8,128)(2,1)S(1)}, u32[]{:S(2)}, u32[]{:S(2)}) %collective-permute-start.16) | collective-permute-done | bytes 65568 | tf_op jit(solution)/shard_map/ppermute | solution.py:157
  111.5 0.0 collective-permute-done.14
  111.5 0.9 select_bitcast_fusion.3
  112.4 5.5 %collective-permute-start.19 = (bf16[2,16,2048]{2,1,0:T(8,128)(2,1)S(1)}, bf16[2,16,2048]{2,1,0:T(8,128)(2,1)S(1)}, u32[]{:S(2)}, u32[]{:S(2)}) collective-permute-start(bf16[2,16,2048]{2,1,0:T(8,128)(2,1)S(1)} %pad_maximum_fusion.6), channel_id=1, source_target_pairs={{0,496},{8,504},{16,0},{24,8},{32,16},{40,24},{48,32},{56,40},{64,... | collective-permute-start | bytes 393224 | tf_op jit(solution)/shard_map/ppermute | solution.py:20
  118.0 13.8 %collective-permute-start.23 = (bf16[2,16,2048]{2,1,0:T(8,128)(2,1)S(1)}, bf16[2,16,2048]{2,1,0:T(8,128)(2,1)S(1)}, u32[]{:S(2)}, u32[]{:S(2)}) collective-permute-start(bf16[2,16,2048]{2,1,0:T(8,128)(2,1)S(1)} %pad_maximum_fusion.8), channel_id=1, source_target_pairs={{0,464},{8,472},{16,480},{24,488},{32,496},{40,504},{48,0},{56,8},... | collective-permute-start | bytes 393224 | tf_op jit(solution)/shard_map/ppermute | solution.py:20
  131.9 1.9 %collective-permute-start.22 = (bf16[2,16,2048]{2,1,0:T(8,128)(2,1)S(1)}, bf16[2,16,2048]{2,1,0:T(8,128)(2,1)S(1)}, u32[]{:S(2)}, u32[]{:S(2)}) collective-permute-start(bf16[2,16,2048]{2,1,0:T(8,128)(2,1)S(1)} %pad_maximum_fusion.7), channel_id=1, source_target_pairs={{0,480},{8,488},{16,496},{24,504},{32,0},{40,8},{48,16},{56,24},{6... | collective-permute-start | bytes 393224 | tf_op jit(solution)/shard_map/ppermute | solution.py:20
  133.8 1.1 fusion
  134.9 0.0 collective-permute-done.18
  134.9 0.0 collective-permute-done.17
  134.9 6.2 %collective-permute-done.22 = bf16[2,16,2048]{2,1,0:T(8,128)(2,1)S(1)} collective-permute-done((bf16[2,16,2048]{2,1,0:T(8,128)(2,1)S(1)}, bf16[2,16,2048]{2,1,0:T(8,128)(2,1)S(1)}, u32[]{:S(2)}, u32[]{:S(2)}) %collective-permute-start.22) | collective-permute-done | bytes 131104 | tf_op jit(solution)/shard_map/ppermute | solution.py:20
  141.2 1.9 %collective-permute-start.24 = (bf16[16,2048]{1,0:T(8,128)(2,1)S(1)}, bf16[16,2048]{1,0:T(8,128)(2,1)S(1)}, u32[]{:S(2)}, u32[]{:S(2)}) collective-permute-start(bf16[16,2048]{1,0:T(8,128)(2,1)S(1)} %fusion.3), channel_id=1, source_target_pairs={{0,504},{8,0},{16,8},{24,16},{32,24},{40,32},{48,40},{56,48},{64,5... | collective-permute-start | bytes 196616 | tf_op jit(solution)/shard_map/ppermute | solution.py:20
  143.1 1.3 collective-permute-start.20
  144.4 5.4 %collective-permute-start.21 = (bf16[64,2048]{1,0:T(8,128)(2,1)S(1)}, bf16[64,2048]{1,0:T(8,128)(2,1)S(1)}, u32[]{:S(2)}, u32[]{:S(2)}) collective-permute-start(bf16[64,2048]{1,0:T(8,128)(2,1)S(1)} %get-tuple-element.43), channel_id=1, source_target_pairs={{6,0},{7,1},{0,2},{1,3},{14,8},{15,9},{8,10},{9,11},{22,16},{23,17... | collective-permute-start | bytes 786440 | tf_op jit(solution)/shard_map/ppermute | solution.py:157
  149.9 0.7 fusion.4
  150.5 4.2 %collective-permute-done.20 = bf16[64,2048]{1,0:T(8,128)(2,1)S(1)} collective-permute-done((bf16[64,2048]{1,0:T(8,128)(2,1)S(1)}, bf16[64,2048]{1,0:T(8,128)(2,1)S(1)}, u32[]{:S(2)}, u32[]{:S(2)}) %collective-permute-start.20) | collective-permute-done | bytes 262176 | tf_op jit(solution)/shard_map/ppermute | solution.py:157
  154.8 2.8 %collective-permute-done.21 = bf16[64,2048]{1,0:T(8,128)(2,1)S(1)} collective-permute-done((bf16[64,2048]{1,0:T(8,128)(2,1)S(1)}, bf16[64,2048]{1,0:T(8,128)(2,1)S(1)}, u32[]{:S(2)}, u32[]{:S(2)}) %collective-permute-start.21) | collective-permute-done | bytes 262176 | tf_op jit(solution)/shard_map/ppermute | solution.py:157
  157.6 2.1 %add_convert_fusion.1 = bf16[1,128,2048]{2,1,0:T(8,128)(2,1)} fusion(bf16[4,128,2048]{2,1,0:T(8,128)(2,1)S(1)} %add_convert_fusion, bf16[1,64,2048]{2,1,0:T(8,128)(2,1)} %bitcast.21, bf16[1,64,2048]{2,1,0:T(8,128)(2,1)S(1)} %bitcast.83, bf16[1,64,2048]{2,1,0:T(8,128)(2,1)S(1)} %bitcast.84, bf16[1,64,2048]{2,1,0:T(8,128)(2,1)} %bitcast.22), kind=kLoop, calls=%fused_computation.2 | loop fusion | flops 3145728 | bytes 2097152 | tf_op jit(solution)/shard_map/convert_element_type | solution.py:153
  (36 shorter events, 0.3 us)
Async XLA Ops:
  0.6 16.5 %collective-permute-start = (bf16[1,16,2048]{2,1,0:T(8,128)(2,1)}, bf16[1,16,2048]{2,1,0:T(8,128)(2,1)S(1)}, u32[]{:S(2)}, u32[]{:S(2)}) collective-permute-start(bf16[1,16,2048]{2,1,0:T(8,128)(2,1)} %param.8), channel_id=1, source_target_pairs={{0,8},{8,16},{16,24},{24,32},{32,40},{40,48},{48,56},{56,64},{64,7... | collective-permute-start | bytes 196616 | tf_op jit(solution)/shard_map/ppermute | solution.py:20
  3.9 44.1 %copy-start = (bf16[1,128,2048]{2,1,0:T(8,128)(2,1)S(1)}, bf16[1,128,2048]{2,1,0:T(8,128)(2,1)}, u32[]{:S(2)}) copy-start(bf16[1,128,2048]{2,1,0:T(8,128)(2,1)} %param.7) | copy-start | bytes 1572868
  3.9 25.2 %collective-permute-start.4 = (bf16[64,2048]{1,0:T(8,128)(2,1)S(1)}, bf16[64,2048]{1,0:T(8,128)(2,1)S(1)}, u32[]{:S(2)}, u32[]{:S(2)}) collective-permute-start(bf16[64,2048]{1,0:T(8,128)(2,1)S(1)} %get-tuple-element.32), channel_id=1, source_target_pairs={{0,2},{1,3},{2,4},{3,5},{4,6},{5,7},{8,10},{9,11},{10,12},{11,13},... | collective-permute-start | bytes 786440 | tf_op jit(solution)/shard_map/ppermute | solution.py:157
  10.2 21.4 %collective-permute-start.5 = (bf16[64,2048]{1,0:T(8,128)(2,1)S(1)}, bf16[64,2048]{1,0:T(8,128)(2,1)S(1)}, u32[]{:S(2)}, u32[]{:S(2)}) collective-permute-start(bf16[64,2048]{1,0:T(8,128)(2,1)S(1)} %get-tuple-element.31), channel_id=1, source_target_pairs={{0,6},{1,7},{2,0},{3,1},{8,14},{9,15},{10,8},{11,9},{16,22},{17,23... | collective-permute-start | bytes 786440 | tf_op jit(solution)/shard_map/ppermute | solution.py:157
  17.2 15.1 %collective-permute-start.3 = (bf16[2,16,2048]{2,1,0:T(8,128)(2,1)S(1)}, bf16[2,16,2048]{2,1,0:T(8,128)(2,1)S(1)}, u32[]{:S(2)}, u32[]{:S(2)}) collective-permute-start(bf16[2,16,2048]{2,1,0:T(8,128)(2,1)S(1)} %get-tuple-element.67), channel_id=1, source_target_pairs={{0,48},{8,56},{16,64},{24,72},{32,80},{40,88},{48,96},{56,104},{64... | collective-permute-start | bytes 393224 | tf_op jit(solution)/shard_map/ppermute | solution.py:20
  20.9 11.3 %collective-permute-start.2 = (bf16[2,16,2048]{2,1,0:T(8,128)(2,1)S(1)}, bf16[2,16,2048]{2,1,0:T(8,128)(2,1)S(1)}, u32[]{:S(2)}, u32[]{:S(2)}) collective-permute-start(bf16[2,16,2048]{2,1,0:T(8,128)(2,1)S(1)} %get-tuple-element.67), channel_id=1, source_target_pairs={{0,32},{8,40},{16,48},{24,56},{32,64},{40,72},{48,80},{56,88},{64,... | collective-permute-start | bytes 393224 | tf_op jit(solution)/shard_map/ppermute | solution.py:20
  25.6 6.9 %collective-permute-start.1 = (bf16[2,16,2048]{2,1,0:T(8,128)(2,1)S(1)}, bf16[2,16,2048]{2,1,0:T(8,128)(2,1)S(1)}, u32[]{:S(2)}, u32[]{:S(2)}) collective-permute-start(bf16[2,16,2048]{2,1,0:T(8,128)(2,1)S(1)} %get-tuple-element.67), channel_id=1, source_target_pairs={{0,16},{8,24},{16,32},{24,40},{32,48},{40,56},{48,64},{56,72},{64,... | collective-permute-start | bytes 393224 | tf_op jit(solution)/shard_map/ppermute | solution.py:20
  29.1 18.9 %collective-permute-start.9 = (bf16[64,2048]{1,0:T(8,128)(2,1)S(1)}, bf16[64,2048]{1,0:T(8,128)(2,1)S(1)}, u32[]{:S(2)}, u32[]{:S(2)}) collective-permute-start(bf16[64,2048]{1,0:T(8,128)(2,1)S(1)} %get-tuple-element.31), channel_id=1, source_target_pairs={{0,2},{1,3},{2,4},{3,5},{4,6},{5,7},{8,10},{9,11},{10,12},{11,13},... | collective-permute-start | bytes 786440 | tf_op jit(solution)/shard_map/ppermute | solution.py:157
  31.6 16.4 %collective-permute-start.10 = (bf16[64,2048]{1,0:T(8,128)(2,1)S(1)}, bf16[64,2048]{1,0:T(8,128)(2,1)S(1)}, u32[]{:S(2)}, u32[]{:S(2)}) collective-permute-start(bf16[64,2048]{1,0:T(8,128)(2,1)S(1)} %get-tuple-element.32), channel_id=1, source_target_pairs={{1,7},{9,15},{17,23},{25,31},{33,39},{41,47},{49,55},{57,63},{65,7... | collective-permute-start | bytes 786440 | tf_op jit(solution)/shard_map/ppermute | solution.py:157
  32.5 27.5 %copy-start.3 = (bf16[16,2048]{1,0:T(8,128)(2,1)}, bf16[16,2048]{1,0:T(8,128)(2,1)S(1)}, u32[]{:S(2)}) copy-start(bf16[16,2048]{1,0:T(8,128)(2,1)S(1)} %dynamic-slice_bitcast_fusion.refs_0_.refs_8_) | copy-start | bytes 196612
  32.5 18.2 %collective-permute-start.6 = (bf16[16,2048]{1,0:T(8,128)(2,1)S(1)}, bf16[16,2048]{1,0:T(8,128)(2,1)S(1)}, u32[]{:S(2)}, u32[]{:S(2)}) collective-permute-start(bf16[16,2048]{1,0:T(8,128)(2,1)S(1)} %dynamic-slice_bitcast_fusion.refs_0_.refs_8_), channel_id=1, source_target_pairs={{0,4},{1,5},{2,6},{3,7},{4,0},{5,1},{6,2},{7,3},{8,12},{9,13},{10,... | collective-permute-start | bytes 196616 | tf_op jit(solution)/shard_map/ppermute | solution.py:157
  36.3 16.4 %collective-permute-start.8 = (bf16[80,2048]{1,0:T(8,128)(2,1)S(1)}, bf16[80,2048]{1,0:T(8,128)(2,1)S(1)}, u32[]{:S(2)}, u32[]{:S(2)}) collective-permute-start(bf16[80,2048]{1,0:T(8,128)(2,1)S(1)} %get-tuple-element.65), channel_id=1, source_target_pairs={{0,6},{1,7},{2,0},{3,1},{4,2},{5,3},{6,4},{7,5},{8,14},{9,15},{10,... | collective-permute-start | bytes 983048 | tf_op jit(solution)/shard_map/ppermute | solution.py:157
  41.6 18.4 %collective-permute-start.7 = (bf16[80,2048]{1,0:T(8,128)(2,1)S(1)}, bf16[80,2048]{1,0:T(8,128)(2,1)S(1)}, u32[]{:S(2)}, u32[]{:S(2)}) collective-permute-start(bf16[80,2048]{1,0:T(8,128)(2,1)S(1)} %get-tuple-element.66), channel_id=1, source_target_pairs={{0,2},{1,3},{2,4},{3,5},{4,6},{5,7},{6,0},{7,1},{8,10},{9,11},{10,... | collective-permute-start | bytes 983048 | tf_op jit(solution)/shard_map/ppermute | solution.py:157
  48.0 0.8 copy-start.2
  48.3 13.7 %copy-start.7 = (s32[1,3]{1,0:T(1,128)S(1)}, s32[1,3]{1,0:T(1,128)}, u32[]{:S(2)}) copy-start(s32[1,3]{1,0:T(1,128)} %param.10) | copy-start | bytes 40
  48.8 15.6 %collective-permute-start.11 = (bf16[256,2048]{1,0:T(8,128)(2,1)S(1)}, bf16[256,2048]{1,0:T(8,128)(2,1)}, u32[]{:S(2)}, u32[]{:S(2)}) collective-permute-start(bf16[256,2048]{1,0:T(8,128)(2,1)S(1)} %pad_maximum_fusion), channel_id=1, source_target_pairs={{0,1},{1,0},{2,3},{3,2},{4,5},{5,4},{6,7},{7,6},{8,9},{9,8},{10,11... | collective-permute-start | bytes 3145736 | tf_op jit(solution)/shard_map/ppermute | solution.py:157
  50.7 13.7 %copy-start.6 = (bf16[16,2048]{1,0:T(8,128)(2,1)}, bf16[16,2048]{1,0:T(8,128)(2,1)S(1)}, u32[]{:S(2)}) copy-start(bf16[16,2048]{1,0:T(8,128)(2,1)S(1)} %collective-permute-done.6.refs_1_.refs_9_) | copy-start | bytes 196612
  52.8 11.6 %copy-start.4 = (bf16[80,2048]{1,0:T(8,128)(2,1)}, bf16[80,2048]{1,0:T(8,128)(2,1)S(1)}, u32[]{:S(2)}) copy-start(bf16[80,2048]{1,0:T(8,128)(2,1)S(1)} %collective-permute-done.8.refs_3_.refs_11_) | copy-start | bytes 983044
  60.0 4.4 %copy-start.5 = (bf16[80,2048]{1,0:T(8,128)(2,1)}, bf16[80,2048]{1,0:T(8,128)(2,1)S(1)}, u32[]{:S(2)}) copy-start(bf16[80,2048]{1,0:T(8,128)(2,1)S(1)} %collective-permute-done.7.refs_2_.refs_10_) | copy-start | bytes 983044
  60.1 4.3 %collective-permute-start.12 = (bf16[192,2048]{1,0:T(8,128)(2,1)S(1)}, bf16[192,2048]{1,0:T(8,128)(2,1)}, u32[]{:S(2)}, u32[]{:S(2)}) collective-permute-start(bf16[192,2048]{1,0:T(8,128)(2,1)S(1)} %pad_maximum_fusion.1), channel_id=1, source_target_pairs={{0,1},{1,0},{2,3},{3,2},{4,5},{5,4},{6,7},{7,6},{8,9},{9,8},{10,11... | collective-permute-start | bytes 2359304 | tf_op jit(solution)/shard_map/ppermute | solution.py:157
  82.0 5.9 %collective-permute-start.13 = (bf16[448,2048]{1,0:T(8,128)(2,1)}, bf16[448,2048]{1,0:T(8,128)(2,1)S(1)}, u32[]{:S(2)}, u32[]{:S(2)}) collective-permute-start(bf16[448,2048]{1,0:T(8,128)(2,1)} %get-tuple-element.35), channel_id=1, source_target_pairs={{0,1},{1,0},{2,3},{3,2},{4,5},{5,4},{6,7},{7,6},{8,9},{9,8},{10,11... | collective-permute-start | bytes 5505032 | tf_op jit(solution)/shard_map/ppermute | solution.py:157
  87.9 1.5 copy-start.1
  90.9 20.6 %collective-permute-start.14 = (bf16[80,2048]{1,0:T(8,128)(2,1)S(1)}, bf16[80,2048]{1,0:T(8,128)(2,1)S(1)}, u32[]{:S(2)}, u32[]{:S(2)}) collective-permute-start(bf16[80,2048]{1,0:T(8,128)(2,1)S(1)} %pad_maximum_fusion.4), channel_id=1, source_target_pairs={{0,6},{1,7},{2,0},{3,1},{4,2},{5,3},{6,4},{7,5},{8,14},{9,15},{10,... | collective-permute-start | bytes 983048 | tf_op jit(solution)/shard_map/ppermute | solution.py:157
  93.5 18.0 %collective-permute-start.15 = (bf16[80,2048]{1,0:T(8,128)(2,1)S(1)}, bf16[80,2048]{1,0:T(8,128)(2,1)}, u32[]{:S(2)}, u32[]{:S(2)}) collective-permute-start(bf16[80,2048]{1,0:T(8,128)(2,1)S(1)} %pad_maximum_fusion.5), channel_id=1, source_target_pairs={{0,2},{1,3},{2,4},{3,5},{4,6},{5,7},{6,0},{7,1},{8,10},{9,11},{10,... | collective-permute-start | bytes 983048 | tf_op jit(solution)/shard_map/ppermute | solution.py:157
  97.7 13.8 %collective-permute-start.16 = (bf16[16,2048]{1,0:T(8,128)(2,1)S(1)}, bf16[16,2048]{1,0:T(8,128)(2,1)S(1)}, u32[]{:S(2)}, u32[]{:S(2)}) collective-permute-start(bf16[16,2048]{1,0:T(8,128)(2,1)S(1)} %get-tuple-element.57), channel_id=1, source_target_pairs={{0,4},{1,5},{2,6},{3,7},{4,0},{5,1},{6,2},{7,3},{8,12},{9,13},{10,... | collective-permute-start | bytes 196616 | tf_op jit(solution)/shard_map/ppermute | solution.py:157
  102.9 32.0 %collective-permute-start.18 = (bf16[64,2048]{1,0:T(8,128)(2,1)}, bf16[64,2048]{1,0:T(8,128)(2,1)}, u32[]{:S(2)}, u32[]{:S(2)}) collective-permute-start(bf16[64,2048]{1,0:T(8,128)(2,1)} %get-tuple-element.47), channel_id=1, source_target_pairs={{7,1},{15,9},{23,17},{31,25},{39,33},{47,41},{55,49},{63,57},{71,6... | collective-permute-start | bytes 786440 | tf_op jit(solution)/shard_map/ppermute | solution.py:157
  104.3 30.6 %collective-permute-start.17 = (bf16[64,2048]{1,0:T(8,128)(2,1)}, bf16[64,2048]{1,0:T(8,128)(2,1)}, u32[]{:S(2)}, u32[]{:S(2)}) collective-permute-start(bf16[64,2048]{1,0:T(8,128)(2,1)} %get-tuple-element.48), channel_id=1, source_target_pairs={{2,0},{3,1},{4,2},{5,3},{6,4},{7,5},{10,8},{11,9},{12,10},{13,11},... | collective-permute-start | bytes 786440 | tf_op jit(solution)/shard_map/ppermute | solution.py:157
  112.4 22.5 %collective-permute-start.19 = (bf16[2,16,2048]{2,1,0:T(8,128)(2,1)S(1)}, bf16[2,16,2048]{2,1,0:T(8,128)(2,1)S(1)}, u32[]{:S(2)}, u32[]{:S(2)}) collective-permute-start(bf16[2,16,2048]{2,1,0:T(8,128)(2,1)S(1)} %pad_maximum_fusion.6), channel_id=1, source_target_pairs={{0,496},{8,504},{16,0},{24,8},{32,16},{40,24},{48,32},{56,40},{64,... | collective-permute-start | bytes 393224 | tf_op jit(solution)/shard_map/ppermute | solution.py:20
  118.0 16.9 %collective-permute-start.23 = (bf16[2,16,2048]{2,1,0:T(8,128)(2,1)S(1)}, bf16[2,16,2048]{2,1,0:T(8,128)(2,1)S(1)}, u32[]{:S(2)}, u32[]{:S(2)}) collective-permute-start(bf16[2,16,2048]{2,1,0:T(8,128)(2,1)S(1)} %pad_maximum_fusion.8), channel_id=1, source_target_pairs={{0,464},{8,472},{16,480},{24,488},{32,496},{40,504},{48,0},{56,8},... | collective-permute-start | bytes 393224 | tf_op jit(solution)/shard_map/ppermute | solution.py:20
  131.9 9.3 %collective-permute-start.22 = (bf16[2,16,2048]{2,1,0:T(8,128)(2,1)S(1)}, bf16[2,16,2048]{2,1,0:T(8,128)(2,1)S(1)}, u32[]{:S(2)}, u32[]{:S(2)}) collective-permute-start(bf16[2,16,2048]{2,1,0:T(8,128)(2,1)S(1)} %pad_maximum_fusion.7), channel_id=1, source_target_pairs={{0,480},{8,488},{16,496},{24,504},{32,0},{40,8},{48,16},{56,24},{6... | collective-permute-start | bytes 393224 | tf_op jit(solution)/shard_map/ppermute | solution.py:20
  141.2 8.7 %collective-permute-start.24 = (bf16[16,2048]{1,0:T(8,128)(2,1)S(1)}, bf16[16,2048]{1,0:T(8,128)(2,1)S(1)}, u32[]{:S(2)}, u32[]{:S(2)}) collective-permute-start(bf16[16,2048]{1,0:T(8,128)(2,1)S(1)} %fusion.3), channel_id=1, source_target_pairs={{0,504},{8,0},{16,8},{24,16},{32,24},{40,32},{48,40},{56,48},{64,5... | collective-permute-start | bytes 196616 | tf_op jit(solution)/shard_map/ppermute | solution.py:20
  143.1 11.7 %collective-permute-start.20 = (bf16[64,2048]{1,0:T(8,128)(2,1)S(1)}, bf16[64,2048]{1,0:T(8,128)(2,1)S(1)}, u32[]{:S(2)}, u32[]{:S(2)}) collective-permute-start(bf16[64,2048]{1,0:T(8,128)(2,1)S(1)} %get-tuple-element.40), channel_id=1, source_target_pairs={{2,0},{3,1},{4,2},{5,3},{6,4},{7,5},{10,8},{11,9},{12,10},{13,11},... | collective-permute-start | bytes 786440 | tf_op jit(solution)/shard_map/ppermute | solution.py:157
  144.4 13.2 %collective-permute-start.21 = (bf16[64,2048]{1,0:T(8,128)(2,1)S(1)}, bf16[64,2048]{1,0:T(8,128)(2,1)S(1)}, u32[]{:S(2)}, u32[]{:S(2)}) collective-permute-start(bf16[64,2048]{1,0:T(8,128)(2,1)S(1)} %get-tuple-element.43), channel_id=1, source_target_pairs={{6,0},{7,1},{0,2},{1,3},{14,8},{15,9},{8,10},{9,11},{22,16},{23,17... | collective-permute-start | bytes 786440 | tf_op jit(solution)/shard_map/ppermute | solution.py:157

commit v8 on v7

--- a/solution.py
+++ b/solution.py
@@ -11,7 +11,7 @@
 HD = 128
 SPREAD = 8
 NEG = -1e30
-UNIT = 2
+UNIT = 4
 LOG2E = 1.4426950408889634
 
 

time: 161 us -> 160 us (level)
  no operation moved by 1% of the time
where the time goes in v8:
time: 160 us; the launch traced here: 159 us
  starting transfers between devices  90.2 us (56%)
  waiting for transfers between devices  38.5 us (24%)
  Pallas kernels  17.4 us (11%)
  other arithmetic  7.95 us (5%)
  local copies, waits for them, and re-layouts  3.58 us (2%)
  between operations  1.87 us (1%)
    ppermute x17, starting transfers between devices, along_seq(): return lax.ppermute(value, 'seq', pairs)  53.6 us
    ppermute x8, starting transfers between devices, passed_along(): lax.ppermute(value, axis, [(i, (i + by) % peers) for i in range(peers)])  36.6 us
    ppermute x17, waiting for transfers between devices, along_seq(): return lax.ppermute(value, 'seq', pairs)  32.1 us
    pallas_call x1, Pallas kernels, attend(): pl.pallas_call(functools.partial(attention_kernel, span, n_seq), grid_spe...  17.4 us
    ppermute x8, waiting for transfers between devices, passed_along(): lax.ppermute(value, axis, [(i, (i + by) % peers) for i in range(peers)])  6.37 us
    convert_element_type x5, other arithmetic, added(): return total.astype(jnp.bfloat16)  4.97 us
  transfers between devices with their start and end apart: 25, of which 10 were waited for; matrix products, arithmetic and copies ran while one was open for 4% of the time, Pallas kernels for 0%

profile of v8, /device:TPU:68, one launch (start us, length us, event | category | flops | bytes accessed | tf_op | source)
XLA Modules:
  0.0 159.5 jit_solution(5305735429662219995)
XLA Ops:
  0.6 2.2 %collective-permute-start = (bf16[1,16,2048]{2,1,0:T(8,128)(2,1)}, bf16[1,16,2048]{2,1,0:T(8,128)(2,1)S(1)}, u32[]{:S(2)}, u32[]{:S(2)}) collective-permute-start(bf16[1,16,2048]{2,1,0:T(8,128)(2,1)} %param.8), channel_id=1, source_target_pairs={{0,8},{8,16},{16,24},{24,32},{32,40},{40,48},{48,56},{56,64},{64,7... | collective-permute-start | bytes 196616 | tf_op jit(solution)/shard_map/ppermute | solution.py:20
  2.8 1.1 slice_bitcast_fusion.6
  3.9 0.0 copy-start
  3.9 6.2 %collective-permute-start.4 = (bf16[64,2048]{1,0:T(8,128)(2,1)S(1)}, bf16[64,2048]{1,0:T(8,128)(2,1)S(1)}, u32[]{:S(2)}, u32[]{:S(2)}) collective-permute-start(bf16[64,2048]{1,0:T(8,128)(2,1)S(1)} %get-tuple-element.32), channel_id=1, source_target_pairs={{0,2},{1,3},{2,4},{3,5},{4,6},{5,7},{8,10},{9,11},{10,12},{11,13},... | collective-permute-start | bytes 786440 | tf_op jit(solution)/shard_map/ppermute | solution.py:157
  10.2 6.1 %collective-permute-start.5 = (bf16[64,2048]{1,0:T(8,128)(2,1)S(1)}, bf16[64,2048]{1,0:T(8,128)(2,1)S(1)}, u32[]{:S(2)}, u32[]{:S(2)}) collective-permute-start(bf16[64,2048]{1,0:T(8,128)(2,1)S(1)} %get-tuple-element.31), channel_id=1, source_target_pairs={{0,6},{1,7},{2,0},{3,1},{8,14},{9,15},{10,8},{11,9},{16,22},{17,23... | collective-permute-start | bytes 786440 | tf_op jit(solution)/shard_map/ppermute | solution.py:157
  16.3 0.9 constant_dynamic-update-slice_fusion.1
  17.1 0.0 collective-permute-done
  17.2 3.8 %collective-permute-start.3 = (bf16[2,16,2048]{2,1,0:T(8,128)(2,1)S(1)}, bf16[2,16,2048]{2,1,0:T(8,128)(2,1)S(1)}, u32[]{:S(2)}, u32[]{:S(2)}) collective-permute-start(bf16[2,16,2048]{2,1,0:T(8,128)(2,1)S(1)} %get-tuple-element.67), channel_id=1, source_target_pairs={{0,48},{8,56},{16,64},{24,72},{32,80},{40,88},{48,96},{56,104},{64... | collective-permute-start | bytes 393224 | tf_op jit(solution)/shard_map/ppermute | solution.py:20
  20.9 4.6 %collective-permute-start.2 = (bf16[2,16,2048]{2,1,0:T(8,128)(2,1)S(1)}, bf16[2,16,2048]{2,1,0:T(8,128)(2,1)S(1)}, u32[]{:S(2)}, u32[]{:S(2)}) collective-permute-start(bf16[2,16,2048]{2,1,0:T(8,128)(2,1)S(1)} %get-tuple-element.67), channel_id=1, source_target_pairs={{0,32},{8,40},{16,48},{24,56},{32,64},{40,72},{48,80},{56,88},{64,... | collective-permute-start | bytes 393224 | tf_op jit(solution)/shard_map/ppermute | solution.py:20
  25.6 2.8 %collective-permute-start.1 = (bf16[2,16,2048]{2,1,0:T(8,128)(2,1)S(1)}, bf16[2,16,2048]{2,1,0:T(8,128)(2,1)S(1)}, u32[]{:S(2)}, u32[]{:S(2)}) collective-permute-start(bf16[2,16,2048]{2,1,0:T(8,128)(2,1)S(1)} %get-tuple-element.67), channel_id=1, source_target_pairs={{0,16},{8,24},{16,32},{24,40},{32,48},{40,56},{48,64},{56,72},{64,... | collective-permute-start | bytes 393224 | tf_op jit(solution)/shard_map/ppermute | solution.py:20
  29.1 2.5 %collective-permute-start.9 = (bf16[64,2048]{1,0:T(8,128)(2,1)S(1)}, bf16[64,2048]{1,0:T(8,128)(2,1)S(1)}, u32[]{:S(2)}, u32[]{:S(2)}) collective-permute-start(bf16[64,2048]{1,0:T(8,128)(2,1)S(1)} %get-tuple-element.31), channel_id=1, source_target_pairs={{0,2},{1,3},{2,4},{3,5},{4,6},{5,7},{8,10},{9,11},{10,12},{11,13},... | collective-permute-start | bytes 786440 | tf_op jit(solution)/shard_map/ppermute | solution.py:157
  31.6 0.7 collective-permute-start.10
  32.3 0.0 collective-permute-done.3
  32.3 0.0 collective-permute-done.2
  32.3 0.2 collective-permute-done.1
  32.5 0.0 copy-start.3
  32.5 3.7 %collective-permute-start.6 = (bf16[16,2048]{1,0:T(8,128)(2,1)S(1)}, bf16[16,2048]{1,0:T(8,128)(2,1)S(1)}, u32[]{:S(2)}, u32[]{:S(2)}) collective-permute-start(bf16[16,2048]{1,0:T(8,128)(2,1)S(1)} %dynamic-slice_bitcast_fusion.refs_0_.refs_8_), channel_id=1, source_target_pairs={{0,4},{1,5},{2,6},{3,7},{4,0},{5,1},{6,2},{7,3},{8,12},{9,13},{10,... | collective-permute-start | bytes 196616 | tf_op jit(solution)/shard_map/ppermute | solution.py:157
  36.3 0.1 pad_maximum_fusion.2
  36.3 5.3 %collective-permute-start.8 = (bf16[80,2048]{1,0:T(8,128)(2,1)S(1)}, bf16[80,2048]{1,0:T(8,128)(2,1)S(1)}, u32[]{:S(2)}, u32[]{:S(2)}) collective-permute-start(bf16[80,2048]{1,0:T(8,128)(2,1)S(1)} %get-tuple-element.65), channel_id=1, source_target_pairs={{0,6},{1,7},{2,0},{3,1},{4,2},{5,3},{6,4},{7,5},{8,14},{9,15},{10,... | collective-permute-start | bytes 983048 | tf_op jit(solution)/shard_map/ppermute | solution.py:157
  41.6 1.9 %collective-permute-start.7 = (bf16[80,2048]{1,0:T(8,128)(2,1)S(1)}, bf16[80,2048]{1,0:T(8,128)(2,1)S(1)}, u32[]{:S(2)}, u32[]{:S(2)}) collective-permute-start(bf16[80,2048]{1,0:T(8,128)(2,1)S(1)} %get-tuple-element.66), channel_id=1, source_target_pairs={{0,2},{1,3},{2,4},{3,5},{4,6},{5,7},{6,0},{7,1},{8,10},{9,11},{10,... | collective-permute-start | bytes 983048 | tf_op jit(solution)/shard_map/ppermute | solution.py:157
  43.5 4.4 %collective-permute-done.9 = bf16[64,2048]{1,0:T(8,128)(2,1)S(1)} collective-permute-done((bf16[64,2048]{1,0:T(8,128)(2,1)S(1)}, bf16[64,2048]{1,0:T(8,128)(2,1)S(1)}, u32[]{:S(2)}, u32[]{:S(2)}) %collective-permute-start.9) | collective-permute-done | bytes 262176 | tf_op jit(solution)/shard_map/ppermute | solution.py:157
  48.0 0.0 copy-start.2
  48.0 0.3 broadcast_select_fusion
  48.3 0.0 copy-start.7
  48.3 0.1 pad_maximum_fusion
  48.4 0.3 copy-done.2
  48.8 1.9 %collective-permute-start.11 = (bf16[256,2048]{1,0:T(8,128)(2,1)S(1)}, bf16[256,2048]{1,0:T(8,128)(2,1)}, u32[]{:S(2)}, u32[]{:S(2)}) collective-permute-start(bf16[256,2048]{1,0:T(8,128)(2,1)S(1)} %pad_maximum_fusion), channel_id=1, source_target_pairs={{0,1},{1,0},{2,3},{3,2},{4,5},{5,4},{6,7},{7,6},{8,9},{9,8},{10,11... | collective-permute-start | bytes 3145736 | tf_op jit(solution)/shard_map/ppermute | solution.py:157
  50.7 0.0 collective-permute-done.6.refs_1_.refs_9_
  50.7 2.1 %collective-permute-done.8.refs_3_.refs_11_ = bf16[80,2048]{1,0:T(8,128)(2,1)S(1)} collective-permute-done((bf16[80,2048]{1,0:T(8,128)(2,1)S(1)}, bf16[80,2048]{1,0:T(8,128)(2,1)S(1)}, u32[]{:S(2)}, u32[]{:S(2)}) %collective-permute-start.8) | collective-permute-done | bytes 327712 | tf_op jit(solution)/shard_map/ppermute | solution.py:157
  52.8 7.2 %collective-permute-done.7.refs_2_.refs_10_ = bf16[80,2048]{1,0:T(8,128)(2,1)S(1)} collective-permute-done((bf16[80,2048]{1,0:T(8,128)(2,1)S(1)}, bf16[80,2048]{1,0:T(8,128)(2,1)S(1)}, u32[]{:S(2)}, u32[]{:S(2)}) %collective-permute-start.7) | collective-permute-done | bytes 327712 | tf_op jit(solution)/shard_map/ppermute | solution.py:157
  60.0 0.1 pad_maximum_fusion.1
  60.1 1.9 %collective-permute-start.12 = (bf16[192,2048]{1,0:T(8,128)(2,1)S(1)}, bf16[192,2048]{1,0:T(8,128)(2,1)}, u32[]{:S(2)}, u32[]{:S(2)}) collective-permute-start(bf16[192,2048]{1,0:T(8,128)(2,1)S(1)} %pad_maximum_fusion.1), channel_id=1, source_target_pairs={{0,1},{1,0},{2,3},{3,2},{4,5},{5,4},{6,7},{7,6},{8,9},{9,8},{10,11... | collective-permute-start | bytes 2359304 | tf_op jit(solution)/shard_map/ppermute | solution.py:157
  62.0 0.2 reduce-window_clone.1
  62.2 0.6 select_reduce_fusion
  62.8 1.6 %collective-permute-done.12.refs_7_.refs_15_ = bf16[192,2048]{1,0:T(8,128)(2,1)} collective-permute-done((bf16[192,2048]{1,0:T(8,128)(2,1)S(1)}, bf16[192,2048]{1,0:T(8,128)(2,1)}, u32[]{:S(2)}, u32[]{:S(2)}) %collective-permute-start.12) | collective-permute-done | bytes 786464 | tf_op jit(solution)/shard_map/ppermute | solution.py:157
  64.4 17.4 %shard_map.85 = (bf16[128,4096]{1,0:T(8,128)(2,1)}, bf16[3,128,2048]{2,1,0:T(8,128)(2,1)}, bf16[448,2048]{1,0:T(8,128)(2,1)}, bf16[64,2048]{1,0:T(8,128)(2,1)}) custom-call(s32[1]{0:T(128)} %bitcast.info, bf16[128,4096]{1,0:T(8,128)(2,1)} %bitcast.85, bf16[128,4096]{1,0:T(8,128)(2,1)} %bitcast.86, s32[1,128]{1,0:T(1,128)} %bitcast.88, ...), custom_call_target="tpu_custom_call" | custom-call | flops 4697620480 | bytes 12582912 | tf_op jit(solution)/shard_map/pallas_call | solution.py:114
  81.8 2.0 %collective-permute-start.13 = (bf16[448,2048]{1,0:T(8,128)(2,1)}, bf16[448,2048]{1,0:T(8,128)(2,1)S(1)}, u32[]{:S(2)}, u32[]{:S(2)}) collective-permute-start(bf16[448,2048]{1,0:T(8,128)(2,1)} %get-tuple-element.35), channel_id=1, source_target_pairs={{0,1},{1,0},{2,3},{3,2},{4,5},{5,4},{6,7},{7,6},{8,9},{9,8},{10,11... | collective-permute-start | bytes 5505032 | tf_op jit(solution)/shard_map/ppermute | solution.py:157
  83.9 3.8 %collective-permute-done.13 = bf16[448,2048]{1,0:T(8,128)(2,1)S(1)} collective-permute-done((bf16[448,2048]{1,0:T(8,128)(2,1)}, bf16[448,2048]{1,0:T(8,128)(2,1)S(1)}, u32[]{:S(2)}, u32[]{:S(2)}) %collective-permute-start.13) | collective-permute-done | bytes 1835040 | tf_op jit(solution)/shard_map/ppermute | solution.py:157
  87.7 1.1 add_convert_fusion.2
  88.9 0.1 slice.137
  89.0 0.2 copy-done.1
  89.2 0.6 add_convert_fusion
  89.9 0.9 slice_bitcast_fusion
  90.7 2.5 %collective-permute-start.14 = (bf16[80,2048]{1,0:T(8,128)(2,1)S(1)}, bf16[80,2048]{1,0:T(8,128)(2,1)S(1)}, u32[]{:S(2)}, u32[]{:S(2)}) collective-permute-start(bf16[80,2048]{1,0:T(8,128)(2,1)S(1)} %pad_maximum_fusion.4), channel_id=1, source_target_pairs={{0,6},{1,7},{2,0},{3,1},{4,2},{5,3},{6,4},{7,5},{8,14},{9,15},{10,... | collective-permute-start | bytes 983048 | tf_op jit(solution)/shard_map/ppermute | solution.py:157
  93.3 4.2 %collective-permute-start.15 = (bf16[80,2048]{1,0:T(8,128)(2,1)S(1)}, bf16[80,2048]{1,0:T(8,128)(2,1)}, u32[]{:S(2)}, u32[]{:S(2)}) collective-permute-start(bf16[80,2048]{1,0:T(8,128)(2,1)S(1)} %pad_maximum_fusion.5), channel_id=1, source_target_pairs={{0,2},{1,3},{2,4},{3,5},{4,6},{5,7},{6,0},{7,1},{8,10},{9,11},{10,... | collective-permute-start | bytes 983048 | tf_op jit(solution)/shard_map/ppermute | solution.py:157
  97.5 5.2 %collective-permute-start.16 = (bf16[16,2048]{1,0:T(8,128)(2,1)S(1)}, bf16[16,2048]{1,0:T(8,128)(2,1)S(1)}, u32[]{:S(2)}, u32[]{:S(2)}) collective-permute-start(bf16[16,2048]{1,0:T(8,128)(2,1)S(1)} %get-tuple-element.57), channel_id=1, source_target_pairs={{0,4},{1,5},{2,6},{3,7},{4,0},{5,1},{6,2},{7,3},{8,12},{9,13},{10,... | collective-permute-start | bytes 196616 | tf_op jit(solution)/shard_map/ppermute | solution.py:157
  102.7 1.4 collective-permute-start.18
  104.1 1.3 collective-permute-start.17
  105.4 5.9 %collective-permute-done.16 = bf16[16,2048]{1,0:T(8,128)(2,1)S(1)} collective-permute-done((bf16[16,2048]{1,0:T(8,128)(2,1)S(1)}, bf16[16,2048]{1,0:T(8,128)(2,1)S(1)}, u32[]{:S(2)}, u32[]{:S(2)}) %collective-permute-start.16) | collective-permute-done | bytes 65568 | tf_op jit(solution)/shard_map/ppermute | solution.py:157
  111.3 0.9 select_bitcast_fusion.3
  112.3 5.5 %collective-permute-start.19 = (bf16[2,16,2048]{2,1,0:T(8,128)(2,1)S(1)}, bf16[2,16,2048]{2,1,0:T(8,128)(2,1)S(1)}, u32[]{:S(2)}, u32[]{:S(2)}) collective-permute-start(bf16[2,16,2048]{2,1,0:T(8,128)(2,1)S(1)} %pad_maximum_fusion.6), channel_id=1, source_target_pairs={{0,496},{8,504},{16,0},{24,8},{32,16},{40,24},{48,32},{56,40},{64,... | collective-permute-start | bytes 393224 | tf_op jit(solution)/shard_map/ppermute | solution.py:20
  117.8 13.8 %collective-permute-start.23 = (bf16[2,16,2048]{2,1,0:T(8,128)(2,1)S(1)}, bf16[2,16,2048]{2,1,0:T(8,128)(2,1)S(1)}, u32[]{:S(2)}, u32[]{:S(2)}) collective-permute-start(bf16[2,16,2048]{2,1,0:T(8,128)(2,1)S(1)} %pad_maximum_fusion.8), channel_id=1, source_target_pairs={{0,464},{8,472},{16,480},{24,488},{32,496},{40,504},{48,0},{56,8},... | collective-permute-start | bytes 393224 | tf_op jit(solution)/shard_map/ppermute | solution.py:20
  131.7 1.9 %collective-permute-start.22 = (bf16[2,16,2048]{2,1,0:T(8,128)(2,1)S(1)}, bf16[2,16,2048]{2,1,0:T(8,128)(2,1)S(1)}, u32[]{:S(2)}, u32[]{:S(2)}) collective-permute-start(bf16[2,16,2048]{2,1,0:T(8,128)(2,1)S(1)} %pad_maximum_fusion.7), channel_id=1, source_target_pairs={{0,480},{8,488},{16,496},{24,504},{32,0},{40,8},{48,16},{56,24},{6... | collective-permute-start | bytes 393224 | tf_op jit(solution)/shard_map/ppermute | solution.py:20
  133.6 1.1 fusion
  134.7 0.0 collective-permute-done.18
  134.7 0.0 collective-permute-done.23
  134.8 6.2 %collective-permute-done.22 = bf16[2,16,2048]{2,1,0:T(8,128)(2,1)S(1)} collective-permute-done((bf16[2,16,2048]{2,1,0:T(8,128)(2,1)S(1)}, bf16[2,16,2048]{2,1,0:T(8,128)(2,1)S(1)}, u32[]{:S(2)}, u32[]{:S(2)}) %collective-permute-start.22) | collective-permute-done | bytes 131104 | tf_op jit(solution)/shard_map/ppermute | solution.py:20
  141.0 1.9 %collective-permute-start.24 = (bf16[16,2048]{1,0:T(8,128)(2,1)S(1)}, bf16[16,2048]{1,0:T(8,128)(2,1)S(1)}, u32[]{:S(2)}, u32[]{:S(2)}) collective-permute-start(bf16[16,2048]{1,0:T(8,128)(2,1)S(1)} %fusion.3), channel_id=1, source_target_pairs={{0,504},{8,0},{16,8},{24,16},{32,24},{40,32},{48,40},{56,48},{64,5... | collective-permute-start | bytes 196616 | tf_op jit(solution)/shard_map/ppermute | solution.py:20
  142.9 1.3 collective-permute-start.20
  144.2 5.4 %collective-permute-start.21 = (bf16[64,2048]{1,0:T(8,128)(2,1)S(1)}, bf16[64,2048]{1,0:T(8,128)(2,1)S(1)}, u32[]{:S(2)}, u32[]{:S(2)}) collective-permute-start(bf16[64,2048]{1,0:T(8,128)(2,1)S(1)} %get-tuple-element.43), channel_id=1, source_target_pairs={{6,0},{7,1},{0,2},{1,3},{14,8},{15,9},{8,10},{9,11},{22,16},{23,17... | collective-permute-start | bytes 786440 | tf_op jit(solution)/shard_map/ppermute | solution.py:157
  149.7 0.7 fusion.4
  150.4 4.2 %collective-permute-done.20 = bf16[64,2048]{1,0:T(8,128)(2,1)S(1)} collective-permute-done((bf16[64,2048]{1,0:T(8,128)(2,1)S(1)}, bf16[64,2048]{1,0:T(8,128)(2,1)S(1)}, u32[]{:S(2)}, u32[]{:S(2)}) %collective-permute-start.20) | collective-permute-done | bytes 262176 | tf_op jit(solution)/shard_map/ppermute | solution.py:157
  154.6 2.8 %collective-permute-done.21 = bf16[64,2048]{1,0:T(8,128)(2,1)S(1)} collective-permute-done((bf16[64,2048]{1,0:T(8,128)(2,1)S(1)}, bf16[64,2048]{1,0:T(8,128)(2,1)S(1)}, u32[]{:S(2)}, u32[]{:S(2)}) %collective-permute-start.21) | collective-permute-done | bytes 262176 | tf_op jit(solution)/shard_map/ppermute | solution.py:157
  157.4 2.1 %add_convert_fusion.1 = bf16[1,128,2048]{2,1,0:T(8,128)(2,1)} fusion(bf16[4,128,2048]{2,1,0:T(8,128)(2,1)S(1)} %add_convert_fusion, bf16[1,64,2048]{2,1,0:T(8,128)(2,1)} %bitcast.21, bf16[1,64,2048]{2,1,0:T(8,128)(2,1)S(1)} %bitcast.83, bf16[1,64,2048]{2,1,0:T(8,128)(2,1)S(1)} %bitcast.84, bf16[1,64,2048]{2,1,0:T(8,128)(2,1)} %bitcast.22), kind=kLoop, calls=%fused_computation.2 | loop fusion | flops 3145728 | bytes 2097152 | tf_op jit(solution)/shard_map/convert_element_type | solution.py:153
  (36 shorter events, 0.3 us)
Async XLA Ops:
  0.6 16.5 %collective-permute-start = (bf16[1,16,2048]{2,1,0:T(8,128)(2,1)}, bf16[1,16,2048]{2,1,0:T(8,128)(2,1)S(1)}, u32[]{:S(2)}, u32[]{:S(2)}) collective-permute-start(bf16[1,16,2048]{2,1,0:T(8,128)(2,1)} %param.8), channel_id=1, source_target_pairs={{0,8},{8,16},{16,24},{24,32},{32,40},{40,48},{48,56},{56,64},{64,7... | collective-permute-start | bytes 196616 | tf_op jit(solution)/shard_map/ppermute | solution.py:20
  3.9 44.1 %copy-start = (bf16[1,128,2048]{2,1,0:T(8,128)(2,1)S(1)}, bf16[1,128,2048]{2,1,0:T(8,128)(2,1)}, u32[]{:S(2)}) copy-start(bf16[1,128,2048]{2,1,0:T(8,128)(2,1)} %param.7) | copy-start | bytes 1572868
  3.9 25.2 %collective-permute-start.4 = (bf16[64,2048]{1,0:T(8,128)(2,1)S(1)}, bf16[64,2048]{1,0:T(8,128)(2,1)S(1)}, u32[]{:S(2)}, u32[]{:S(2)}) collective-permute-start(bf16[64,2048]{1,0:T(8,128)(2,1)S(1)} %get-tuple-element.32), channel_id=1, source_target_pairs={{0,2},{1,3},{2,4},{3,5},{4,6},{5,7},{8,10},{9,11},{10,12},{11,13},... | collective-permute-start | bytes 786440 | tf_op jit(solution)/shard_map/ppermute | solution.py:157
  10.2 21.4 %collective-permute-start.5 = (bf16[64,2048]{1,0:T(8,128)(2,1)S(1)}, bf16[64,2048]{1,0:T(8,128)(2,1)S(1)}, u32[]{:S(2)}, u32[]{:S(2)}) collective-permute-start(bf16[64,2048]{1,0:T(8,128)(2,1)S(1)} %get-tuple-element.31), channel_id=1, source_target_pairs={{0,6},{1,7},{2,0},{3,1},{8,14},{9,15},{10,8},{11,9},{16,22},{17,23... | collective-permute-start | bytes 786440 | tf_op jit(solution)/shard_map/ppermute | solution.py:157
  17.2 15.1 %collective-permute-start.3 = (bf16[2,16,2048]{2,1,0:T(8,128)(2,1)S(1)}, bf16[2,16,2048]{2,1,0:T(8,128)(2,1)S(1)}, u32[]{:S(2)}, u32[]{:S(2)}) collective-permute-start(bf16[2,16,2048]{2,1,0:T(8,128)(2,1)S(1)} %get-tuple-element.67), channel_id=1, source_target_pairs={{0,48},{8,56},{16,64},{24,72},{32,80},{40,88},{48,96},{56,104},{64... | collective-permute-start | bytes 393224 | tf_op jit(solution)/shard_map/ppermute | solution.py:20
  20.9 11.3 %collective-permute-start.2 = (bf16[2,16,2048]{2,1,0:T(8,128)(2,1)S(1)}, bf16[2,16,2048]{2,1,0:T(8,128)(2,1)S(1)}, u32[]{:S(2)}, u32[]{:S(2)}) collective-permute-start(bf16[2,16,2048]{2,1,0:T(8,128)(2,1)S(1)} %get-tuple-element.67), channel_id=1, source_target_pairs={{0,32},{8,40},{16,48},{24,56},{32,64},{40,72},{48,80},{56,88},{64,... | collective-permute-start | bytes 393224 | tf_op jit(solution)/shard_map/ppermute | solution.py:20
  25.6 6.9 %collective-permute-start.1 = (bf16[2,16,2048]{2,1,0:T(8,128)(2,1)S(1)}, bf16[2,16,2048]{2,1,0:T(8,128)(2,1)S(1)}, u32[]{:S(2)}, u32[]{:S(2)}) collective-permute-start(bf16[2,16,2048]{2,1,0:T(8,128)(2,1)S(1)} %get-tuple-element.67), channel_id=1, source_target_pairs={{0,16},{8,24},{16,32},{24,40},{32,48},{40,56},{48,64},{56,72},{64,... | collective-permute-start | bytes 393224 | tf_op jit(solution)/shard_map/ppermute | solution.py:20
  29.1 18.9 %collective-permute-start.9 = (bf16[64,2048]{1,0:T(8,128)(2,1)S(1)}, bf16[64,2048]{1,0:T(8,128)(2,1)S(1)}, u32[]{:S(2)}, u32[]{:S(2)}) collective-permute-start(bf16[64,2048]{1,0:T(8,128)(2,1)S(1)} %get-tuple-element.31), channel_id=1, source_target_pairs={{0,2},{1,3},{2,4},{3,5},{4,6},{5,7},{8,10},{9,11},{10,12},{11,13},... | collective-permute-start | bytes 786440 | tf_op jit(solution)/shard_map/ppermute | solution.py:157
  31.6 16.4 %collective-permute-start.10 = (bf16[64,2048]{1,0:T(8,128)(2,1)S(1)}, bf16[64,2048]{1,0:T(8,128)(2,1)S(1)}, u32[]{:S(2)}, u32[]{:S(2)}) collective-permute-start(bf16[64,2048]{1,0:T(8,128)(2,1)S(1)} %get-tuple-element.32), channel_id=1, source_target_pairs={{1,7},{9,15},{17,23},{25,31},{33,39},{41,47},{49,55},{57,63},{65,7... | collective-permute-start | bytes 786440 | tf_op jit(solution)/shard_map/ppermute | solution.py:157
  32.5 27.5 %copy-start.3 = (bf16[16,2048]{1,0:T(8,128)(2,1)}, bf16[16,2048]{1,0:T(8,128)(2,1)S(1)}, u32[]{:S(2)}) copy-start(bf16[16,2048]{1,0:T(8,128)(2,1)S(1)} %dynamic-slice_bitcast_fusion.refs_0_.refs_8_) | copy-start | bytes 196612
  32.5 18.2 %collective-permute-start.6 = (bf16[16,2048]{1,0:T(8,128)(2,1)S(1)}, bf16[16,2048]{1,0:T(8,128)(2,1)S(1)}, u32[]{:S(2)}, u32[]{:S(2)}) collective-permute-start(bf16[16,2048]{1,0:T(8,128)(2,1)S(1)} %dynamic-slice_bitcast_fusion.refs_0_.refs_8_), channel_id=1, source_target_pairs={{0,4},{1,5},{2,6},{3,7},{4,0},{5,1},{6,2},{7,3},{8,12},{9,13},{10,... | collective-permute-start | bytes 196616 | tf_op jit(solution)/shard_map/ppermute | solution.py:157
  36.3 16.4 %collective-permute-start.8 = (bf16[80,2048]{1,0:T(8,128)(2,1)S(1)}, bf16[80,2048]{1,0:T(8,128)(2,1)S(1)}, u32[]{:S(2)}, u32[]{:S(2)}) collective-permute-start(bf16[80,2048]{1,0:T(8,128)(2,1)S(1)} %get-tuple-element.65), channel_id=1, source_target_pairs={{0,6},{1,7},{2,0},{3,1},{4,2},{5,3},{6,4},{7,5},{8,14},{9,15},{10,... | collective-permute-start | bytes 983048 | tf_op jit(solution)/shard_map/ppermute | solution.py:157
  41.6 18.4 %collective-permute-start.7 = (bf16[80,2048]{1,0:T(8,128)(2,1)S(1)}, bf16[80,2048]{1,0:T(8,128)(2,1)S(1)}, u32[]{:S(2)}, u32[]{:S(2)}) collective-permute-start(bf16[80,2048]{1,0:T(8,128)(2,1)S(1)} %get-tuple-element.66), channel_id=1, source_target_pairs={{0,2},{1,3},{2,4},{3,5},{4,6},{5,7},{6,0},{7,1},{8,10},{9,11},{10,... | collective-permute-start | bytes 983048 | tf_op jit(solution)/shard_map/ppermute | solution.py:157
  48.0 0.8 copy-start.2
  48.3 13.7 %copy-start.7 = (s32[1,3]{1,0:T(1,128)S(1)}, s32[1,3]{1,0:T(1,128)}, u32[]{:S(2)}) copy-start(s32[1,3]{1,0:T(1,128)} %param.10) | copy-start | bytes 40
  48.8 15.6 %collective-permute-start.11 = (bf16[256,2048]{1,0:T(8,128)(2,1)S(1)}, bf16[256,2048]{1,0:T(8,128)(2,1)}, u32[]{:S(2)}, u32[]{:S(2)}) collective-permute-start(bf16[256,2048]{1,0:T(8,128)(2,1)S(1)} %pad_maximum_fusion), channel_id=1, source_target_pairs={{0,1},{1,0},{2,3},{3,2},{4,5},{5,4},{6,7},{7,6},{8,9},{9,8},{10,11... | collective-permute-start | bytes 3145736 | tf_op jit(solution)/shard_map/ppermute | solution.py:157
  50.7 13.7 %copy-start.6 = (bf16[16,2048]{1,0:T(8,128)(2,1)}, bf16[16,2048]{1,0:T(8,128)(2,1)S(1)}, u32[]{:S(2)}) copy-start(bf16[16,2048]{1,0:T(8,128)(2,1)S(1)} %collective-permute-done.6.refs_1_.refs_9_) | copy-start | bytes 196612
  52.8 11.6 %copy-start.4 = (bf16[80,2048]{1,0:T(8,128)(2,1)}, bf16[80,2048]{1,0:T(8,128)(2,1)S(1)}, u32[]{:S(2)}) copy-start(bf16[80,2048]{1,0:T(8,128)(2,1)S(1)} %collective-permute-done.8.refs_3_.refs_11_) | copy-start | bytes 983044
  60.0 4.4 %copy-start.5 = (bf16[80,2048]{1,0:T(8,128)(2,1)}, bf16[80,2048]{1,0:T(8,128)(2,1)S(1)}, u32[]{:S(2)}) copy-start(bf16[80,2048]{1,0:T(8,128)(2,1)S(1)} %collective-permute-done.7.refs_2_.refs_10_) | copy-start | bytes 983044
  60.1 4.3 %collective-permute-start.12 = (bf16[192,2048]{1,0:T(8,128)(2,1)S(1)}, bf16[192,2048]{1,0:T(8,128)(2,1)}, u32[]{:S(2)}, u32[]{:S(2)}) collective-permute-start(bf16[192,2048]{1,0:T(8,128)(2,1)S(1)} %pad_maximum_fusion.1), channel_id=1, source_target_pairs={{0,1},{1,0},{2,3},{3,2},{4,5},{5,4},{6,7},{7,6},{8,9},{9,8},{10,11... | collective-permute-start | bytes 2359304 | tf_op jit(solution)/shard_map/ppermute | solution.py:157
  81.8 5.9 %collective-permute-start.13 = (bf16[448,2048]{1,0:T(8,128)(2,1)}, bf16[448,2048]{1,0:T(8,128)(2,1)S(1)}, u32[]{:S(2)}, u32[]{:S(2)}) collective-permute-start(bf16[448,2048]{1,0:T(8,128)(2,1)} %get-tuple-element.35), channel_id=1, source_target_pairs={{0,1},{1,0},{2,3},{3,2},{4,5},{5,4},{6,7},{7,6},{8,9},{9,8},{10,11... | collective-permute-start | bytes 5505032 | tf_op jit(solution)/shard_map/ppermute | solution.py:157
  87.7 1.5 copy-start.1
  90.7 20.6 %collective-permute-start.14 = (bf16[80,2048]{1,0:T(8,128)(2,1)S(1)}, bf16[80,2048]{1,0:T(8,128)(2,1)S(1)}, u32[]{:S(2)}, u32[]{:S(2)}) collective-permute-start(bf16[80,2048]{1,0:T(8,128)(2,1)S(1)} %pad_maximum_fusion.4), channel_id=1, source_target_pairs={{0,6},{1,7},{2,0},{3,1},{4,2},{5,3},{6,4},{7,5},{8,14},{9,15},{10,... | collective-permute-start | bytes 983048 | tf_op jit(solution)/shard_map/ppermute | solution.py:157
  93.3 18.0 %collective-permute-start.15 = (bf16[80,2048]{1,0:T(8,128)(2,1)S(1)}, bf16[80,2048]{1,0:T(8,128)(2,1)}, u32[]{:S(2)}, u32[]{:S(2)}) collective-permute-start(bf16[80,2048]{1,0:T(8,128)(2,1)S(1)} %pad_maximum_fusion.5), channel_id=1, source_target_pairs={{0,2},{1,3},{2,4},{3,5},{4,6},{5,7},{6,0},{7,1},{8,10},{9,11},{10,... | collective-permute-start | bytes 983048 | tf_op jit(solution)/shard_map/ppermute | solution.py:157
  97.5 13.8 %collective-permute-start.16 = (bf16[16,2048]{1,0:T(8,128)(2,1)S(1)}, bf16[16,2048]{1,0:T(8,128)(2,1)S(1)}, u32[]{:S(2)}, u32[]{:S(2)}) collective-permute-start(bf16[16,2048]{1,0:T(8,128)(2,1)S(1)} %get-tuple-element.57), channel_id=1, source_target_pairs={{0,4},{1,5},{2,6},{3,7},{4,0},{5,1},{6,2},{7,3},{8,12},{9,13},{10,... | collective-permute-start | bytes 196616 | tf_op jit(solution)/shard_map/ppermute | solution.py:157
  102.7 32.0 %collective-permute-start.18 = (bf16[64,2048]{1,0:T(8,128)(2,1)}, bf16[64,2048]{1,0:T(8,128)(2,1)}, u32[]{:S(2)}, u32[]{:S(2)}) collective-permute-start(bf16[64,2048]{1,0:T(8,128)(2,1)} %get-tuple-element.47), channel_id=1, source_target_pairs={{7,1},{15,9},{23,17},{31,25},{39,33},{47,41},{55,49},{63,57},{71,6... | collective-permute-start | bytes 786440 | tf_op jit(solution)/shard_map/ppermute | solution.py:157
  104.1 30.6 %collective-permute-start.17 = (bf16[64,2048]{1,0:T(8,128)(2,1)}, bf16[64,2048]{1,0:T(8,128)(2,1)}, u32[]{:S(2)}, u32[]{:S(2)}) collective-permute-start(bf16[64,2048]{1,0:T(8,128)(2,1)} %get-tuple-element.48), channel_id=1, source_target_pairs={{2,0},{3,1},{4,2},{5,3},{6,4},{7,5},{10,8},{11,9},{12,10},{13,11},... | collective-permute-start | bytes 786440 | tf_op jit(solution)/shard_map/ppermute | solution.py:157
  112.3 22.5 %collective-permute-start.19 = (bf16[2,16,2048]{2,1,0:T(8,128)(2,1)S(1)}, bf16[2,16,2048]{2,1,0:T(8,128)(2,1)S(1)}, u32[]{:S(2)}, u32[]{:S(2)}) collective-permute-start(bf16[2,16,2048]{2,1,0:T(8,128)(2,1)S(1)} %pad_maximum_fusion.6), channel_id=1, source_target_pairs={{0,496},{8,504},{16,0},{24,8},{32,16},{40,24},{48,32},{56,40},{64,... | collective-permute-start | bytes 393224 | tf_op jit(solution)/shard_map/ppermute | solution.py:20
  117.8 16.9 %collective-permute-start.23 = (bf16[2,16,2048]{2,1,0:T(8,128)(2,1)S(1)}, bf16[2,16,2048]{2,1,0:T(8,128)(2,1)S(1)}, u32[]{:S(2)}, u32[]{:S(2)}) collective-permute-start(bf16[2,16,2048]{2,1,0:T(8,128)(2,1)S(1)} %pad_maximum_fusion.8), channel_id=1, source_target_pairs={{0,464},{8,472},{16,480},{24,488},{32,496},{40,504},{48,0},{56,8},... | collective-permute-start | bytes 393224 | tf_op jit(solution)/shard_map/ppermute | solution.py:20
  131.7 9.3 %collective-permute-start.22 = (bf16[2,16,2048]{2,1,0:T(8,128)(2,1)S(1)}, bf16[2,16,2048]{2,1,0:T(8,128)(2,1)S(1)}, u32[]{:S(2)}, u32[]{:S(2)}) collective-permute-start(bf16[2,16,2048]{2,1,0:T(8,128)(2,1)S(1)} %pad_maximum_fusion.7), channel_id=1, source_target_pairs={{0,480},{8,488},{16,496},{24,504},{32,0},{40,8},{48,16},{56,24},{6... | collective-permute-start | bytes 393224 | tf_op jit(solution)/shard_map/ppermute | solution.py:20
  141.0 8.7 %collective-permute-start.24 = (bf16[16,2048]{1,0:T(8,128)(2,1)S(1)}, bf16[16,2048]{1,0:T(8,128)(2,1)S(1)}, u32[]{:S(2)}, u32[]{:S(2)}) collective-permute-start(bf16[16,2048]{1,0:T(8,128)(2,1)S(1)} %fusion.3), channel_id=1, source_target_pairs={{0,504},{8,0},{16,8},{24,16},{32,24},{40,32},{48,40},{56,48},{64,5... | collective-permute-start | bytes 196616 | tf_op jit(solution)/shard_map/ppermute | solution.py:20
  142.9 11.7 %collective-permute-start.20 = (bf16[64,2048]{1,0:T(8,128)(2,1)S(1)}, bf16[64,2048]{1,0:T(8,128)(2,1)S(1)}, u32[]{:S(2)}, u32[]{:S(2)}) collective-permute-start(bf16[64,2048]{1,0:T(8,128)(2,1)S(1)} %get-tuple-element.40), channel_id=1, source_target_pairs={{2,0},{3,1},{4,2},{5,3},{6,4},{7,5},{10,8},{11,9},{12,10},{13,11},... | collective-permute-start | bytes 786440 | tf_op jit(solution)/shard_map/ppermute | solution.py:157
  144.2 13.2 %collective-permute-start.21 = (bf16[64,2048]{1,0:T(8,128)(2,1)S(1)}, bf16[64,2048]{1,0:T(8,128)(2,1)S(1)}, u32[]{:S(2)}, u32[]{:S(2)}) collective-permute-start(bf16[64,2048]{1,0:T(8,128)(2,1)S(1)} %get-tuple-element.43), channel_id=1, source_target_pairs={{6,0},{7,1},{0,2},{1,3},{14,8},{15,9},{8,10},{9,11},{22,16},{23,17... | collective-permute-start | bytes 786440 | tf_op jit(solution)/shard_map/ppermute | solution.py:157
